TPU v7x, 256 devices: a whole 4x4x8 slice. The times are simulated.
256 devices in a mesh: tm: 8 (over z), star: 32 (over x, y, core).
Axes of the slice: x: 4, y: 4, z: 8, core: 2. Of those that a mesh axis runs over, the one named last changes fastest.
Arguments:
- star_coef: float32 [5, 524288], P(None, ('tm', 'star')), may hold values from -6 to 6
- att_coef: float32 [12, 524288], P(None, ('tm', 'star')), may hold values from -6 to 6
- cal_coef: float32 [524288], P(('tm', 'star')), may hold values from -6 to 6
- observed: float32 [524288], P(('tm', 'star')), may hold values from -6 to 6
- star_index: int32 [524288], P(('tm', 'star')), may hold values from 0 to 4095
- knot_index: int32 [524288], P(('tm', 'star')), may hold values from 0 to 1023
- cal_index: int32 [524288], P(('tm', 'star')), may hold values from 0 to 2047
- valid_blocks: int32 [8, 32], P('tm', 'star'), may hold values from 6 to 16, as said below
Outputs:
- star_solution: float32 [5, 131072], P(None, 'star')
- attitude_solution: float32 [3, 8192], P(None, 'tm')
- calibration_solution: float32 [2048], replicated
Inputs may be any that keep to these rules, and one draw needn't show every extreme that they name: `valid_blocks`: every value lies between the two bounds, and the largest is reached in every draw.
All inputs are finite; a program needn't handle non-finite values.
Results may differ from a plain program's by a relative error of at most 0.0003.
Values sent between devices are 32-bit elements; how exact they have to be, the bound alone decides.
No kernel may reach another device: no remote copies, remote signals or barrier semaphores. Data moves between devices by JAX's collectives and lax.ppermute only.
A program may use at most 64 MiB of HBM per device.

v0:
```python
import jax
import jax.numpy as jnp
from jax import lax
from jax.sharding import PartitionSpec as P

STAR_DEV = 4096
KNOT_DEV = 1024
CAL = 2048
PAR = 5
ITERS = 3


def from_behind(value, axis, steps):
    count = lax.axis_size(axis)
    first, last = (max(0, -steps), min(count, count - steps))
    return lax.ppermute(value, axis, [(source, source + steps) for source in range(first, last)])


def shards(
    star_coef, att_coef, cal_coef, observed, star_index, knot_index, cal_index, valid_blocks
):
    rows = observed.shape[0]
    live = (lax.iota(jnp.int32, rows) < 128 * valid_blocks[0, 0]).astype(jnp.float32)
    first_tm = lax.axis_index("tm") == 0
    first_star = lax.axis_index("star") == 0
    star_cols = STAR_DEV
    star_weight = first_tm.astype(jnp.float32)
    att_weight = first_star.astype(jnp.float32)
    cal_weight = jnp.logical_and(first_tm, first_star).astype(jnp.float32)
    rhs = observed * live
    vec = (
        jnp.zeros((PAR, star_cols), jnp.float32),
        jnp.zeros((3, KNOT_DEV), jnp.float32),
        jnp.zeros((CAL,), jnp.float32),
    )
    alpha = jnp.float32(0.0)
    rowvec = rhs
    for step in range(ITERS + 1):
        if step == 0:
            update = rhs
        else:
            forward_stars, forward_knots, forward_cals = vec
            head = from_behind(forward_knots[:, :3], "tm", -1)
            extended = jnp.concatenate([forward_knots, head], axis=1)
            total = jnp.sum(star_coef * jnp.take(forward_stars, star_index, axis=1), axis=0)
            for forward_j in range(4):
                taken = jnp.take(extended, knot_index + forward_j, axis=1)
                total = total + jnp.sum(att_coef[3 * forward_j : 3 * forward_j + 3] * taken, axis=0)
            total = total + cal_coef * forward_cals[cal_index]
            update = total * live - alpha * rowvec
        beta = jnp.sqrt(lax.psum(jnp.sum(update * update), ("tm", "star")))
        rowvec = update / beta
        masked = rowvec * live
        star_part = jnp.stack(
            [
                jax.ops.segment_sum(star_coef[p] * masked, star_index, num_segments=STAR_DEV)
                for p in range(PAR)
            ]
        )
        knot_parts = []
        for a in range(3):
            accum = jnp.zeros((KNOT_DEV + 3,), jnp.float32)
            for j in range(4):
                accum = accum + jax.ops.segment_sum(
                    att_coef[3 * j + a] * masked, knot_index + j, num_segments=KNOT_DEV + 3
                )
            knot_parts.append(accum)
        cal_part = jax.ops.segment_sum(cal_coef * masked, cal_index, num_segments=CAL)
        knot_sum = lax.psum(jnp.stack(knot_parts), "star")
        cals = lax.psum(cal_part, ("tm", "star"))
        star_sum = lax.psum(star_part, "tm")
        carried = from_behind(knot_sum[:, KNOT_DEV:], "tm", 1)
        knots = jnp.concatenate([knot_sum[:, :3] + carried, knot_sum[:, 3:KNOT_DEV]], axis=1)
        image = (star_sum, knots, cals)
        nextv = tuple((qi - beta * vi for qi, vi in zip(image, vec)))
        alpha = jnp.sqrt(
            lax.psum(
                star_weight * jnp.sum(nextv[0] * nextv[0])
                + att_weight * jnp.sum(nextv[1] * nextv[1])
                + cal_weight * jnp.sum(nextv[2] * nextv[2]),
                ("tm", "star"),
            )
        )
        vec = tuple((item / alpha for item in nextv))
        if step == 0:
            solution = tuple((jnp.zeros_like(item) for item in vec))
            direction = vec
            phibar = beta
            rhobar = alpha
        else:
            rho = jnp.sqrt(rhobar * rhobar + beta * beta)
            cosine = rhobar / rho
            sine = beta / rho
            theta = sine * alpha
            rhobar = -cosine * alpha
            phi = cosine * phibar
            phibar = sine * phibar
            solution = tuple((xi + phi / rho * wi for xi, wi in zip(solution, direction)))
            direction = tuple((vi - theta / rho * wi for vi, wi in zip(vec, direction)))
    return (solution[0], solution[1], solution[2])


def solution(mesh):
    return jax.shard_map(
        shards,
        mesh=mesh,
        in_specs=(
            P(None, ("tm", "star")),
            P(None, ("tm", "star")),
            P(("tm", "star")),
            P(("tm", "star")),
            P(("tm", "star")),
            P(("tm", "star")),
            P(("tm", "star")),
            P("tm", "star"),
        ),
        out_specs=(P(None, "star"), P(None, "tm"), P()),
        check_vma=False,
    )
```

profile of v0, /device:TPU:1, one launch (start us, length us, event | category | flops | bytes accessed | tf_op | source)
XLA Modules:
  0.0 2294.4 jit_solution(15855935721799617434)
XLA Ops:
  10.8 81.4 %psum.112 = f32[]{:T(128)} all-reduce(f32[]{:T(128)} %multiply_reduce_fusion.12), channel_id=1, replica_groups=mesh['tm'=8,'star'=32] {'tm','star'}, use_global_device_ids=true, to_apply=%region_1.0 | all-reduce | flops 1 | bytes 8 | tf_op jit(solution)/shard_map/psum | solution.py:51
  96.7 14.8 scatter_custom_fusion.5
  111.6 14.7 scatter_custom_fusion.6
  126.2 14.7 scatter_custom_fusion.8
  140.9 14.7 scatter_fusion
  155.6 14.7 scatter_custom_fusion.10
  170.3 14.7 scatter_custom_fusion.9
  185.0 14.7 scatter_custom_fusion.12
  199.6 14.7 scatter_fusion.1
  214.3 14.8 scatter_custom_fusion.14
  229.2 14.7 scatter_custom_fusion.13
  243.9 14.7 scatter_custom_fusion.16
  258.6 14.7 scatter_fusion.2
  273.3 119.5 %psum.114 = f32[3,1027]{1,0:T(4,128)S(1)} all-reduce(f32[3,1027]{1,0:T(4,128)S(1)} %pad_maximum_fusion), channel_id=1, replica_groups=mesh['tm'=8,'star'=32] {'star'}, use_global_device_ids=true, to_apply=%region_21.0 | all-reduce | flops 3081 | bytes 24648 | tf_op jit(solution)/shard_map/psum | solution.py:69
  467.9 77.3 %psum.115 = f32[2048]{0:T(1024)S(1)} all-reduce(f32[2048]{0:T(1024)S(1)} %scatter_custom_fusion.17), channel_id=1, replica_groups=mesh['tm'=8,'star'=32] {'tm','star'}, use_global_device_ids=true, to_apply=%region_24.0 | all-reduce | flops 2048 | bytes 16384 | tf_op jit(solution)/shard_map/psum | solution.py:70
  555.1 74.4 %psum.116 = f32[]{:T(128)} all-reduce(f32[]{:T(128)S(6)} %add.381), channel_id=1, replica_groups=mesh['tm'=8,'star'=32] {'tm','star'}, use_global_device_ids=true, to_apply=%region_26.0 | all-reduce | flops 1 | bytes 8 | tf_op jit(solution)/shard_map/psum | solution.py:77
  643.6 11.8 gather_fusion
  697.7 74.9 %psum.117 = f32[]{:T(128)} all-reduce(f32[]{:T(128)} %get-tuple-element.20), channel_id=1, replica_groups=mesh['tm'=8,'star'=32] {'tm','star'}, use_global_device_ids=true, to_apply=%region_33.36 | all-reduce | flops 1 | bytes 8 | tf_op jit(solution)/shard_map/psum | solution.py:51
  773.6 14.8 scatter_custom_fusion.24
  788.4 14.8 scatter_custom_fusion.23
  803.2 14.8 scatter_custom_fusion.26
  818.0 15.1 scatter_fusion.3
  833.1 14.8 scatter_custom_fusion.28
  847.9 14.8 scatter_custom_fusion.27
  862.8 14.8 scatter_custom_fusion.30
  877.6 14.7 scatter_fusion.4
  892.3 14.8 scatter_custom_fusion.32
  907.1 14.8 scatter_custom_fusion.31
  921.9 14.8 scatter_custom_fusion.34
  936.7 14.7 scatter_fusion.5
  951.5 120.0 %psum.119 = f32[3,1027]{1,0:T(4,128)S(1)} all-reduce(f32[3,1027]{1,0:T(4,128)S(1)} %pad_maximum_fusion.2), channel_id=1, replica_groups=mesh['tm'=8,'star'=32] {'star'}, use_global_device_ids=true, to_apply=%region_53.56 | all-reduce | flops 3081 | bytes 24648 | tf_op jit(solution)/shard_map/psum | solution.py:69
  1072.1 11.5 scatter_custom_fusion.35
  1083.7 77.4 %psum.120 = f32[2048]{0:T(1024)S(1)} all-reduce(f32[2048]{0:T(1024)S(1)} %scatter_custom_fusion.35), channel_id=1, replica_groups=mesh['tm'=8,'star'=32] {'tm','star'}, use_global_device_ids=true, to_apply=%region_56.59 | all-reduce | flops 2048 | bytes 16384 | tf_op jit(solution)/shard_map/psum | solution.py:70
  1164.7 11.4 scatter_custom_fusion.18
  1176.1 11.4 scatter_custom_fusion.19
  1187.5 11.4 scatter_custom_fusion.20
  1223.8 63.3 %all-reduce.6.cloned.1.call-done = f32[5,4096]{1,0:T(8,128)} async-done(((f32[5,4096]{1,0:T(8,128)}), f32[5,4096]{1,0:T(8,128)}) %all-reduce.6.cloned.1.call-update) | async-done | bytes 81936 | tf_op jit(solution)/shard_map/psum | solution.py:71
  1289.3 79.6 %psum.121 = f32[]{:T(128)} all-reduce(f32[]{:T(128)S(6)} %add.397), channel_id=1, replica_groups=mesh['tm'=8,'star'=32] {'tm','star'}, use_global_device_ids=true, to_apply=%region_58.61 | all-reduce | flops 1 | bytes 8 | tf_op jit(solution)/shard_map/psum | solution.py:77
  1386.5 20.6 gather_fusion.1
  1451.4 75.2 %psum.122 = f32[]{:T(128)} all-reduce(f32[]{:T(128)} %get-tuple-element.16), channel_id=1, replica_groups=mesh['tm'=8,'star'=32] {'tm','star'}, use_global_device_ids=true, to_apply=%region_65.68 | all-reduce | flops 1 | bytes 8 | tf_op jit(solution)/shard_map/psum | solution.py:51
  1530.2 14.8 scatter_custom_fusion.42
  1545.0 14.8 scatter_custom_fusion.41
  1559.8 14.8 scatter_custom_fusion.44
  1574.6 14.8 scatter_fusion.6
  1589.5 14.8 scatter_custom_fusion.46
  1604.3 15.2 scatter_custom_fusion.45
  1619.5 14.8 scatter_custom_fusion.48
  1634.4 14.7 scatter_fusion.7
  1649.1 14.8 scatter_custom_fusion.50
  1663.9 14.8 scatter_custom_fusion.49
  1678.7 14.8 scatter_custom_fusion.52
  1693.5 14.7 scatter_fusion.8
  1708.3 119.7 %psum.124 = f32[3,1027]{1,0:T(4,128)S(1)} all-reduce(f32[3,1027]{1,0:T(4,128)S(1)} %pad_maximum_fusion.4), channel_id=1, replica_groups=mesh['tm'=8,'star'=32] {'star'}, use_global_device_ids=true, to_apply=%region_85.88 | all-reduce | flops 3081 | bytes 24648 | tf_op jit(solution)/shard_map/psum | solution.py:69
  1828.1 11.5 scatter_custom_fusion.53
  1839.6 76.5 %psum.125 = f32[2048]{0:T(1024)S(1)} all-reduce(f32[2048]{0:T(1024)S(1)} %scatter_custom_fusion.53), channel_id=1, replica_groups=mesh['tm'=8,'star'=32] {'tm','star'}, use_global_device_ids=true, to_apply=%region_88.91 | all-reduce | flops 2048 | bytes 16384 | tf_op jit(solution)/shard_map/psum | solution.py:70
  1920.6 11.4 scatter_custom_fusion.36
  1932.0 11.6 scatter_custom_fusion.37
  1943.6 11.4 scatter_custom_fusion.38
  1955.0 11.4 scatter_custom_fusion.39
  1966.4 12.0 scatter_custom_fusion.40
  1981.2 62.6 %all-reduce.8.cloned.1.call-done = f32[5,4096]{1,0:T(8,128)} async-done(((f32[5,4096]{1,0:T(8,128)}), f32[5,4096]{1,0:T(8,128)}) %all-reduce.8.cloned.1.call-update) | async-done | bytes 81936 | tf_op jit(solution)/shard_map/psum | solution.py:71
  2046.0 79.6 %psum.126 = f32[]{:T(128)} all-reduce(f32[]{:T(128)S(6)} %add.413), channel_id=1, replica_groups=mesh['tm'=8,'star'=32] {'tm','star'}, use_global_device_ids=true, to_apply=%region_90.93 | all-reduce | flops 1 | bytes 8 | tf_op jit(solution)/shard_map/psum | solution.py:77
  2143.6 20.7 gather_fusion.2
  2209.7 75.2 %psum.127 = f32[]{:T(128)} all-reduce(f32[]{:T(128)} %multiply_reduce_fusion.6), channel_id=1, replica_groups=mesh['tm'=8,'star'=32] {'tm','star'}, use_global_device_ids=true, to_apply=%region_97.100 | all-reduce | flops 1 | bytes 8 | tf_op jit(solution)/shard_map/psum | solution.py:51
  (301 shorter events, 310.7 us)
Async XLA Ops:
  7.2 544.3 %all-reduce.4.cloned.1.call-start = ((), (), s32[]{:S(2)}) async-start(), calls=%async_computation | async-start | bytes 262144 | tf_op jit(solution)/shard_map/psum | solution.py:71
  10.7 762.7 %copy-start.27 = (f32[1,2048]{1,0:T(1,128)}, f32[1,2048]{1,0:T(1,128)S(1)}, u32[]{:S(2)}) copy-start(f32[1,2048]{1,0:T(1,128)S(1)} %get-tuple-element.38) | copy-start | bytes 24580
  10.7 762.7 %copy-start.29 = (f32[1,2048]{1,0:T(1,128)}, f32[1,2048]{1,0:T(1,128)S(1)}, u32[]{:S(2)}) copy-start(f32[1,2048]{1,0:T(1,128)S(1)} %get-tuple-element.39) | copy-start | bytes 24580
  10.7 762.7 %copy-start.38 = (f32[1,2048]{1,0:T(1,128)}, f32[1,2048]{1,0:T(1,128)S(1)}, u32[]{:S(2)}) copy-start(f32[1,2048]{1,0:T(1,128)S(1)} %get-tuple-element.36) | copy-start | bytes 24580
  93.9 679.6 %copy-start.31 = (f32[1,2048]{1,0:T(1,128)}, f32[1,2048]{1,0:T(1,128)S(1)}, u32[]{:S(2)}) copy-start(f32[1,2048]{1,0:T(1,128)S(1)} %get-tuple-element.40) | copy-start | bytes 24580
  93.9 679.6 %copy-start.33 = (f32[1,2048]{1,0:T(1,128)}, f32[1,2048]{1,0:T(1,128)S(1)}, u32[]{:S(2)}) copy-start(f32[1,2048]{1,0:T(1,128)S(1)} %get-tuple-element.41) | copy-start | bytes 24580
  93.9 679.6 %copy-start.35 = (f32[1,2048]{1,0:T(1,128)}, f32[1,2048]{1,0:T(1,128)S(1)}, u32[]{:S(2)}) copy-start(f32[1,2048]{1,0:T(1,128)S(1)} %get-tuple-element.42) | copy-start | bytes 24580
  94.0 679.6 %copy-start.36 = (f32[1,2048]{1,0:T(1,128)}, f32[1,2048]{1,0:T(1,128)S(1)}, u32[]{:S(2)}) copy-start(f32[1,2048]{1,0:T(1,128)S(1)} %get-tuple-element.43) | copy-start | bytes 24580
  94.0 679.6 %copy-start.37 = (f32[1,2048]{1,0:T(1,128)}, f32[1,2048]{1,0:T(1,128)S(1)}, u32[]{:S(2)}) copy-start(f32[1,2048]{1,0:T(1,128)S(1)} %get-tuple-element.44) | copy-start | bytes 24580
  95.3 119.0 %copy-start.73 = (s32[2048]{0:T(1024)}, s32[2048]{0:T(1024)S(1)}, u32[]{:S(2)}) copy-start(s32[2048]{0:T(1024)S(1)} %get-tuple-element.87) | copy-start | bytes 24580
  95.3 148.6 %copy-start.72 = (s32[2048]{0:T(1024)}, s32[2048]{0:T(1024)S(1)}, u32[]{:S(2)}) copy-start(s32[2048]{0:T(1024)S(1)} %get-tuple-element.85) | copy-start | bytes 24580
  95.3 563.1 %copy-start.41 = (s32[2048]{0:T(1024)}, s32[2048]{0:T(1024)S(1)}, u32[]{:S(2)}) copy-start(s32[2048]{0:T(1024)S(1)} %get-tuple-element.89) | copy-start | bytes 24580
  95.3 588.9 %copy-start.39 = (s32[2048]{0:T(1024)}, s32[2048]{0:T(1024)S(1)}, u32[]{:S(2)}) copy-start(s32[2048]{0:T(1024)S(1)} %get-tuple-element.88) | copy-start | bytes 24580
  140.9 29.4 %copy-start.68 = (s32[2048]{0:T(1024)S(1)}, s32[2048]{0:T(1024)}, u32[]{:S(2)}) copy-start(s32[2048]{0:T(1024)} %param.17) | copy-start | bytes 24580
  258.5 138.0 %copy-start.67 = (s32[2048]{0:T(1024)S(1)}, s32[2048]{0:T(1024)}, u32[]{:S(2)}) copy-start(s32[2048]{0:T(1024)} %param.16) | copy-start | bytes 24580
  258.5 195.2 %copy-start.23 = (f32[5,2048]{1,0:T(8,128)S(1)}, f32[5,2048]{1,0:T(8,128)}, u32[]{:S(2)}) copy-start(f32[5,2048]{1,0:T(8,128)} %param.12) | copy-start | bytes 122884
  258.6 196.1 %copy-start.18 = (f32[12,2048]{1,0:T(8,128)S(1)}, f32[12,2048]{1,0:T(8,128)}, u32[]{:S(2)}) copy-start(f32[12,2048]{1,0:T(8,128)} %param.13) | copy-start | bytes 294916
  258.6 197.4 %copy-start.71 = (s32[2048]{0:T(1024)S(1)}, s32[2048]{0:T(1024)}, u32[]{:S(2)}) copy-start(s32[2048]{0:T(1024)} %param.18) | copy-start | bytes 24580
  392.8 63.8 %copy-start.48 = (f32[3,1027]{1,0:T(4,128)}, f32[3,1027]{1,0:T(4,128)S(1)}, u32[]{:S(2)}) copy-start(f32[3,1027]{1,0:T(4,128)S(1)} %psum.114) | copy-start | bytes 36976
  393.4 156.1 %collective-permute-start = (f32[3,3]{1,0:T(4,128)}, f32[3,3]{1,0:T(4,128)}, u32[]{:S(2)}, u32[]{:S(2)}) collective-permute-start(f32[3,3]{1,0:T(4,128)} %slice.211), channel_id=1, source_target_pairs={{0,32},{32,64},{64,96},{96,128},{128,160},{160,192},{192,224},{1,3... | collective-permute-start | bytes 116 | tf_op jit(solution)/shard_map/ppermute | solution.py:16
  453.6 833.4 %all-reduce.6.cloned.1.call-start = ((), (), s32[]{:S(2)}) async-start(), calls=%async_computation.1 | async-start | bytes 262144 | tf_op jit(solution)/shard_map/psum | solution.py:71
  453.7 918.9 %copy-start.26 = (s32[2048]{0:T(1024)}, s32[2048]{0:T(1024)S(1)}, u32[]{:S(2)}) copy-start(s32[2048]{0:T(1024)S(1)} %fusion.51) | copy-start | bytes 24580
  545.2 824.5 %copy-start.21 = (f32[2048]{0:T(1024)}, f32[2048]{0:T(1024)S(1)}, u32[]{:S(2)}) copy-start(f32[2048]{0:T(1024)S(1)} %psum.115) | copy-start | bytes 24580
  553.7 89.9 %copy-start.47 = (s32[2048]{0:T(1024)S(1)}, s32[2048]{0:T(1024)}, u32[]{:S(2)}) copy-start(s32[2048]{0:T(1024)} %fusion.15) | copy-start | bytes 24580
  630.2 739.3 %copy-start.16 = (f32[3,1024]{1,0:T(4,128)}, f32[3,1024]{1,0:T(4,128)S(1)}, u32[]{:S(2)}) copy-start(f32[3,1024]{1,0:T(4,128)S(1)} %broadcast_divide_fusion.4) | copy-start | bytes 36868
  633.2 24.2 %collective-permute-start.1 = (f32[3,3]{1,0:T(4,128)S(1)}, f32[3,3]{1,0:T(4,128)S(1)}, u32[]{:S(2)}, u32[]{:S(2)}) collective-permute-start(f32[3,3]{1,0:T(4,128)S(1)} %slice.213), channel_id=1, source_target_pairs={{32,0},{64,32},{96,64},{128,96},{160,128},{192,160},{224,192},{33,... | collective-permute-start | bytes 116 | tf_op jit(solution)/shard_map/ppermute | solution.py:16
  643.6 11.8 copy-start.64
  655.4 11.6 copy-start.43
  655.4 20.2 copy-start.45
  655.4 37.4 %copy-start.58 = (pred[2048]{0:T(1024)(128)(4,1)S(1)}, pred[2048]{0:T(1024)(128)(4,1)}, u32[]{:S(2)}) copy-start(pred[2048]{0:T(1024)(128)(4,1)} %get-tuple-element.81) | copy-start | bytes 6148
  657.3 37.6 %copy-start.63 = (pred[2048]{0:T(1024)(128)(4,1)S(1)}, pred[2048]{0:T(1024)(128)(4,1)}, u32[]{:S(2)}) copy-start(pred[2048]{0:T(1024)(128)(4,1)} %get-tuple-element.82) | copy-start | bytes 6148
  692.8 2.7 copy-start
  692.8 2.7 copy-start.10
  692.9 2.7 copy-start.61
  697.7 135.4 %copy-start.50 = (f32[2048]{0:T(1024)}, f32[2048]{0:T(1024)S(1)}, u32[]{:S(2)}) copy-start(f32[2048]{0:T(1024)S(1)} %get-tuple-element.21) | copy-start | bytes 24580
  936.7 350.3 %copy-start.6 = (f32[5,4096]{1,0:T(8,128)S(1)}, f32[5,4096]{1,0:T(8,128)}, u32[]{:S(2)}) copy-start(f32[5,4096]{1,0:T(8,128)} %all-reduce.4.cloned.1.call-done) | copy-start | bytes 245764
  1162.3 60.2 %collective-permute-start.2 = (f32[3,3]{1,0:T(4,128)}, f32[3,3]{1,0:T(4,128)S(1)}, u32[]{:S(2)}, u32[]{:S(2)}) collective-permute-start(f32[3,3]{1,0:T(4,128)} %slice.215), channel_id=1, source_target_pairs={{0,32},{32,64},{64,96},{96,128},{128,160},{160,192},{192,224},{1,3... | collective-permute-start | bytes 116 | tf_op jit(solution)/shard_map/ppermute | solution.py:16
  1222.4 821.4 %all-reduce.8.cloned.1.call-start = ((), (), s32[]{:S(2)}) async-start(), calls=%async_computation.2 | async-start | bytes 262144 | tf_op jit(solution)/shard_map/psum | solution.py:71
  1369.7 756.6 %copy-start.14 = (f32[3,1024]{1,0:T(4,128)}, f32[3,1024]{1,0:T(4,128)S(1)}, u32[]{:S(2)}) copy-start(f32[3,1024]{1,0:T(4,128)S(1)} %broadcast_divide_fusion.3) | copy-start | bytes 36868
  1384.8 25.4 %copy-start.44 = (s32[2048]{0:T(1024)S(1)}, s32[2048]{0:T(1024)}, u32[]{:S(2)}) copy-start(s32[2048]{0:T(1024)} %get-tuple-element.84) | copy-start | bytes 24580
  1384.8 34.0 %copy-start.46 = (s32[2048]{0:T(1024)S(1)}, s32[2048]{0:T(1024)}, u32[]{:S(2)}) copy-start(s32[2048]{0:T(1024)} %get-tuple-element.83) | copy-start | bytes 24580
  1384.8 42.6 %copy-start.42 = (s32[2048]{0:T(1024)S(1)}, s32[2048]{0:T(1024)}, u32[]{:S(2)}) copy-start(s32[2048]{0:T(1024)} %copy-done.41) | copy-start | bytes 24580
  1384.8 51.2 %copy-start.40 = (s32[2048]{0:T(1024)S(1)}, s32[2048]{0:T(1024)}, u32[]{:S(2)}) copy-start(s32[2048]{0:T(1024)} %copy-done.39) | copy-start | bytes 24580
  1384.8 22.3 collective-permute-start.3
  1418.8 27.8 %copy-start.62 = (pred[2048]{0:T(1024)(128)(4,1)S(1)}, pred[2048]{0:T(1024)(128)(4,1)}, u32[]{:S(2)}) copy-start(pred[2048]{0:T(1024)(128)(4,1)} %get-tuple-element.79) | copy-start | bytes 6148
  1444.7 4.1 copy-start.13
  1444.7 4.1 copy-start.59
  1446.7 2.8 copy-start.4
  1446.7 2.8 copy-start.11
  1446.7 2.8 copy-start.56
  1448.8 79.9 %copy-start.28 = (f32[1,2048]{1,0:T(1,128)S(1)}, f32[1,2048]{1,0:T(1,128)}, u32[]{:S(2)}) copy-start(f32[1,2048]{1,0:T(1,128)} %copy-done.27) | copy-start | bytes 24580
  1448.8 79.9 %copy-start.30 = (f32[1,2048]{1,0:T(1,128)S(1)}, f32[1,2048]{1,0:T(1,128)}, u32[]{:S(2)}) copy-start(f32[1,2048]{1,0:T(1,128)} %copy-done.29) | copy-start | bytes 24580
  1448.8 79.9 %copy-start.32 = (f32[1,2048]{1,0:T(1,128)S(1)}, f32[1,2048]{1,0:T(1,128)}, u32[]{:S(2)}) copy-start(f32[1,2048]{1,0:T(1,128)} %copy-done.31) | copy-start | bytes 24580
  1448.8 79.9 %copy-start.34 = (f32[1,2048]{1,0:T(1,128)S(1)}, f32[1,2048]{1,0:T(1,128)}, u32[]{:S(2)}) copy-start(f32[1,2048]{1,0:T(1,128)} %copy-done.33) | copy-start | bytes 24580
  1574.6 59.7 %copy-start.54 = (f32[2048]{0:T(1024)S(1)}, f32[2048]{0:T(1024)}, u32[]{:S(2)}) copy-start(f32[2048]{0:T(1024)} %get-tuple-element.51) | copy-start | bytes 24580
  1634.4 59.2 %copy-start.53 = (f32[2048]{0:T(1024)S(1)}, f32[2048]{0:T(1024)}, u32[]{:S(2)}) copy-start(f32[2048]{0:T(1024)} %get-tuple-element.47) | copy-start | bytes 24580
  1917.4 62.5 %collective-permute-start.4 = (f32[3,3]{1,0:T(4,128)S(1)}, f32[3,3]{1,0:T(4,128)S(1)}, u32[]{:S(2)}, u32[]{:S(2)}) collective-permute-start(f32[3,3]{1,0:T(4,128)S(1)} %slice.219), channel_id=1, source_target_pairs={{0,32},{32,64},{64,96},{96,128},{128,160},{160,192},{192,224},{1,3... | collective-permute-start | bytes 116 | tf_op jit(solution)/shard_map/ppermute | solution.py:16
  2127.0 37.2 %collective-permute-start.5 = (f32[3,3]{1,0:T(4,128)}, f32[3,3]{1,0:T(4,128)}, u32[]{:S(2)}, u32[]{:S(2)}) collective-permute-start(f32[3,3]{1,0:T(4,128)} %slice.221), channel_id=1, source_target_pairs={{32,0},{64,32},{96,64},{128,96},{160,128},{192,160},{224,192},{33,... | collective-permute-start | bytes 116 | tf_op jit(solution)/shard_map/ppermute | solution.py:16
  2164.2 40.6 %copy-start.2 = (f32[3,2048]{0,1:T(8,128)S(1)}, f32[3,2048]{0,1:T(8,128)}, u32[]{:S(2)}) copy-start(f32[3,2048]{0,1:T(8,128)} %copy.98) | copy-start | bytes 73732
  2204.8 2.7 copy-start.8
  2207.6 78.2 %copy-start.22 = (f32[2048]{0:T(1024)S(1)}, f32[2048]{0:T(1024)}, u32[]{:S(2)}) copy-start(f32[2048]{0:T(1024)} %copy-done.21) | copy-start | bytes 24580
  2207.6 78.8 %copy-start.15 = (f32[3,1024]{1,0:T(4,128)S(1)}, f32[3,1024]{1,0:T(4,128)}, u32[]{:S(2)}) copy-start(f32[3,1024]{1,0:T(4,128)} %copy-done.14) | copy-start | bytes 36868
  2207.6 78.8 %copy-start.17 = (f32[3,1024]{1,0:T(4,128)S(1)}, f32[3,1024]{1,0:T(4,128)}, u32[]{:S(2)}) copy-start(f32[3,1024]{1,0:T(4,128)} %copy-done.16) | copy-start | bytes 36868
  2207.6 78.8 %copy-start.25 = (f32[3,1024]{1,0:T(4,128)S(1)}, f32[3,1024]{1,0:T(4,128)}, u32[]{:S(2)}) copy-start(f32[3,1024]{1,0:T(4,128)} %copy-done.24) | copy-start | bytes 36868
  (19 other events, 32.9 us)
Sparse Core Ops, SparseCore 0:
  453.7 66.2 all-reduce.3
  1222.6 64.4 all-reduce.5
  1979.9 63.8 all-reduce.7
where the time goes:
time: 2310 us; the launch traced here: 2290 us
  blocking collectives  1130 us (49%)
  other arithmetic  785 us (34%)
  local copies, waits for them, and re-layouts  212 us (9%)
  waiting for transfers between devices  126 us (5%)
  between operations  27.6 us (1%)
    scatter-add x36, other arithmetic, shards(): jax.ops.segment_sum(att_coef[3 * j + a] * masked, knot_index + j, num_seg...  532 us
    psum x3, blocking collectives, shards(): knot_sum = lax.psum(jnp.stack(knot_parts), 'star')  359 us
    psum x4, blocking collectives, shards(): beta = jnp.sqrt(lax.psum(jnp.sum(update * update), ('tm', 'star')))  307 us
    psum x3, blocking collectives, shards(): lax.psum(star_weight * jnp.sum(nextv[0] * nextv[0]) + att_weight * jnp.su...  234 us
    psum x3, blocking collectives, shards(): cals = lax.psum(cal_part, ('tm', 'star'))  231 us
    scatter-add x15, other arithmetic, shards(): jax.ops.segment_sum(star_coef[p] * masked, star_index, num_segments=STAR_...  171 us
    psum x3, waiting for transfers between devices, shards(): star_sum = lax.psum(star_part, 'tm')  126 us
    gather x12, local copies, waits for them, and re-layouts, shards(): taken = jnp.take(extended, knot_index + forward_j, axis=1)  106 us
  transfers between devices with their start and end apart: 9, of which 2 were waited for; matrix products, arithmetic and copies ran while one was open for 12% of the time, Pallas kernels for 0%

commit v1 on v0

v1 whole, which is shorter than its diff:
```python
import functools

import jax
import jax.numpy as jnp
from jax import lax
from jax.experimental import pallas as pl
from jax.experimental.pallas import tpu as pltpu
from jax.sharding import PartitionSpec as P

ROWS = 2048
LO = 128
CHUNK = 512
N_S, N_C, N_B, N_K = 160, 16, 8, 24
N_ALL = N_S + N_C + N_B + N_K
N_Z = N_S + N_C + N_B
SCALAR_LANE = 64
F32, BF16 = jnp.float32, jnp.bfloat16


def iota(shape, axis):
    return lax.broadcasted_iota(jnp.int32, shape, axis)


def split(value):
    first = value.astype(BF16)
    return first, (value - first.astype(F32)).astype(BF16)


def total(value):
    return jnp.sum(jnp.sum(value, axis=1, keepdims=True), axis=0, keepdims=True)


def one_hot(index, count):
    return jnp.where(iota((count, index.shape[1]), 0) == index, 1.0, 0.0)


def chunk_hots(index_ref, columns, count):
    index = index_ref[:, columns]
    low = one_hot(index & (LO - 1), LO).astype(BF16)
    return low, one_hot(index >> 7, count)


def left_shift(knots, following, j):
    if j == 0:
        return knots
    rolled = pltpu.roll(knots, LO - j, 1)
    upper = pltpu.roll(rolled, 7, 0)
    ahead = pltpu.roll(jnp.broadcast_to(following, (8, LO)), LO - j, 1)
    upper = jnp.where(iota((8, LO), 0) == 7, ahead, upper)
    return jnp.where(iota((8, LO), 1) < LO - j, rolled, upper)


def head_rows(bounds, window):
    row = jnp.sum(jnp.where(iota((8, LO), 0) == window, bounds, 0.0), axis=0, keepdims=True)
    lane = iota((1, LO), 1)
    return [jnp.where(lane < 3, row if a == 0 else pltpu.roll(row, LO - 8 * a, 1), 0.0) for a in range(3)]


def with_heads(vec, window):
    bounds = vec[N_S + N_C : N_Z]
    own, following = head_rows(bounds, window), head_rows(bounds, window + 1)
    knots = []
    for a in range(3):
        part = vec[N_Z + 8 * a : N_Z + 8 * a + 8]
        knots.append(part + jnp.where(iota((8, LO), 0) == 0, jnp.broadcast_to(own[a], (8, LO)), 0.0))
    return knots, following


def forward(vec, window, refs, live, out_ref):
    star_ref, att_ref, cal_ref, _, si_ref, ki_ref, ci_ref = refs
    knots, following = with_heads(vec, window)
    shifted = jnp.concatenate(
        [left_shift(knots[a], following[a], j) for j in range(4) for a in range(3)], axis=0
    )
    tables = [
        jnp.concatenate(split(table), axis=1)
        for table in (vec[:N_S], shifted, vec[N_S : N_S + N_C])
    ]
    for start in range(0, ROWS, CHUNK):
        columns = pl.ds(start, CHUNK)
        result = None
        for table, index_ref, coef_ref, count in zip(
            tables, (si_ref, ki_ref, ci_ref), (star_ref, att_ref, cal_ref), (32, 8, 16)
        ):
            low, high = chunk_hots(index_ref, columns, count)
            taken = jnp.dot(table, jnp.concatenate([low, low], axis=0), preferred_element_type=F32)
            mixed = None
            for p in range(coef_ref.shape[0]):
                term = coef_ref[p : p + 1, columns] * taken[p * count : (p + 1) * count]
                mixed = term if mixed is None else mixed + term
            mixed = mixed * high
            for part in range(0, count, 8):
                piece = mixed[part : part + 8]
                result = piece if result is None else result + piece
        out_ref[:, columns] = jnp.sum(result, axis=0, keepdims=True) * live[:, start : start + CHUNK]


def adjoint(row_ref, window, refs):
    star_ref, att_ref, cal_ref, _, si_ref, ki_ref, ci_ref = refs
    sums = [None, None, None]
    for start in range(0, ROWS, CHUNK):
        columns = pl.ds(start, CHUNK)
        row = row_ref[:, columns]
        for which, (index_ref, coef_ref, count) in enumerate(
            zip((si_ref, ki_ref, ci_ref), (star_ref, att_ref, cal_ref), (32, 8, 16))
        ):
            low, high = chunk_hots(index_ref, columns, count)
            pieces = split(coef_ref[:, columns] * row)
            left = jnp.concatenate(
                [
                    (high * piece[p : p + 1].astype(F32)).astype(BF16)
                    for piece in pieces
                    for p in range(coef_ref.shape[0])
                ],
                axis=0,
            )
            added = lax.dot_general(left, low, (((1,), (1,)), ((), ())), preferred_element_type=F32)
            sums[which] = added if sums[which] is None else sums[which] + added
    stars, spread, cals = (item[: item.shape[0] // 2] + item[item.shape[0] // 2 :] for item in sums)
    rows, lanes = iota((8, LO), 0), iota((8, LO), 1)
    knots, heads, tails = [], 0.0, 0.0
    for a in range(3):
        own, over = spread[8 * a : 8 * a + 8], jnp.zeros((8, LO), F32)
        for j in range(1, 4):
            rolled = pltpu.roll(spread[24 * j + 8 * a : 24 * j + 8 * a + 8], j, 1)
            wrapped = pltpu.roll(rolled, 1, 0)
            own = own + jnp.where(lanes >= j, rolled, jnp.where(rows > 0, wrapped, 0.0))
            over = over + jnp.where(lanes < j, wrapped, 0.0)
        is_head = jnp.logical_and(rows == 0, lanes < 3)
        knots.append(jnp.where(is_head, 0.0, own))
        head, tail = jnp.where(is_head, own, 0.0), jnp.where(rows == 0, over, 0.0)
        if a > 0:
            head, tail = pltpu.roll(head, 8 * a, 1), pltpu.roll(tail, 8 * a, 1)
        heads, tails = heads + head, tails + tail
    head = jnp.broadcast_to(heads[:1], (8, LO))
    tail = jnp.broadcast_to(tails[:1], (8, LO))
    bounds = jnp.where(rows == window, head, 0.0) + jnp.where(rows == window + 1, tail, 0.0)
    return stars, cals, bounds, jnp.concatenate(knots, axis=0)


def write_sums(parts, scalars, scale, sum_refs):
    stars, cals, bounds, knots = parts
    wide_ref, knot_ref = sum_refs
    rows, lanes = iota((8, LO), 0), iota((8, LO), 1)
    block = bounds * scale
    for i, scalar in enumerate(scalars):
        block = jnp.where(jnp.logical_and(rows == i, lanes == SCALAR_LANE), jnp.broadcast_to(scalar, (8, LO)), block)
    wide_ref[:N_S] = stars * scale
    wide_ref[N_S : N_S + N_C] = cals * scale
    wide_ref[N_S + N_C :] = block
    knot_ref[...] = knots * scale


def read_sums(stars_ref, rest_ref):
    rest = rest_ref[...]
    bounds = rest[N_C : N_C + N_B]
    rows, lanes = iota((8, LO), 0), iota((8, LO), 1)
    scalars = [
        total(jnp.where(jnp.logical_and(rows == i, lanes == SCALAR_LANE), bounds, 0.0)) for i in range(3)
    ]
    bounds = jnp.where(lanes < SCALAR_LANE, bounds, 0.0)
    vec = jnp.concatenate([stars_ref[...], rest[:N_C], bounds, rest[N_C + N_B :]], axis=0)
    return vec, scalars


def square(vec):
    part = vec * vec
    return (
        total(part[:N_S]) * (1.0 / 8)
        + total(part[N_S:N_Z]) * (1.0 / 256)
        + total(part[N_Z:]) * (1.0 / 32)
    )


def live_rows(blocks_ref):
    return jnp.where(iota((1, ROWS), 1) < 128 * blocks_ref[0, 0], 1.0, 0.0)


def keep(scalars, ref):
    rows = iota((8, LO), 0)
    block = jnp.zeros((8, LO), F32)
    for i, scalar in enumerate(scalars):
        block = jnp.where(rows == i, jnp.broadcast_to(scalar, (8, LO)), block)
    ref[...] = block


def kept(ref):
    return [ref[i : i + 1, 0:1] for i in range(8)]


def start_kernel(blocks_ref, window_ref, *args):
    refs, (wide_ref, knot_ref, row_ref) = args[:7], args[7:]
    live = live_rows(blocks_ref)
    row_ref[...] = refs[3][...] * live
    norm = total(row_ref[...] * row_ref[...])
    size = 0.0
    for coef_ref in refs[:3]:
        coef = coef_ref[...]
        size = size + total(jnp.sum(coef * coef, axis=0, keepdims=True) * live)
    write_sums(adjoint(row_ref, window_ref[0], refs), [norm, size], 1.0, (wide_ref, knot_ref))


def first_kernel(blocks_ref, window_ref, *args):
    refs, (stars_ref, rest_ref), outs = args[:7], args[7:9], args[9:]
    wide_ref, knot_ref, grad_ref, row_ref, kept_ref = outs
    live = live_rows(blocks_ref)
    vec, (norm, size, _) = read_sums(stars_ref, rest_ref)
    inverse, length = lax.rsqrt(size), jnp.sqrt(norm)
    grad = vec * inverse / length
    grad_ref[...] = grad
    forward(grad, window_ref[0], refs, live * inverse, row_ref)
    row = row_ref[...]
    keep([inverse, length], kept_ref)
    parts = adjoint(row_ref, window_ref[0], refs)
    write_sums(parts, [square(grad), total(row * row)], inverse, (wide_ref, knot_ref))


def second_kernel(blocks_ref, window_ref, *args):
    refs, (stars_ref, rest_ref, grad_ref, q_ref, old_ref), outs = args[:7], args[7:12], args[12:]
    wide_ref, knot_ref, new_ref, image_ref, row_ref, kept_ref = outs
    live = live_rows(blocks_ref)
    inverse, length = kept(old_ref)[:2]
    image, (gamma, delta, _) = read_sums(stars_ref, rest_ref)
    image_ref[...] = image
    grad = grad_ref[...] - (gamma / delta) * image
    new_ref[...] = grad
    forward(grad, window_ref[0], refs, live * inverse, row_ref)
    row = row_ref[...]
    keep([inverse, length, gamma, delta], kept_ref)
    parts = adjoint(row_ref, window_ref[0], refs)
    write_sums(parts, [square(grad), total(row * row), total(row * q_ref[...])], inverse, (wide_ref, knot_ref))


def third_kernel(blocks_ref, window_ref, *args):
    refs, ins, outs = args[:7], args[7:15], args[15:]
    stars_ref, rest_ref, first_ref, grad_ref, image_ref, q_ref, row_ref, old_ref = ins
    new_ref, x_ref, direction_ref, kept_ref, scalar_ref, work_ref = outs
    live = live_rows(blocks_ref)
    inverse, length, gamma0, delta0 = kept(old_ref)[:4]
    image, (gamma1, square1, cross1) = read_sums(stars_ref, rest_ref)
    beta = gamma1 / gamma0
    first, grad = first_ref[...], grad_ref[...]
    direction = grad + beta * first
    q = row_ref[...] + beta * q_ref[...]
    delta1 = square1 + 2.0 * beta * cross1 + beta * beta * delta0
    image = image + beta * image_ref[...]
    step = gamma1 / delta1
    x_ref[...] = (gamma0 / delta0) * first + step * direction
    direction_ref[...] = direction
    grad = grad - step * image
    new_ref[...] = grad
    forward(grad, window_ref[0], refs, live * inverse, work_ref)
    row = work_ref[...]
    keep([inverse, length, gamma1, delta1], kept_ref)
    lane = iota((1, LO), 1)
    scalar_ref[...] = (
        jnp.where(lane == 0, square(grad), 0.0)
        + jnp.where(lane == 1, total(row * row), 0.0)
        + jnp.where(lane == 2, total(row * q), 0.0)
    )


def last_kernel(window_ref, sums_ref, grad_ref, x_ref, direction_ref, old_ref, star_ref, att_ref, cal_ref):
    inverse, length, gamma1, delta1 = kept(old_ref)[:4]
    sums = jnp.sum(sums_ref[...], axis=0, keepdims=True)
    gamma2, square2, cross2 = (sums[:, i : i + 1] for i in range(3))
    beta = gamma2 / gamma1
    delta2 = square2 + 2.0 * beta * cross2 + beta * beta * delta1
    direction = grad_ref[...] + beta * direction_ref[...]
    x = (x_ref[...] + (gamma2 / delta2) * direction) * (inverse * length)
    for hi in range(32):
        for p in range(5):
            star_ref[p : p + 1, LO * hi : LO * hi + LO] = x[32 * p + hi : 32 * p + hi + 1]
    knots, _ = with_heads(x, window_ref[0])
    for a in range(3):
        for hi in range(8):
            att_ref[a : a + 1, LO * hi : LO * hi + LO] = knots[a][hi : hi + 1]
    cal_ref[...] = x[N_S : N_S + N_C]


def call(kernel, smem, vmem, outs, scratch=()):
    return pl.pallas_call(
        kernel,
        out_shape=[jax.ShapeDtypeStruct(shape, F32) for shape in outs],
        in_specs=[pl.BlockSpec(memory_space=pltpu.SMEM)] * len(smem)
        + [pl.BlockSpec(memory_space=pltpu.VMEM)] * len(vmem),
        out_specs=[pl.BlockSpec(memory_space=pltpu.VMEM)] * len(outs),
        scratch_shapes=list(scratch),
        compiler_params=pltpu.CompilerParams(vmem_limit_bytes=40 * 1024 * 1024),
    )(*smem, *vmem)


def swap(value, axis, bits):
    count = lax.axis_size(axis)
    return lax.ppermute(value, axis, [(i, i ^ bits) for i in range(count)])


def reduce(wide, knots):
    for bits in (1, 2, 6):
        wide = wide + swap(wide, "tm", bits)
    rest = jnp.concatenate([wide[N_S:], knots], axis=0)
    rest = rest + swap(rest, "star", 1)
    for near, wrap, far in ((8, 24, 16), (2, 6, 4)):
        arrived = [swap(rest, "star", bits) for bits in (near, wrap, far)]
        rest = (rest + arrived[0]) + (arrived[1] + arrived[2])
    return wide[:N_S], rest


def shards(star_coef, att_coef, cal_coef, observed, star_index, knot_index, cal_index, valid_blocks):
    window = lax.axis_index("tm").astype(jnp.int32).reshape(1)
    smem = (valid_blocks, window)
    rows = (
        star_coef,
        att_coef,
        cal_coef.reshape(1, ROWS),
        observed.reshape(1, ROWS),
        star_index.reshape(1, ROWS),
        knot_index.reshape(1, ROWS),
        cal_index.reshape(1, ROWS),
    )
    wide_shape, knot_shape, vec_shape = (N_Z, LO), (N_K, LO), (N_ALL, LO)
    row_shape, small = (1, ROWS), (8, LO)
    sums = (wide_shape, knot_shape)
    row_scratch = [pltpu.VMEM(row_shape, F32)]
    wide, knots = call(start_kernel, smem, rows, sums, row_scratch)
    arrived = reduce(wide, knots)
    wide, knots, grad0, row0, scalars = call(
        first_kernel, smem, rows + arrived, sums + (vec_shape, row_shape, small)
    )
    arrived = reduce(wide, knots)
    wide, knots, grad1, image0, row1, scalars = call(
        second_kernel,
        smem,
        rows + arrived + (grad0, row0, scalars),
        sums + (vec_shape, vec_shape, row_shape, small),
    )
    arrived = reduce(wide, knots)
    grad2, x, direction, scalars, partial = call(
        third_kernel,
        smem,
        rows + arrived + (grad0, grad1, image0, row0, row1, scalars),
        (vec_shape, vec_shape, vec_shape, small, (1, LO)),
        row_scratch,
    )
    count = lax.axis_size("tm") * lax.axis_size("star")
    everyone = lax.all_to_all(
        jnp.broadcast_to(partial[None], (count, 1, LO)), ("tm", "star"), 0, 0
    ).reshape(count, LO)
    stars, attitude, cals = call(
        last_kernel,
        (window,),
        (everyone, grad2, x, direction, scalars),
        ((5, 4096), (3, 1024), (N_C, LO)),
    )
    return stars, attitude, cals.reshape(-1)


def solution(mesh):
    by_row = P(("tm", "star"))
    return jax.shard_map(
        shards,
        mesh=mesh,
        in_specs=(P(None, ("tm", "star")), P(None, ("tm", "star"))) + (by_row,) * 5 + (P("tm", "star"),),
        out_specs=(P(None, "star"), P(None, "tm"), P()),
        check_vma=False,
    )
```

time: 2310 us -> 141 us (0.06)
  blocking collectives: 1130 us -> 24.4 us
  other arithmetic: 785 us -> 0.19 us
  local copies, waits for them, and re-layouts: 212 us -> 3.97 us
  waiting for transfers between devices: 126 us -> 39.1 us
  starting transfers between devices: 13.1 us -> 64.8 us
  between operations: 27.6 us -> 1.45 us
    psum x13 -> x0, blocking collectives: 1130 us -> none  [the longest x3 359 us: shards(): knot_sum = lax.psum(jnp.stack(knot_parts), 'star')]
    scatter-add x54 -> x0, other arithmetic: 737 us -> none  [the longest x36 532 us: shards(): jax.ops.segment_sum(att_coef[3 * j + a] * masked, knot_index + j, num_seg...]
    gather x18 -> x0, local copies, waits for them, and re-layouts: 188 us -> none  [the longest x12 106 us: shards(): taken = jnp.take(extended, knot_index + forward_j, axis=1)]
    psum x3 -> x0, waiting for transfers between devices: 126 us -> none  [shards(): star_sum = lax.psum(star_part, 'tm')]
    ppermute x6 -> x30, starting transfers between devices: 13 us -> 64.8 us  [swap(): return lax.ppermute(value, axis, [(i, i ^ bits) for i in range(count)])]
    ppermute x6 -> x30, waiting for transfers between devices: 0.02 us -> 39.1 us  [swap(): return lax.ppermute(value, axis, [(i, i ^ bits) for i in range(count)])]
    reduce_sum x26 -> x0, other arithmetic: 32.3 us -> none  [the longest x10 13.2 us: shards(): jnp.sum(att_coef[3 * forward_j:3 * forward_j + 3] * taken, axis=0)]
    all_to_all x0 -> x1, blocking collectives: none -> 24.4 us  [shards(): lax.all_to_all(jnp.broadcast_to(partial[None], (count, 1, LO)), ('tm', 's...]
  transfers between devices with their start and end apart: 9 -> 30, of which waited for: 2 -> 26; matrix products, arithmetic and copies ran while one was open for 12% -> 0% of each run, Pallas kernels for 0% -> 0%
where the time goes in v1:
time: 141 us
  starting transfers between devices  64.8 us (46%)
  waiting for transfers between devices  39.1 us (28%)
  blocking collectives  24.4 us (17%)
  Pallas kernels  7.24 us (5%)
  local copies, waits for them, and re-layouts  3.97 us (3%)
  between operations  1.45 us (1%)
    ppermute x30, starting transfers between devices, swap(): return lax.ppermute(value, axis, [(i, i ^ bits) for i in range(count)])  64.8 us
    ppermute x30, waiting for transfers between devices, swap(): return lax.ppermute(value, axis, [(i, i ^ bits) for i in range(count)])  39.1 us
    all_to_all x1, blocking collectives, shards(): lax.all_to_all(jnp.broadcast_to(partial[None], (count, 1, LO)), ('tm', 's...  24.4 us
    pallas_call x5, Pallas kernels, call(): pl.pallas_call(kernel, out_shape=[jax.ShapeDtypeStruct(shape, F32) for sh...  7.24 us
    unnamed x14, local copies, waits for them, and re-layouts  3.86 us
  transfers between devices with their start and end apart: 30, of which 26 were waited for; matrix products, arithmetic and copies ran while one was open for 0% of the time, Pallas kernels for 0%

profile of v1, /device:TPU:1, one launch (start us, length us, event | category | flops | bytes accessed | tf_op | source)
XLA Modules:
  0.0 141.1 jit_solution(9972839885183357210)
XLA Ops:
  1.4 0.9 copy-done
  2.3 0.8 copy-done.1
  3.1 0.7 copy-done.4
  3.8 0.7 copy-done.5
  4.5 0.7 copy-done.6
  5.2 1.0 shard_map.103
  6.2 2.5 %collective-permute-start = (f32[184,128]{1,0:T(8,128)S(1)}, f32[184,128]{1,0:T(8,128)S(1)}, u32[]{:S(2)}, u32[]{:S(2)}) collective-permute-start(f32[184,128]{1,0:T(8,128)S(1)} %get-tuple-element.24), channel_id=1, source_target_pairs={{0,32},{32,0},{64,96},{96,64},{128,160},{160,128},{192,224},{224,1... | collective-permute-start | bytes 282632 | tf_op jit(solution)/shard_map/ppermute | solution.py:295
  8.7 2.0 %collective-permute-done = f32[184,128]{1,0:T(8,128)S(1)} collective-permute-done((f32[184,128]{1,0:T(8,128)S(1)}, f32[184,128]{1,0:T(8,128)S(1)}, u32[]{:S(2)}, u32[]{:S(2)}) %collective-permute-start) | collective-permute-done | bytes 94240 | tf_op jit(solution)/shard_map/ppermute | solution.py:295
  10.7 3.4 %collective-permute-start.1 = (f32[184,128]{1,0:T(8,128)S(1)}, f32[184,128]{1,0:T(8,128)S(1)}, u32[]{:S(2)}, u32[]{:S(2)}) collective-permute-start(f32[184,128]{1,0:T(8,128)S(1)} %add.90), channel_id=1, source_target_pairs={{0,64},{32,96},{64,0},{96,32},{128,192},{160,224},{192,128},{224,1... | collective-permute-start | bytes 282632 | tf_op jit(solution)/shard_map/ppermute | solution.py:295
  14.1 3.0 %collective-permute-done.1 = f32[184,128]{1,0:T(8,128)S(1)} collective-permute-done((f32[184,128]{1,0:T(8,128)S(1)}, f32[184,128]{1,0:T(8,128)S(1)}, u32[]{:S(2)}, u32[]{:S(2)}) %collective-permute-start.1) | collective-permute-done | bytes 94240 | tf_op jit(solution)/shard_map/ppermute | solution.py:295
  17.1 4.1 %collective-permute-start.2 = (f32[184,128]{1,0:T(8,128)S(1)}, f32[184,128]{1,0:T(8,128)S(1)}, u32[]{:S(2)}, u32[]{:S(2)}) collective-permute-start(f32[184,128]{1,0:T(8,128)S(1)} %add.91), channel_id=1, source_target_pairs={{0,192},{32,224},{64,128},{96,160},{128,64},{160,96},{192,0},{224,... | collective-permute-start | bytes 282632 | tf_op jit(solution)/shard_map/ppermute | solution.py:295
  21.1 2.0 %collective-permute-done.2 = f32[184,128]{1,0:T(8,128)S(1)} collective-permute-done((f32[184,128]{1,0:T(8,128)S(1)}, f32[184,128]{1,0:T(8,128)S(1)}, u32[]{:S(2)}, u32[]{:S(2)}) %collective-permute-start.2) | collective-permute-done | bytes 94240 | tf_op jit(solution)/shard_map/ppermute | solution.py:295
  23.2 4.4 %collective-permute-start.3 = (f32[48,128]{1,0:T(8,128)S(1)}, f32[48,128]{1,0:T(8,128)S(1)}, u32[]{:S(2)}, u32[]{:S(2)}) collective-permute-start(f32[48,128]{1,0:T(8,128)S(1)} %pad_maximum_fusion), channel_id=1, source_target_pairs={{0,1},{1,0},{2,3},{3,2},{4,5},{5,4},{6,7},{7,6},{8,9},{9,8},{10,11... | collective-permute-start | bytes 73736 | tf_op jit(solution)/shard_map/ppermute | solution.py:295
  27.6 0.8 collective-permute-done.3
  28.5 2.2 %collective-permute-start.6 = (f32[48,128]{1,0:T(8,128)S(1)}, f32[48,128]{1,0:T(8,128)S(1)}, u32[]{:S(2)}, u32[]{:S(2)}) collective-permute-start(f32[48,128]{1,0:T(8,128)S(1)} %fusion.2), channel_id=1, source_target_pairs={{0,16},{1,17},{2,18},{3,19},{4,20},{5,21},{6,22},{7,23},{8,24},{9,... | collective-permute-start | bytes 73736 | tf_op jit(solution)/shard_map/ppermute | solution.py:295
  30.7 0.9 collective-permute-start.5
  31.6 1.1 collective-permute-done.6
  32.6 2.0 %collective-permute-done.5 = f32[48,128]{1,0:T(8,128)S(1)} collective-permute-done((f32[48,128]{1,0:T(8,128)S(1)}, f32[48,128]{1,0:T(8,128)S(1)}, u32[]{:S(2)}, u32[]{:S(2)}) %collective-permute-start.5) | collective-permute-done | bytes 24608 | tf_op jit(solution)/shard_map/ppermute | solution.py:295
  34.6 3.0 %collective-permute-start.9 = (f32[48,128]{1,0:T(8,128)S(1)}, f32[48,128]{1,0:T(8,128)S(1)}, u32[]{:S(2)}, u32[]{:S(2)}) collective-permute-start(f32[48,128]{1,0:T(8,128)S(1)} %add_add_fusion.5), channel_id=1, source_target_pairs={{0,4},{1,5},{2,6},{3,7},{4,0},{5,1},{6,2},{7,3},{8,12},{9,13},{10,... | collective-permute-start | bytes 73736 | tf_op jit(solution)/shard_map/ppermute | solution.py:295
  37.6 0.8 collective-permute-start.8
  38.4 0.5 collective-permute-done.9
  38.9 2.6 %collective-permute-done.8 = f32[48,128]{1,0:T(8,128)S(1)} collective-permute-done((f32[48,128]{1,0:T(8,128)S(1)}, f32[48,128]{1,0:T(8,128)S(1)}, u32[]{:S(2)}, u32[]{:S(2)}) %collective-permute-start.8) | collective-permute-done | bytes 24608 | tf_op jit(solution)/shard_map/ppermute | solution.py:295
  41.5 2.0 %shard_map.104 = (f32[184,128]{1,0:T(8,128)S(1)}, f32[24,128]{1,0:T(8,128)S(1)}, f32[208,128]{1,0:T(8,128)S(1)}, f32[1,2048]{1,0:T(1,128)S(1)}, f32[8,128]{1,0:T(8,128)S(1)}) custom-call(s32[1,1]{1,0:T(1,128)S(6)} %copy.11.blocks_ref, s32[1]{0:T(128)} %bitcast.window_ref, f32[5,2048]{1,0:T(8,128)S(1)} %copy-done.1, f32[12,2048]{1,0:T(8,128)S(1)} %copy-done, ...), custom_call_target="tpu_custom_call" | custom-call | tf_op jit(solution)/shard_map/pallas_call | solution.py:282
  43.5 2.2 %collective-permute-start.10 = (f32[184,128]{1,0:T(8,128)S(1)}, f32[184,128]{1,0:T(8,128)S(1)}, u32[]{:S(2)}, u32[]{:S(2)}) collective-permute-start(f32[184,128]{1,0:T(8,128)S(1)} %get-tuple-element.26), channel_id=1, source_target_pairs={{0,32},{32,0},{64,96},{96,64},{128,160},{160,128},{192,224},{224,1... | collective-permute-start | bytes 282632 | tf_op jit(solution)/shard_map/ppermute | solution.py:295
  45.7 2.0 %collective-permute-done.10 = f32[184,128]{1,0:T(8,128)S(1)} collective-permute-done((f32[184,128]{1,0:T(8,128)S(1)}, f32[184,128]{1,0:T(8,128)S(1)}, u32[]{:S(2)}, u32[]{:S(2)}) %collective-permute-start.10) | collective-permute-done | bytes 94240 | tf_op jit(solution)/shard_map/ppermute | solution.py:295
  47.7 2.5 %collective-permute-start.11 = (f32[184,128]{1,0:T(8,128)S(1)}, f32[184,128]{1,0:T(8,128)S(1)}, u32[]{:S(2)}, u32[]{:S(2)}) collective-permute-start(f32[184,128]{1,0:T(8,128)S(1)} %add.100), channel_id=1, source_target_pairs={{0,64},{32,96},{64,0},{96,32},{128,192},{160,224},{192,128},{224,1... | collective-permute-start | bytes 282632 | tf_op jit(solution)/shard_map/ppermute | solution.py:295
  50.2 2.0 %collective-permute-done.11 = f32[184,128]{1,0:T(8,128)S(1)} collective-permute-done((f32[184,128]{1,0:T(8,128)S(1)}, f32[184,128]{1,0:T(8,128)S(1)}, u32[]{:S(2)}, u32[]{:S(2)}) %collective-permute-start.11) | collective-permute-done | bytes 94240 | tf_op jit(solution)/shard_map/ppermute | solution.py:295
  52.1 4.0 %collective-permute-start.12 = (f32[184,128]{1,0:T(8,128)S(1)}, f32[184,128]{1,0:T(8,128)S(1)}, u32[]{:S(2)}, u32[]{:S(2)}) collective-permute-start(f32[184,128]{1,0:T(8,128)S(1)} %add.101), channel_id=1, source_target_pairs={{0,192},{32,224},{64,128},{96,160},{128,64},{160,96},{192,0},{224,... | collective-permute-start | bytes 282632 | tf_op jit(solution)/shard_map/ppermute | solution.py:295
  56.1 2.0 %collective-permute-done.12 = f32[184,128]{1,0:T(8,128)S(1)} collective-permute-done((f32[184,128]{1,0:T(8,128)S(1)}, f32[184,128]{1,0:T(8,128)S(1)}, u32[]{:S(2)}, u32[]{:S(2)}) %collective-permute-start.12) | collective-permute-done | bytes 94240 | tf_op jit(solution)/shard_map/ppermute | solution.py:295
  58.2 8.1 %collective-permute-start.13 = (f32[48,128]{1,0:T(8,128)S(1)}, f32[48,128]{1,0:T(8,128)S(1)}, u32[]{:S(2)}, u32[]{:S(2)}) collective-permute-start(f32[48,128]{1,0:T(8,128)S(1)} %pad_maximum_fusion.1), channel_id=1, source_target_pairs={{0,1},{1,0},{2,3},{3,2},{4,5},{5,4},{6,7},{7,6},{8,9},{9,8},{10,11... | collective-permute-start | bytes 73736 | tf_op jit(solution)/shard_map/ppermute | solution.py:295
  66.2 0.8 collective-permute-done.13
  67.1 1.1 collective-permute-start.16
  68.2 0.9 collective-permute-start.15
  69.1 0.6 collective-permute-start.14
  69.7 1.5 %collective-permute-done.16 = f32[48,128]{1,0:T(8,128)S(1)} collective-permute-done((f32[48,128]{1,0:T(8,128)S(1)}, f32[48,128]{1,0:T(8,128)S(1)}, u32[]{:S(2)}, u32[]{:S(2)}) %collective-permute-start.16) | collective-permute-done | bytes 24608 | tf_op jit(solution)/shard_map/ppermute | solution.py:295
  71.3 1.1 collective-permute-done.15
  72.4 0.8 collective-permute-start.19
  73.2 1.3 collective-permute-start.18
  74.4 0.7 collective-permute-start.17
  75.1 1.5 %collective-permute-done.19 = f32[48,128]{1,0:T(8,128)S(1)} collective-permute-done((f32[48,128]{1,0:T(8,128)S(1)}, f32[48,128]{1,0:T(8,128)S(1)}, u32[]{:S(2)}, u32[]{:S(2)}) %collective-permute-start.19) | collective-permute-done | bytes 24608 | tf_op jit(solution)/shard_map/ppermute | solution.py:295
  76.7 0.4 collective-permute-done.18
  77.0 0.1 collective-permute-done.17
  77.1 2.0 %shard_map.105 = (f32[184,128]{1,0:T(8,128)S(1)}, f32[24,128]{1,0:T(8,128)S(1)}, f32[208,128]{1,0:T(8,128)S(1)}, f32[208,128]{1,0:T(8,128)S(1)}, f32[1,2048]{1,0:T(1,128)S(1)}, /*index=5*/f32[8,128]{1,0:T(8,128)S(1)}) custom-call(s32[1,1]{1,0:T(1,128)S(6)} %copy.11.blocks_ref, s32[1]{0:T(128)} %bitcast.window_ref, f32[5,2048]{1,0:T(8,128)S(1)} %copy-done.1, ...), custom_call_target="tpu_custom_call" | custom-call | tf_op jit(solution)/shard_map/pallas_call | solution.py:282
  79.1 1.4 collective-permute-start.20
  80.5 2.1 %collective-permute-done.20 = f32[184,128]{1,0:T(8,128)S(1)} collective-permute-done((f32[184,128]{1,0:T(8,128)S(1)}, f32[184,128]{1,0:T(8,128)S(1)}, u32[]{:S(2)}, u32[]{:S(2)}) %collective-permute-start.20) | collective-permute-done | bytes 94240 | tf_op jit(solution)/shard_map/ppermute | solution.py:295
  82.6 2.2 %collective-permute-start.21 = (f32[184,128]{1,0:T(8,128)S(1)}, f32[184,128]{1,0:T(8,128)S(1)}, u32[]{:S(2)}, u32[]{:S(2)}) collective-permute-start(f32[184,128]{1,0:T(8,128)S(1)} %add.110), channel_id=1, source_target_pairs={{0,64},{32,96},{64,0},{96,32},{128,192},{160,224},{192,128},{224,1... | collective-permute-start | bytes 282632 | tf_op jit(solution)/shard_map/ppermute | solution.py:295
  84.9 2.3 %collective-permute-done.21 = f32[184,128]{1,0:T(8,128)S(1)} collective-permute-done((f32[184,128]{1,0:T(8,128)S(1)}, f32[184,128]{1,0:T(8,128)S(1)}, u32[]{:S(2)}, u32[]{:S(2)}) %collective-permute-start.21) | collective-permute-done | bytes 94240 | tf_op jit(solution)/shard_map/ppermute | solution.py:295
  87.2 3.0 %collective-permute-start.22 = (f32[184,128]{1,0:T(8,128)S(1)}, f32[184,128]{1,0:T(8,128)S(1)}, u32[]{:S(2)}, u32[]{:S(2)}) collective-permute-start(f32[184,128]{1,0:T(8,128)S(1)} %add.111), channel_id=1, source_target_pairs={{0,192},{32,224},{64,128},{96,160},{128,64},{160,96},{192,0},{224,... | collective-permute-start | bytes 282632 | tf_op jit(solution)/shard_map/ppermute | solution.py:295
  90.2 2.6 %collective-permute-done.22 = f32[184,128]{1,0:T(8,128)S(1)} collective-permute-done((f32[184,128]{1,0:T(8,128)S(1)}, f32[184,128]{1,0:T(8,128)S(1)}, u32[]{:S(2)}, u32[]{:S(2)}) %collective-permute-start.22) | collective-permute-done | bytes 94240 | tf_op jit(solution)/shard_map/ppermute | solution.py:295
  92.8 8.4 %collective-permute-start.23 = (f32[48,128]{1,0:T(8,128)S(1)}, f32[48,128]{1,0:T(8,128)S(1)}, u32[]{:S(2)}, u32[]{:S(2)}) collective-permute-start(f32[48,128]{1,0:T(8,128)S(1)} %pad_maximum_fusion.2), channel_id=1, source_target_pairs={{0,1},{1,0},{2,3},{3,2},{4,5},{5,4},{6,7},{7,6},{8,9},{9,8},{10,11... | collective-permute-start | bytes 73736 | tf_op jit(solution)/shard_map/ppermute | solution.py:295
  101.2 0.8 collective-permute-done.23
  102.1 2.4 %collective-permute-start.26 = (f32[48,128]{1,0:T(8,128)S(1)}, f32[48,128]{1,0:T(8,128)S(1)}, u32[]{:S(2)}, u32[]{:S(2)}) collective-permute-start(f32[48,128]{1,0:T(8,128)S(1)} %fusion), channel_id=1, source_target_pairs={{0,16},{1,17},{2,18},{3,19},{4,20},{5,21},{6,22},{7,23},{8,24},{9,... | collective-permute-start | bytes 73736 | tf_op jit(solution)/shard_map/ppermute | solution.py:295
  104.5 1.0 collective-permute-start.25
  105.4 0.8 collective-permute-done.26
  106.3 2.1 %collective-permute-done.25 = f32[48,128]{1,0:T(8,128)S(1)} collective-permute-done((f32[48,128]{1,0:T(8,128)S(1)}, f32[48,128]{1,0:T(8,128)S(1)}, u32[]{:S(2)}, u32[]{:S(2)}) %collective-permute-start.25) | collective-permute-done | bytes 24608 | tf_op jit(solution)/shard_map/ppermute | solution.py:295
  108.4 1.7 %collective-permute-start.29 = (f32[48,128]{1,0:T(8,128)S(1)}, f32[48,128]{1,0:T(8,128)S(1)}, u32[]{:S(2)}, u32[]{:S(2)}) collective-permute-start(f32[48,128]{1,0:T(8,128)S(1)} %add_add_fusion.1), channel_id=1, source_target_pairs={{0,4},{1,5},{2,6},{3,7},{4,0},{5,1},{6,2},{7,3},{8,12},{9,13},{10,... | collective-permute-start | bytes 73736 | tf_op jit(solution)/shard_map/ppermute | solution.py:295
  110.0 1.4 collective-permute-start.28
  111.4 1.2 collective-permute-done.29
  112.6 1.3 collective-permute-done.28
  113.9 0.5 collective-permute-done.27
  114.4 1.2 shard_map.106
  115.6 0.1 broadcast_in_dim.9
  115.7 24.4 %all_to_all.5 = f32[256,1,128]{2,1,0:T(1,128)S(1)} all-to-all(f32[256,1,128]{2,1,0:T(1,128)S(1)} %broadcast_in_dim.9), channel_id=1, replica_groups=mesh['tm'=8,'star'=32] {'tm','star'}, dimensions={0} | all-to-all | bytes 262144 | tf_op jit(solution)/shard_map/all_to_all | solution.py:346
  140.1 1.0 shard_map.107
  (44 shorter events, 0.3 us)
Async XLA Ops:
  0.6 0.7 copy-start.3
  0.6 0.7 copy-start.2
  1.4 0.9 copy-start
  2.3 0.8 copy-start.1
  3.1 0.7 copy-start.4
  3.8 0.7 copy-start.5
  4.5 0.7 copy-start.6
  6.2 4.5 %collective-permute-start = (f32[184,128]{1,0:T(8,128)S(1)}, f32[184,128]{1,0:T(8,128)S(1)}, u32[]{:S(2)}, u32[]{:S(2)}) collective-permute-start(f32[184,128]{1,0:T(8,128)S(1)} %get-tuple-element.24), channel_id=1, source_target_pairs={{0,32},{32,0},{64,96},{96,64},{128,160},{160,128},{192,224},{224,1... | collective-permute-start | bytes 282632 | tf_op jit(solution)/shard_map/ppermute | solution.py:295
  10.7 6.4 %collective-permute-start.1 = (f32[184,128]{1,0:T(8,128)S(1)}, f32[184,128]{1,0:T(8,128)S(1)}, u32[]{:S(2)}, u32[]{:S(2)}) collective-permute-start(f32[184,128]{1,0:T(8,128)S(1)} %add.90), channel_id=1, source_target_pairs={{0,64},{32,96},{64,0},{96,32},{128,192},{160,224},{192,128},{224,1... | collective-permute-start | bytes 282632 | tf_op jit(solution)/shard_map/ppermute | solution.py:295
  17.1 6.1 %collective-permute-start.2 = (f32[184,128]{1,0:T(8,128)S(1)}, f32[184,128]{1,0:T(8,128)S(1)}, u32[]{:S(2)}, u32[]{:S(2)}) collective-permute-start(f32[184,128]{1,0:T(8,128)S(1)} %add.91), channel_id=1, source_target_pairs={{0,192},{32,224},{64,128},{96,160},{128,64},{160,96},{192,0},{224,... | collective-permute-start | bytes 282632 | tf_op jit(solution)/shard_map/ppermute | solution.py:295
  23.2 5.3 %collective-permute-start.3 = (f32[48,128]{1,0:T(8,128)S(1)}, f32[48,128]{1,0:T(8,128)S(1)}, u32[]{:S(2)}, u32[]{:S(2)}) collective-permute-start(f32[48,128]{1,0:T(8,128)S(1)} %pad_maximum_fusion), channel_id=1, source_target_pairs={{0,1},{1,0},{2,3},{3,2},{4,5},{5,4},{6,7},{7,6},{8,9},{9,8},{10,11... | collective-permute-start | bytes 73736 | tf_op jit(solution)/shard_map/ppermute | solution.py:295
  28.5 4.2 %collective-permute-start.6 = (f32[48,128]{1,0:T(8,128)S(1)}, f32[48,128]{1,0:T(8,128)S(1)}, u32[]{:S(2)}, u32[]{:S(2)}) collective-permute-start(f32[48,128]{1,0:T(8,128)S(1)} %fusion.2), channel_id=1, source_target_pairs={{0,16},{1,17},{2,18},{3,19},{4,20},{5,21},{6,22},{7,23},{8,24},{9,... | collective-permute-start | bytes 73736 | tf_op jit(solution)/shard_map/ppermute | solution.py:295
  30.7 3.9 %collective-permute-start.5 = (f32[48,128]{1,0:T(8,128)S(1)}, f32[48,128]{1,0:T(8,128)S(1)}, u32[]{:S(2)}, u32[]{:S(2)}) collective-permute-start(f32[48,128]{1,0:T(8,128)S(1)} %fusion.2), channel_id=1, source_target_pairs={{0,24},{1,25},{2,26},{3,27},{4,28},{5,29},{6,30},{7,31},{8,16},{9,... | collective-permute-start | bytes 73736 | tf_op jit(solution)/shard_map/ppermute | solution.py:295
  31.6 3.0 %collective-permute-start.4 = (f32[48,128]{1,0:T(8,128)S(1)}, f32[48,128]{1,0:T(8,128)S(1)}, u32[]{:S(2)}, u32[]{:S(2)}) collective-permute-start(f32[48,128]{1,0:T(8,128)S(1)} %fusion.2), channel_id=1, source_target_pairs={{0,8},{1,9},{2,10},{3,11},{4,12},{5,13},{6,14},{7,15},{8,0},{9,1},... | collective-permute-start | bytes 73736 | tf_op jit(solution)/shard_map/ppermute | solution.py:295
  34.6 4.3 %collective-permute-start.9 = (f32[48,128]{1,0:T(8,128)S(1)}, f32[48,128]{1,0:T(8,128)S(1)}, u32[]{:S(2)}, u32[]{:S(2)}) collective-permute-start(f32[48,128]{1,0:T(8,128)S(1)} %add_add_fusion.5), channel_id=1, source_target_pairs={{0,4},{1,5},{2,6},{3,7},{4,0},{5,1},{6,2},{7,3},{8,12},{9,13},{10,... | collective-permute-start | bytes 73736 | tf_op jit(solution)/shard_map/ppermute | solution.py:295
  37.6 3.9 %collective-permute-start.8 = (f32[48,128]{1,0:T(8,128)S(1)}, f32[48,128]{1,0:T(8,128)S(1)}, u32[]{:S(2)}, u32[]{:S(2)}) collective-permute-start(f32[48,128]{1,0:T(8,128)S(1)} %add_add_fusion.5), channel_id=1, source_target_pairs={{0,6},{1,7},{2,4},{3,5},{4,2},{5,3},{6,0},{7,1},{8,14},{9,15},{10,... | collective-permute-start | bytes 73736 | tf_op jit(solution)/shard_map/ppermute | solution.py:295
  38.4 3.1 %collective-permute-start.7 = (f32[48,128]{1,0:T(8,128)S(1)}, f32[48,128]{1,0:T(8,128)S(1)}, u32[]{:S(2)}, u32[]{:S(2)}) collective-permute-start(f32[48,128]{1,0:T(8,128)S(1)} %add_add_fusion.5), channel_id=1, source_target_pairs={{0,2},{1,3},{2,0},{3,1},{4,6},{5,7},{6,4},{7,5},{8,10},{9,11},{10,... | collective-permute-start | bytes 73736 | tf_op jit(solution)/shard_map/ppermute | solution.py:295
  43.5 4.2 %collective-permute-start.10 = (f32[184,128]{1,0:T(8,128)S(1)}, f32[184,128]{1,0:T(8,128)S(1)}, u32[]{:S(2)}, u32[]{:S(2)}) collective-permute-start(f32[184,128]{1,0:T(8,128)S(1)} %get-tuple-element.26), channel_id=1, source_target_pairs={{0,32},{32,0},{64,96},{96,64},{128,160},{160,128},{192,224},{224,1... | collective-permute-start | bytes 282632 | tf_op jit(solution)/shard_map/ppermute | solution.py:295
  47.7 4.4 %collective-permute-start.11 = (f32[184,128]{1,0:T(8,128)S(1)}, f32[184,128]{1,0:T(8,128)S(1)}, u32[]{:S(2)}, u32[]{:S(2)}) collective-permute-start(f32[184,128]{1,0:T(8,128)S(1)} %add.100), channel_id=1, source_target_pairs={{0,64},{32,96},{64,0},{96,32},{128,192},{160,224},{192,128},{224,1... | collective-permute-start | bytes 282632 | tf_op jit(solution)/shard_map/ppermute | solution.py:295
  52.1 6.0 %collective-permute-start.12 = (f32[184,128]{1,0:T(8,128)S(1)}, f32[184,128]{1,0:T(8,128)S(1)}, u32[]{:S(2)}, u32[]{:S(2)}) collective-permute-start(f32[184,128]{1,0:T(8,128)S(1)} %add.101), channel_id=1, source_target_pairs={{0,192},{32,224},{64,128},{96,160},{128,64},{160,96},{192,0},{224,... | collective-permute-start | bytes 282632 | tf_op jit(solution)/shard_map/ppermute | solution.py:295
  58.2 8.9 %collective-permute-start.13 = (f32[48,128]{1,0:T(8,128)S(1)}, f32[48,128]{1,0:T(8,128)S(1)}, u32[]{:S(2)}, u32[]{:S(2)}) collective-permute-start(f32[48,128]{1,0:T(8,128)S(1)} %pad_maximum_fusion.1), channel_id=1, source_target_pairs={{0,1},{1,0},{2,3},{3,2},{4,5},{5,4},{6,7},{7,6},{8,9},{9,8},{10,11... | collective-permute-start | bytes 73736 | tf_op jit(solution)/shard_map/ppermute | solution.py:295
  67.1 4.2 %collective-permute-start.16 = (f32[48,128]{1,0:T(8,128)S(1)}, f32[48,128]{1,0:T(8,128)S(1)}, u32[]{:S(2)}, u32[]{:S(2)}) collective-permute-start(f32[48,128]{1,0:T(8,128)S(1)} %fusion.1), channel_id=1, source_target_pairs={{0,16},{1,17},{2,18},{3,19},{4,20},{5,21},{6,22},{7,23},{8,24},{9,... | collective-permute-start | bytes 73736 | tf_op jit(solution)/shard_map/ppermute | solution.py:295
  68.2 4.2 %collective-permute-start.15 = (f32[48,128]{1,0:T(8,128)S(1)}, f32[48,128]{1,0:T(8,128)S(1)}, u32[]{:S(2)}, u32[]{:S(2)}) collective-permute-start(f32[48,128]{1,0:T(8,128)S(1)} %fusion.1), channel_id=1, source_target_pairs={{0,24},{1,25},{2,26},{3,27},{4,28},{5,29},{6,30},{7,31},{8,16},{9,... | collective-permute-start | bytes 73736 | tf_op jit(solution)/shard_map/ppermute | solution.py:295
  69.1 3.3 %collective-permute-start.14 = (f32[48,128]{1,0:T(8,128)S(1)}, f32[48,128]{1,0:T(8,128)S(1)}, u32[]{:S(2)}, u32[]{:S(2)}) collective-permute-start(f32[48,128]{1,0:T(8,128)S(1)} %fusion.1), channel_id=1, source_target_pairs={{0,8},{1,9},{2,10},{3,11},{4,12},{5,13},{6,14},{7,15},{8,0},{9,1},... | collective-permute-start | bytes 73736 | tf_op jit(solution)/shard_map/ppermute | solution.py:295
  72.4 4.3 %collective-permute-start.19 = (f32[48,128]{1,0:T(8,128)S(1)}, f32[48,128]{1,0:T(8,128)S(1)}, u32[]{:S(2)}, u32[]{:S(2)}) collective-permute-start(f32[48,128]{1,0:T(8,128)S(1)} %add_add_fusion.3), channel_id=1, source_target_pairs={{0,4},{1,5},{2,6},{3,7},{4,0},{5,1},{6,2},{7,3},{8,12},{9,13},{10,... | collective-permute-start | bytes 73736 | tf_op jit(solution)/shard_map/ppermute | solution.py:295
  73.2 3.9 %collective-permute-start.18 = (f32[48,128]{1,0:T(8,128)S(1)}, f32[48,128]{1,0:T(8,128)S(1)}, u32[]{:S(2)}, u32[]{:S(2)}) collective-permute-start(f32[48,128]{1,0:T(8,128)S(1)} %add_add_fusion.3), channel_id=1, source_target_pairs={{0,6},{1,7},{2,4},{3,5},{4,2},{5,3},{6,0},{7,1},{8,14},{9,15},{10,... | collective-permute-start | bytes 73736 | tf_op jit(solution)/shard_map/ppermute | solution.py:295
  74.4 2.7 %collective-permute-start.17 = (f32[48,128]{1,0:T(8,128)S(1)}, f32[48,128]{1,0:T(8,128)S(1)}, u32[]{:S(2)}, u32[]{:S(2)}) collective-permute-start(f32[48,128]{1,0:T(8,128)S(1)} %add_add_fusion.3), channel_id=1, source_target_pairs={{0,2},{1,3},{2,0},{3,1},{4,6},{5,7},{6,4},{7,5},{8,10},{9,11},{10,... | collective-permute-start | bytes 73736 | tf_op jit(solution)/shard_map/ppermute | solution.py:295
  79.1 3.5 %collective-permute-start.20 = (f32[184,128]{1,0:T(8,128)S(1)}, f32[184,128]{1,0:T(8,128)S(1)}, u32[]{:S(2)}, u32[]{:S(2)}) collective-permute-start(f32[184,128]{1,0:T(8,128)S(1)} %get-tuple-element.31), channel_id=1, source_target_pairs={{0,32},{32,0},{64,96},{96,64},{128,160},{160,128},{192,224},{224,1... | collective-permute-start | bytes 282632 | tf_op jit(solution)/shard_map/ppermute | solution.py:295
  82.6 4.5 %collective-permute-start.21 = (f32[184,128]{1,0:T(8,128)S(1)}, f32[184,128]{1,0:T(8,128)S(1)}, u32[]{:S(2)}, u32[]{:S(2)}) collective-permute-start(f32[184,128]{1,0:T(8,128)S(1)} %add.110), channel_id=1, source_target_pairs={{0,64},{32,96},{64,0},{96,32},{128,192},{160,224},{192,128},{224,1... | collective-permute-start | bytes 282632 | tf_op jit(solution)/shard_map/ppermute | solution.py:295
  87.2 5.6 %collective-permute-start.22 = (f32[184,128]{1,0:T(8,128)S(1)}, f32[184,128]{1,0:T(8,128)S(1)}, u32[]{:S(2)}, u32[]{:S(2)}) collective-permute-start(f32[184,128]{1,0:T(8,128)S(1)} %add.111), channel_id=1, source_target_pairs={{0,192},{32,224},{64,128},{96,160},{128,64},{160,96},{192,0},{224,... | collective-permute-start | bytes 282632 | tf_op jit(solution)/shard_map/ppermute | solution.py:295
  92.8 9.3 %collective-permute-start.23 = (f32[48,128]{1,0:T(8,128)S(1)}, f32[48,128]{1,0:T(8,128)S(1)}, u32[]{:S(2)}, u32[]{:S(2)}) collective-permute-start(f32[48,128]{1,0:T(8,128)S(1)} %pad_maximum_fusion.2), channel_id=1, source_target_pairs={{0,1},{1,0},{2,3},{3,2},{4,5},{5,4},{6,7},{7,6},{8,9},{9,8},{10,11... | collective-permute-start | bytes 73736 | tf_op jit(solution)/shard_map/ppermute | solution.py:295
  102.1 4.2 %collective-permute-start.26 = (f32[48,128]{1,0:T(8,128)S(1)}, f32[48,128]{1,0:T(8,128)S(1)}, u32[]{:S(2)}, u32[]{:S(2)}) collective-permute-start(f32[48,128]{1,0:T(8,128)S(1)} %fusion), channel_id=1, source_target_pairs={{0,16},{1,17},{2,18},{3,19},{4,20},{5,21},{6,22},{7,23},{8,24},{9,... | collective-permute-start | bytes 73736 | tf_op jit(solution)/shard_map/ppermute | solution.py:295
  104.5 3.9 %collective-permute-start.25 = (f32[48,128]{1,0:T(8,128)S(1)}, f32[48,128]{1,0:T(8,128)S(1)}, u32[]{:S(2)}, u32[]{:S(2)}) collective-permute-start(f32[48,128]{1,0:T(8,128)S(1)} %fusion), channel_id=1, source_target_pairs={{0,24},{1,25},{2,26},{3,27},{4,28},{5,29},{6,30},{7,31},{8,16},{9,... | collective-permute-start | bytes 73736 | tf_op jit(solution)/shard_map/ppermute | solution.py:295
  105.4 2.9 %collective-permute-start.24 = (f32[48,128]{1,0:T(8,128)S(1)}, f32[48,128]{1,0:T(8,128)S(1)}, u32[]{:S(2)}, u32[]{:S(2)}) collective-permute-start(f32[48,128]{1,0:T(8,128)S(1)} %fusion), channel_id=1, source_target_pairs={{0,8},{1,9},{2,10},{3,11},{4,12},{5,13},{6,14},{7,15},{8,0},{9,1},... | collective-permute-start | bytes 73736 | tf_op jit(solution)/shard_map/ppermute | solution.py:295
  108.4 4.3 %collective-permute-start.29 = (f32[48,128]{1,0:T(8,128)S(1)}, f32[48,128]{1,0:T(8,128)S(1)}, u32[]{:S(2)}, u32[]{:S(2)}) collective-permute-start(f32[48,128]{1,0:T(8,128)S(1)} %add_add_fusion.1), channel_id=1, source_target_pairs={{0,4},{1,5},{2,6},{3,7},{4,0},{5,1},{6,2},{7,3},{8,12},{9,13},{10,... | collective-permute-start | bytes 73736 | tf_op jit(solution)/shard_map/ppermute | solution.py:295
  110.0 3.9 %collective-permute-start.28 = (f32[48,128]{1,0:T(8,128)S(1)}, f32[48,128]{1,0:T(8,128)S(1)}, u32[]{:S(2)}, u32[]{:S(2)}) collective-permute-start(f32[48,128]{1,0:T(8,128)S(1)} %add_add_fusion.1), channel_id=1, source_target_pairs={{0,6},{1,7},{2,4},{3,5},{4,2},{5,3},{6,0},{7,1},{8,14},{9,15},{10,... | collective-permute-start | bytes 73736 | tf_op jit(solution)/shard_map/ppermute | solution.py:295
  111.4 3.0 %collective-permute-start.27 = (f32[48,128]{1,0:T(8,128)S(1)}, f32[48,128]{1,0:T(8,128)S(1)}, u32[]{:S(2)}, u32[]{:S(2)}) collective-permute-start(f32[48,128]{1,0:T(8,128)S(1)} %add_add_fusion.1), channel_id=1, source_target_pairs={{0,2},{1,3},{2,0},{3,1},{4,6},{5,7},{6,4},{7,5},{8,10},{9,11},{10,... | collective-permute-start | bytes 73736 | tf_op jit(solution)/shard_map/ppermute | solution.py:295

commit v2 on v1

v2 whole, which is shorter than its diff:
```python
import jax
import jax.numpy as jnp
from jax import lax
from jax.experimental import pallas as pl
from jax.experimental.pallas import tpu as pltpu
from jax.sharding import Mesh
from jax.sharding import PartitionSpec as P

ROWS = 2048
LO = 128
MASKS = (0, 2, 4, 6)
REST = (1,)
GROUP = len(MASKS)
BITS = 0
for _mask in MASKS:
    BITS |= _mask
N_S, N_C, N_B, N_K = 160, 16, 8, 24
N_Z = N_S + N_C + N_B
N_ALL = N_Z + N_K * GROUP
STAR, ATT, CAL, INDEX, RIGHT, PACKED = 0, 5, 17, 18, 21, 24
PARTS = ((STAR, 5, 32), (ATT, 12, 8), (CAL, 1, 16))
SCALAR_LANE = 64
TM = ("tm_high", "tm_low")
F32, BF16 = jnp.float32, jnp.bfloat16


def iota(shape, axis):
    return lax.broadcasted_iota(jnp.int32, shape, axis)


def member_of(window):
    return (window >> 1) & (GROUP - 1)


def window_of(window, member):
    return (window & ~BITS) | (member << 1)


def split(value):
    first = value.astype(BF16)
    return first, (value - first.astype(F32)).astype(BF16)


def total(value):
    return jnp.sum(jnp.sum(value, axis=1, keepdims=True), axis=0, keepdims=True)


def one_hot(index, count):
    return jnp.where(iota((count, index.shape[1]), 0) == index, 1.0, 0.0)


def left_shift(knots, following, j):
    if j == 0:
        return knots
    rolled = pltpu.roll(knots, LO - j, 1)
    upper = pltpu.roll(rolled, 7, 0)
    ahead = pltpu.roll(jnp.broadcast_to(following, (8, LO)), LO - j, 1)
    upper = jnp.where(iota((8, LO), 0) == 7, ahead, upper)
    return jnp.where(iota((8, LO), 1) < LO - j, rolled, upper)


def head_rows(bounds, window):
    row = jnp.sum(jnp.where(iota((8, LO), 0) == window, bounds, 0.0), axis=0, keepdims=True)
    lane = iota((1, LO), 1)
    return [
        jnp.where(lane < 3, row if a == 0 else pltpu.roll(row, LO - 8 * a, 1), 0.0) for a in range(3)
    ]


def with_heads(vec_ref, window, member):
    bounds = vec_ref[N_S + N_C : N_Z]
    own, following = head_rows(bounds, window), head_rows(bounds, window + 1)
    knots = []
    for a in range(3):
        part = vec_ref[pl.ds(pl.multiple_of(N_Z + N_K * member + 8 * a, 8), 8)]
        knots.append(part + jnp.where(iota((8, LO), 0) == 0, jnp.broadcast_to(own[a], (8, LO)), 0.0))
    return knots, following


def shifted_knots(vec_ref, window, member):
    knots, following = with_heads(vec_ref, window, member)
    return jnp.concatenate(
        [left_shift(knots[a], following[a], j) for j in range(4) for a in range(3)], axis=0
    )


def hots_of(data_ref, slot, kinds):
    places = iota((LO, ROWS), 0).astype(F32).astype(BF16)
    hots = []
    for kind in kinds:
        index = data_ref[slot, INDEX + kind : INDEX + kind + 1].astype(jnp.int32)
        low = (index & (LO - 1)).astype(F32).astype(BF16)
        low = jnp.where(places == low, jnp.ones((), BF16), jnp.zeros((), BF16))
        hots.append((PARTS[kind], low, one_hot(index >> 7, PARTS[kind][2])))
    return hots


def forward(data_ref, slot, hots, tables):
    result = None
    for ((base, coefs, count), low, high), table in zip(hots, tables):
        taken = jnp.dot(table, jnp.concatenate([low, low], axis=0), preferred_element_type=F32)
        mixed = None
        for p in range(coefs):
            term = data_ref[slot, base + p : base + p + 1] * taken[p * count : (p + 1) * count]
            mixed = term if mixed is None else mixed + term
        mixed = mixed * high
        for part in range(0, count, 8):
            piece = mixed[part : part + 8]
            result = piece if result is None else result + piece
    return jnp.sum(result, axis=0, keepdims=True)


def adjoint(data_ref, slot, hots, row):
    sums = []
    for (base, coefs, count), low, high in hots:
        pieces = split(data_ref[slot, base : base + coefs] * row)
        left = jnp.concatenate(
            [
                (high * piece[p : p + 1].astype(F32)).astype(BF16)
                for piece in pieces
                for p in range(coefs)
            ],
            axis=0,
        )
        sums.append(lax.dot_general(left, low, (((1,), (1,)), ((), ())), preferred_element_type=F32))
    return sums


def fold(sums):
    return sums[: sums.shape[0] // 2] + sums[sums.shape[0] // 2 :]


def knot_sums(spread, window):
    rows, lanes = iota((8, LO), 0), iota((8, LO), 1)
    knots, heads, tails = [], 0.0, 0.0
    for a in range(3):
        own, over = spread[8 * a : 8 * a + 8], jnp.zeros((8, LO), F32)
        for j in range(1, 4):
            rolled = pltpu.roll(spread[24 * j + 8 * a : 24 * j + 8 * a + 8], j, 1)
            wrapped = pltpu.roll(rolled, 1, 0)
            own = own + jnp.where(lanes >= j, rolled, jnp.where(rows > 0, wrapped, 0.0))
            over = over + jnp.where(lanes < j, wrapped, 0.0)
        is_head = jnp.logical_and(rows == 0, lanes < 3)
        knots.append(jnp.where(is_head, 0.0, own))
        head, tail = jnp.where(is_head, own, 0.0), jnp.where(rows == 0, over, 0.0)
        if a > 0:
            head, tail = pltpu.roll(head, 8 * a, 1), pltpu.roll(tail, 8 * a, 1)
        heads, tails = heads + head, tails + tail
    head = jnp.broadcast_to(heads[:1], (8, LO))
    tail = jnp.broadcast_to(tails[:1], (8, LO))
    bounds = jnp.where(rows == window, head, 0.0) + jnp.where(rows == window + 1, tail, 0.0)
    return jnp.concatenate(knots, axis=0), bounds


def set_scalars(ref, base, scalars):
    rows, lanes = iota((8, LO), 0), iota((8, LO), 1)
    block = ref[base:]
    for i, scalar in enumerate(scalars):
        here = jnp.logical_and(rows == i, lanes == SCALAR_LANE)
        block = jnp.where(here, jnp.broadcast_to(scalar, (8, LO)), block)
    ref[base:] = block


def get_scalars(rest_ref):
    bounds = rest_ref[N_C : N_C + N_B]
    rows, lanes = iota((8, LO), 0), iota((8, LO), 1)
    return [
        total(jnp.where(jnp.logical_and(rows == i, lanes == SCALAR_LANE), bounds, 0.0)) for i in range(3)
    ]


def read_sums(stars_ref, rest_ref):
    bounds = jnp.where(iota((8, LO), 1) < SCALAR_LANE, rest_ref[N_C : N_C + N_B], 0.0)
    return jnp.concatenate([stars_ref[...], rest_ref[:N_C], bounds, rest_ref[N_C + N_B :]], axis=0)


def square(vec):
    part = vec * vec
    return (
        total(part[:N_S]) * (GROUP / 8)
        + total(part[N_S:N_Z]) * (GROUP / 256)
        + total(part[N_Z:]) * (1 / 32)
    )


def keep(scalars, ref):
    rows = iota((8, LO), 0)
    block = jnp.zeros((8, LO), F32)
    for i, scalar in enumerate(scalars):
        block = jnp.where(rows == i, jnp.broadcast_to(scalar, (8, LO)), block)
    ref[...] = block


def kept(ref):
    return [ref[i : i + 1, 0:1] for i in range(8)]


def start_kernel(blocks_ref, *args):
    sources, data_ref, scratch = args[:7], args[7], args[8:]
    held, semaphore = scratch[:7], scratch[7]
    copies = [
        pltpu.make_async_copy(source, target, semaphore.at[i])
        for i, (source, target) in enumerate(zip(sources, held))
    ]
    for copy in copies:
        copy.start()
    for copy in copies:
        copy.wait()
    live = jnp.where(iota((1, ROWS), 1) < 128 * blocks_ref[0, 0], 1.0, 0.0)
    data_ref[0, STAR : STAR + 5] = held[0][...] * live
    data_ref[0, ATT : ATT + 12] = held[1][...] * live
    data_ref[0, CAL : CAL + 1] = held[2][...] * live
    for which in range(3):
        data_ref[0, INDEX + which : INDEX + which + 1] = held[4 + which][...].astype(F32)
    data_ref[0, RIGHT : RIGHT + 1] = held[3][...] * live
    data_ref[0, RIGHT + 1 :] = jnp.zeros((PACKED - RIGHT - 1, ROWS), F32)


def gather_kernel(window_ref, data_ref, *args):
    wide_ref, knot_ref, star_ref, cal_ref = args
    window = window_ref[0]
    clear((wide_ref, star_ref, cal_ref))
    norm, size = 0.0, 0.0
    for member in range(GROUP):
        slot = member_of(window) ^ member
        row = data_ref[slot, RIGHT : RIGHT + 1]
        coefs = data_ref[slot, :INDEX]
        norm += total(row * row)
        size += total(jnp.sum(coefs * coefs, axis=0, keepdims=True))
        hots = hots_of(data_ref, slot, (0, 1, 2))
        add_sums(data_ref, slot, hots, row, window, member, args)
    finish_sums(args)
    set_scalars(wide_ref, N_S + N_C, [norm, size])


def clear(refs):
    for ref in refs:
        ref[...] = jnp.zeros(ref.shape, F32)


def add_sums(data_ref, slot, hots, row, window, member, sums):
    wide_ref, knot_ref, star_ref, cal_ref = sums
    stars, spread, cals = adjoint(data_ref, slot, hots, row)
    star_ref[...] += stars
    cal_ref[...] += cals
    knots, bounds = knot_sums(fold(spread), window_of(window, member))
    knot_ref[N_K * member : N_K * member + N_K] = knots
    wide_ref[N_S + N_C :] += bounds


def finish_sums(sums):
    wide_ref, _, star_ref, cal_ref = sums
    wide_ref[:N_S] = fold(star_ref[...])
    wide_ref[N_S : N_S + N_C] = fold(cal_ref[...])


def apply(window, vec_ref, data_ref, scale, row_ref, sums=None):
    vec = vec_ref[:N_Z]
    star_table = jnp.concatenate(split(vec[:N_S]), axis=1)
    cal_table = jnp.concatenate(split(vec[N_S : N_S + N_C]), axis=1)
    if sums is not None:
        clear((sums[0], sums[2], sums[3]))
    for member in range(GROUP):
        slot = member_of(window) ^ member
        knots = shifted_knots(vec_ref, window_of(window, member), member)
        tables = (star_table, jnp.concatenate(split(knots), axis=1), cal_table)
        hots = hots_of(data_ref, slot, (0, 1, 2))
        row = forward(data_ref, slot, hots, tables) * scale
        row_ref[member : member + 1] = row
        if sums is not None:
            add_sums(data_ref, slot, hots, row * scale, window, member, sums)
    if sums is not None:
        finish_sums(sums)


def first_kernel(window_ref, data_ref, stars_ref, rest_ref, *args):
    wide_ref, knot_ref, grad_ref, row_ref, kept_ref, star_ref, cal_ref = args
    window = window_ref[0]
    norm, size, _ = get_scalars(rest_ref)
    inverse, length = lax.rsqrt(size), jnp.sqrt(norm)
    grad = read_sums(stars_ref, rest_ref) * inverse / length
    grad_ref[...] = grad
    keep([inverse, length], kept_ref)
    apply(window, grad_ref, data_ref, inverse, row_ref, (wide_ref, knot_ref, star_ref, cal_ref))
    row = row_ref[...]
    set_scalars(wide_ref, N_S + N_C, [square(grad), total(row * row)])


def second_kernel(window_ref, data_ref, stars_ref, rest_ref, grad_ref, q_ref, old_ref, *args):
    wide_ref, knot_ref, new_ref, image_ref, row_ref, kept_ref, star_ref, cal_ref = args
    inverse, length = kept(old_ref)[:2]
    gamma, delta, _ = get_scalars(rest_ref)
    image = read_sums(stars_ref, rest_ref)
    image_ref[...] = image
    grad = grad_ref[...] - (gamma / delta) * image
    new_ref[...] = grad
    keep([inverse, length, gamma, delta], kept_ref)
    sums = (wide_ref, knot_ref, star_ref, cal_ref)
    apply(window_ref[0], new_ref, data_ref, inverse, row_ref, sums)
    row = row_ref[...]
    set_scalars(wide_ref, N_S + N_C, [square(grad), total(row * row), total(row * q_ref[...])])


def third_kernel(window_ref, data_ref, *args):
    stars_ref, rest_ref, first_ref, grad_ref, image_ref, q_ref, row_ref, old_ref = args[:8]
    new_ref, x_ref, direction_ref, kept_ref, scalar_ref, work_ref = args[8:]
    inverse, length, gamma0, delta0 = kept(old_ref)[:4]
    gamma1, square1, cross1 = get_scalars(rest_ref)
    beta = gamma1 / gamma0
    first, grad = first_ref[...], grad_ref[...]
    direction = grad + beta * first
    q = row_ref[...] + beta * q_ref[...]
    delta1 = square1 + 2.0 * beta * cross1 + beta * beta * delta0
    image = read_sums(stars_ref, rest_ref) + beta * image_ref[...]
    step = gamma1 / delta1
    x_ref[...] = (gamma0 / delta0) * first + step * direction
    direction_ref[...] = direction
    grad = grad - step * image
    new_ref[...] = grad
    keep([inverse, length, gamma1, delta1], kept_ref)
    apply(window_ref[0], new_ref, data_ref, inverse, work_ref)
    row = work_ref[...]
    lane = iota((1, LO), 1)
    scalar_ref[...] = (
        jnp.where(lane == 0, square(grad), 0.0)
        + jnp.where(lane == 1, total(row * row), 0.0)
        + jnp.where(lane == 2, total(row * q), 0.0)
    )


def last_kernel(window_ref, sums_ref, grad_ref, x_ref, direction_ref, old_ref, *args):
    star_ref, att_ref, cal_ref, out_ref = args
    inverse, length, gamma1, delta1 = kept(old_ref)[:4]
    sums = jnp.sum(sums_ref[...], axis=0, keepdims=True)
    gamma2, square2, cross2 = (sums[:, i : i + 1] for i in range(3))
    beta = gamma2 / gamma1
    delta2 = square2 + 2.0 * beta * cross2 + beta * beta * delta1
    direction = grad_ref[...] + beta * direction_ref[...]
    x = (x_ref[...] + (gamma2 / delta2) * direction) * (inverse * length)
    out_ref[...] = x
    for hi in range(32):
        for p in range(5):
            star_ref[p : p + 1, LO * hi : LO * hi + LO] = x[32 * p + hi : 32 * p + hi + 1]
    knots, _ = with_heads(out_ref, window_ref[0], member_of(window_ref[0]))
    for a in range(3):
        for hi in range(8):
            att_ref[a : a + 1, LO * hi : LO * hi + LO] = knots[a][hi : hi + 1]
    cal_ref[...] = x[N_S : N_S + N_C]


def call(kernel, smem, vmem, outs, scratch=(), space=pltpu.VMEM, mebibytes=40):
    return pl.pallas_call(
        kernel,
        out_shape=[jax.ShapeDtypeStruct(shape, F32) for shape in outs],
        in_specs=[pl.BlockSpec(memory_space=pltpu.SMEM)] * len(smem)
        + [pl.BlockSpec(memory_space=space)] * len(vmem),
        out_specs=[pl.BlockSpec(memory_space=pltpu.VMEM)] * len(outs),
        scratch_shapes=list(scratch),
        compiler_params=pltpu.CompilerParams(vmem_limit_bytes=mebibytes * 1024 * 1024),
    )(*smem, *vmem)


def swap(value, axis, bits):
    count = lax.axis_size(axis)
    return lax.ppermute(value, axis, [(i, i ^ bits) for i in range(count)])


def add_swapped(value, axis, bits):
    arrived = [swap(value, axis, one) for one in bits]
    if len(bits) == 1:
        return value + arrived[0]
    return (value + arrived[0]) + (arrived[1] + arrived[2])


def over_star(rest):
    for bits in ((1,), (8, 24, 16), (2, 6, 4)):
        rest = add_swapped(rest, "star", bits)
    return rest


def share(data):
    near, wrap = swap(data, TM, 2), swap(data, TM, 6)
    half = ROWS // 2
    far = [swap(wrap[..., :half], TM, 2), swap(near[..., half:], TM, 6)]
    return jnp.concatenate([data, near, jnp.concatenate(far, axis=2), wrap], axis=0)


def reduce(wide, knots):
    wide = add_swapped(wide, TM, REST)
    return wide[:N_S], over_star(jnp.concatenate([wide[N_S:], knots], axis=0))


def shards(star_coef, att_coef, cal_coef, observed, star_index, knot_index, cal_index, valid_blocks):
    window = lax.axis_index(TM).astype(jnp.int32).reshape(1)
    arrays = (
        star_coef,
        att_coef,
        cal_coef.reshape(1, ROWS),
        observed.reshape(1, ROWS),
        star_index.reshape(1, ROWS),
        knot_index.reshape(1, ROWS),
        cal_index.reshape(1, ROWS),
    )
    wide_shape, vec_shape, small = (N_Z, LO), (N_ALL, LO), (8, LO)
    row_shape = (GROUP, ROWS)
    sums = (wide_shape, (N_K * GROUP, LO))
    scratch = [pltpu.VMEM((2 * N_S, LO), F32), pltpu.VMEM((2 * N_C, LO), F32)]
    (data,) = call(
        start_kernel,
        (valid_blocks,),
        arrays,
        ((1, PACKED, ROWS),),
        [pltpu.VMEM(item.shape, item.dtype) for item in arrays] + [pltpu.SemaphoreType.DMA((7,))],
        pltpu.HBM,
        60,
    )
    data = share(data)
    wide, knots = call(gather_kernel, (window,), (data,), sums, scratch)
    arrived = reduce(wide, knots)
    wide, knots, grad0, row0, scalars = call(
        first_kernel,
        (window,),
        (data,) + arrived,
        sums + (vec_shape, row_shape, small),
        scratch,
    )
    arrived = reduce(wide, knots)
    wide, knots, grad1, image0, row1, scalars = call(
        second_kernel,
        (window,),
        (data,) + arrived + (grad0, row0, scalars),
        sums + (vec_shape, vec_shape, row_shape, small),
        scratch,
    )
    arrived = reduce(wide, knots)
    grad2, x, direction, scalars, partial = call(
        third_kernel,
        (window,),
        (data,) + arrived + (grad0, grad1, image0, row0, row1, scalars),
        (vec_shape, vec_shape, vec_shape, small, (1, LO)),
        [pltpu.VMEM(row_shape, F32)],
    )
    axes = ("tm_low", "star")
    count = lax.axis_size(axes)
    everyone = lax.all_to_all(jnp.broadcast_to(partial[None], (count, 1, LO)), axes, 0, 0)
    stars, attitude, cals = call(
        last_kernel,
        (window,),
        (everyone.reshape(count, LO), grad2, x, direction, scalars),
        ((5, 4096), (3, 1024), (N_C, LO)),
        [pltpu.VMEM(vec_shape, F32)],
    )
    return stars, attitude, cals.reshape(-1)


def solution(mesh):
    split_mesh = Mesh(mesh.devices.reshape(4, 2, 32), TM + ("star",))
    by_row = P(TM + ("star",))
    return jax.shard_map(
        shards,
        mesh=split_mesh,
        in_specs=(P(None, TM + ("star",)),) * 2 + (by_row,) * 5 + (P(TM, "star"),),
        out_specs=(P(None, "star"), P(None, TM), P()),
        check_vma=False,
    )
```

time: 141 us -> 126 us (0.89)
  starting transfers between devices: 64.8 us -> 45.4 us
  Pallas kernels: 7.24 us -> 18.5 us
  blocking collectives: 24.4 us -> 16.8 us
  waiting for transfers between devices: 39.1 us -> 43.1 us
  local copies, waits for them, and re-layouts: 3.97 us -> 0.07 us
    ppermute x30 -> x28, starting transfers between devices: 64.8 us -> 45.4 us  [swap(): return lax.ppermute(value, axis, [(i, i ^ bits) for i in range(count)])]
    pallas_call x5 -> x6, Pallas kernels: 7.24 us -> 18.5 us  [call(): pl.pallas_call(kernel, out_shape=[jax.ShapeDtypeStruct(shape, F32) for sh...]
    all_to_all x1, blocking collectives: 24.4 us -> 16.8 us  [shards(): lax.all_to_all(jnp.broadcast_to(partial[None], (count, 1, LO)), axes, 0, 0)]
    ppermute x30 -> x28, waiting for transfers between devices: 39.1 us -> 43.1 us  [swap(): return lax.ppermute(value, axis, [(i, i ^ bits) for i in range(count)])]
    unnamed x14 -> x2, local copies, waits for them, and re-layouts: 3.86 us -> 0.01 us
  transfers between devices with their start and end apart: 30 -> 28, of which waited for: 26 -> 21; matrix products, arithmetic and copies ran while one was open for 0% -> 0% of each run, Pallas kernels for 0% -> 0%
where the time goes in v2:
time: 126 us
  starting transfers between devices  45.4 us (36%)
  waiting for transfers between devices  43.1 us (34%)
  Pallas kernels  18.5 us (15%)
  blocking collectives  16.8 us (13%)
  between operations  1.44 us (1%)
    ppermute x28, starting transfers between devices, swap(): return lax.ppermute(value, axis, [(i, i ^ bits) for i in range(count)])  45.4 us
    ppermute x28, waiting for transfers between devices, swap(): return lax.ppermute(value, axis, [(i, i ^ bits) for i in range(count)])  43.1 us
    pallas_call x6, Pallas kernels, call(): pl.pallas_call(kernel, out_shape=[jax.ShapeDtypeStruct(shape, F32) for sh...  18.5 us
    all_to_all x1, blocking collectives, shards(): lax.all_to_all(jnp.broadcast_to(partial[None], (count, 1, LO)), axes, 0, 0)  16.8 us
  transfers between devices with their start and end apart: 28, of which 21 were waited for; matrix products, arithmetic and copies ran while one was open for 0% of the time, Pallas kernels for 0%

profile of v2, /device:TPU:1, one launch (start us, length us, event | category | flops | bytes accessed | tf_op | source)
XLA Modules:
  0.0 125.7 jit_solution(8834812253088976053)
XLA Ops:
  1.3 1.7 %shard_map.103 = f32[1,24,2048]{2,1,0:T(8,128)} custom-call(s32[1,1]{1,0:T(1,128)S(6)} %copy.11.blocks_ref, f32[5,2048]{1,0:T(8,128)} %args_0_.4, f32[12,2048]{1,0:T(8,128)} %args_1_.4, f32[1,2048]{1,0:T(1,128)} %bitcast.11, f32[1,2048]{1,0:T(1,128)} %bitcast.12, s32[1,2048]{1,0:T(1,128)} %bitcast.13, s32[1,2048]{1,0:T(1,128)} %bitcast.14, s32[1,2048]{1,0:T(1,128)} %bitcast.15), custom_call_target="tpu_custom_call" | custom-call | tf_op jit(solution)/shard_map/pallas_call | solution.py:352
  3.0 6.9 %collective-permute-start.1 = (f32[1,24,2048]{2,1,0:T(8,128)}, f32[1,24,2048]{2,1,0:T(8,128)S(1)}, u32[]{:S(2)}, u32[]{:S(2)}) collective-permute-start(f32[1,24,2048]{2,1,0:T(8,128)} %shard_map.103), channel_id=1, source_target_pairs={{0,192},{32,224},{64,128},{96,160},{128,64},{160,96},{192,0},{224,... | collective-permute-start | bytes 589832 | tf_op jit(solution)/shard_map/ppermute | solution.py:365
  10.0 1.2 collective-permute-start
  11.1 7.4 %collective-permute-done.1 = f32[1,24,2048]{2,1,0:T(8,128)S(1)} collective-permute-done((f32[1,24,2048]{2,1,0:T(8,128)}, f32[1,24,2048]{2,1,0:T(8,128)S(1)}, u32[]{:S(2)}, u32[]{:S(2)}) %collective-permute-start.1) | collective-permute-done | bytes 196640 | tf_op jit(solution)/shard_map/ppermute | solution.py:365
  18.5 1.8 %collective-permute-start.2 = (f32[1,24,1024]{2,1,0:T(8,128)S(1)}, f32[1,24,1024]{2,1,0:T(8,128)S(1)}, u32[]{:S(2)}, u32[]{:S(2)}) collective-permute-start(f32[1,24,1024]{2,1,0:T(8,128)S(1)} %slice.32), channel_id=1, source_target_pairs={{0,64},{32,96},{64,0},{96,32},{128,192},{160,224},{192,128},{224,1... | collective-permute-start | bytes 294920 | tf_op jit(solution)/shard_map/ppermute | solution.py:365
  20.3 0.0 collective-permute-done
  20.3 2.7 %collective-permute-start.3 = (f32[1,24,1024]{2,1,0:T(8,128)S(1)}, f32[1,24,1024]{2,1,0:T(8,128)S(1)}, u32[]{:S(2)}, u32[]{:S(2)}) collective-permute-start(f32[1,24,1024]{2,1,0:T(8,128)S(1)} %slice.33), channel_id=1, source_target_pairs={{0,192},{32,224},{64,128},{96,160},{128,64},{160,96},{192,0},{224,... | collective-permute-start | bytes 294920 | tf_op jit(solution)/shard_map/ppermute | solution.py:365
  23.1 0.0 collective-permute-done.2
  23.1 4.0 %collective-permute-done.3 = f32[1,24,1024]{2,1,0:T(8,128)S(1)} collective-permute-done((f32[1,24,1024]{2,1,0:T(8,128)S(1)}, f32[1,24,1024]{2,1,0:T(8,128)S(1)}, u32[]{:S(2)}, u32[]{:S(2)}) %collective-permute-start.3) | collective-permute-done | bytes 98336 | tf_op jit(solution)/shard_map/ppermute | solution.py:365
  27.0 0.1 pad_maximum_fusion.data_ref
  27.1 3.0 %shard_map.104 = (f32[184,128]{1,0:T(8,128)S(1)}, f32[96,128]{1,0:T(8,128)S(1)}) custom-call(s32[1]{0:T(128)} %bitcast.window_ref, f32[4,24,2048]{2,1,0:T(8,128)S(1)} %pad_maximum_fusion.data_ref), custom_call_target="tpu_custom_call" | custom-call | tf_op jit(solution)/shard_map/pallas_call | solution.py:352
  30.1 0.2 collective-permute-start.4
  30.3 3.3 %collective-permute-done.4 = f32[184,128]{1,0:T(8,128)S(1)} collective-permute-done((f32[184,128]{1,0:T(8,128)S(1)}, f32[184,128]{1,0:T(8,128)S(1)}, u32[]{:S(2)}, u32[]{:S(2)}) %collective-permute-start.4) | collective-permute-done | bytes 94240 | tf_op jit(solution)/shard_map/ppermute | solution.py:365
  33.6 3.8 %collective-permute-start.5 = (f32[120,128]{1,0:T(8,128)S(1)}, f32[120,128]{1,0:T(8,128)S(1)}, u32[]{:S(2)}, u32[]{:S(2)}) collective-permute-start(f32[120,128]{1,0:T(8,128)S(1)} %pad_maximum_fusion.1), channel_id=1, source_target_pairs={{0,1},{1,0},{2,3},{3,2},{4,5},{5,4},{6,7},{7,6},{8,9},{9,8},{10,11... | collective-permute-start | bytes 184328 | tf_op jit(solution)/shard_map/ppermute | solution.py:365
  37.5 0.9 collective-permute-done.5
  38.4 2.8 %collective-permute-start.8 = (f32[120,128]{1,0:T(8,128)S(1)}, f32[120,128]{1,0:T(8,128)S(1)}, u32[]{:S(2)}, u32[]{:S(2)}) collective-permute-start(f32[120,128]{1,0:T(8,128)S(1)} %fusion.2), channel_id=1, source_target_pairs={{0,16},{1,17},{2,18},{3,19},{4,20},{5,21},{6,22},{7,23},{8,24},{9,... | collective-permute-start | bytes 184328 | tf_op jit(solution)/shard_map/ppermute | solution.py:365
  41.2 0.9 collective-permute-start.7
  42.1 0.0 collective-permute-start.6
  42.1 1.0 collective-permute-done.8
  43.0 2.5 %collective-permute-done.7 = f32[120,128]{1,0:T(8,128)S(1)} collective-permute-done((f32[120,128]{1,0:T(8,128)S(1)}, f32[120,128]{1,0:T(8,128)S(1)}, u32[]{:S(2)}, u32[]{:S(2)}) %collective-permute-start.7) | collective-permute-done | bytes 61472 | tf_op jit(solution)/shard_map/ppermute | solution.py:365
  45.5 0.0 collective-permute-done.6
  45.5 3.0 %collective-permute-start.11 = (f32[120,128]{1,0:T(8,128)S(1)}, f32[120,128]{1,0:T(8,128)S(1)}, u32[]{:S(2)}, u32[]{:S(2)}) collective-permute-start(f32[120,128]{1,0:T(8,128)S(1)} %add_add_fusion.5), channel_id=1, source_target_pairs={{0,4},{1,5},{2,6},{3,7},{4,0},{5,1},{6,2},{7,3},{8,12},{9,13},{10,... | collective-permute-start | bytes 184328 | tf_op jit(solution)/shard_map/ppermute | solution.py:365
  48.5 0.8 collective-permute-start.10
  49.3 0.0 collective-permute-start.9
  49.3 0.9 collective-permute-done.11
  50.2 2.9 %collective-permute-done.10 = f32[120,128]{1,0:T(8,128)S(1)} collective-permute-done((f32[120,128]{1,0:T(8,128)S(1)}, f32[120,128]{1,0:T(8,128)S(1)}, u32[]{:S(2)}, u32[]{:S(2)}) %collective-permute-start.10) | collective-permute-done | bytes 61472 | tf_op jit(solution)/shard_map/ppermute | solution.py:365
  53.1 0.0 collective-permute-done.9
  53.1 5.1 %shard_map.105 = (f32[184,128]{1,0:T(8,128)S(1)}, f32[96,128]{1,0:T(8,128)S(1)}, f32[280,128]{1,0:T(8,128)S(1)}, f32[4,2048]{1,0:T(4,128)S(1)}, f32[8,128]{1,0:T(8,128)S(1)}) custom-call(s32[1]{0:T(128)} %bitcast.window_ref, f32[4,24,2048]{2,1,0:T(8,128)S(1)} %pad_maximum_fusion.data_ref, f32[160,128]{1,0:T(8,128)S(1)} %slice.34.stars_ref, ...), custom_call_target="tpu_custom_call" | custom-call | tf_op jit(solution)/shard_map/pallas_call | solution.py:352
  58.2 1.5 %collective-permute-start.12 = (f32[184,128]{1,0:T(8,128)S(1)}, f32[184,128]{1,0:T(8,128)S(1)}, u32[]{:S(2)}, u32[]{:S(2)}) collective-permute-start(f32[184,128]{1,0:T(8,128)S(1)} %get-tuple-element.26), channel_id=1, source_target_pairs={{0,32},{32,0},{64,96},{96,64},{128,160},{160,128},{192,224},{224,1... | collective-permute-start | bytes 282632 | tf_op jit(solution)/shard_map/ppermute | solution.py:365
  59.7 2.0 %collective-permute-done.12 = f32[184,128]{1,0:T(8,128)S(1)} collective-permute-done((f32[184,128]{1,0:T(8,128)S(1)}, f32[184,128]{1,0:T(8,128)S(1)}, u32[]{:S(2)}, u32[]{:S(2)}) %collective-permute-start.12) | collective-permute-done | bytes 94240 | tf_op jit(solution)/shard_map/ppermute | solution.py:365
  61.8 4.2 %collective-permute-start.13 = (f32[120,128]{1,0:T(8,128)S(1)}, f32[120,128]{1,0:T(8,128)S(1)}, u32[]{:S(2)}, u32[]{:S(2)}) collective-permute-start(f32[120,128]{1,0:T(8,128)S(1)} %pad_maximum_fusion.2), channel_id=1, source_target_pairs={{0,1},{1,0},{2,3},{3,2},{4,5},{5,4},{6,7},{7,6},{8,9},{9,8},{10,11... | collective-permute-start | bytes 184328 | tf_op jit(solution)/shard_map/ppermute | solution.py:365
  66.0 0.9 collective-permute-done.13
  66.9 1.3 %collective-permute-start.16 = (f32[120,128]{1,0:T(8,128)S(1)}, f32[120,128]{1,0:T(8,128)S(1)}, u32[]{:S(2)}, u32[]{:S(2)}) collective-permute-start(f32[120,128]{1,0:T(8,128)S(1)} %fusion.1), channel_id=1, source_target_pairs={{0,16},{1,17},{2,18},{3,19},{4,20},{5,21},{6,22},{7,23},{8,24},{9,... | collective-permute-start | bytes 184328 | tf_op jit(solution)/shard_map/ppermute | solution.py:365
  68.1 1.0 collective-permute-start.15
  69.2 0.4 collective-permute-start.14
  69.6 1.9 %collective-permute-done.16 = f32[120,128]{1,0:T(8,128)S(1)} collective-permute-done((f32[120,128]{1,0:T(8,128)S(1)}, f32[120,128]{1,0:T(8,128)S(1)}, u32[]{:S(2)}, u32[]{:S(2)}) %collective-permute-start.16) | collective-permute-done | bytes 61472 | tf_op jit(solution)/shard_map/ppermute | solution.py:365
  71.5 1.9 %collective-permute-done.15 = f32[120,128]{1,0:T(8,128)S(1)} collective-permute-done((f32[120,128]{1,0:T(8,128)S(1)}, f32[120,128]{1,0:T(8,128)S(1)}, u32[]{:S(2)}, u32[]{:S(2)}) %collective-permute-start.15) | collective-permute-done | bytes 61472 | tf_op jit(solution)/shard_map/ppermute | solution.py:365
  73.5 0.0 collective-permute-done.14
  73.5 1.3 %collective-permute-start.19 = (f32[120,128]{1,0:T(8,128)S(1)}, f32[120,128]{1,0:T(8,128)S(1)}, u32[]{:S(2)}, u32[]{:S(2)}) collective-permute-start(f32[120,128]{1,0:T(8,128)S(1)} %add_add_fusion.3), channel_id=1, source_target_pairs={{0,4},{1,5},{2,6},{3,7},{4,0},{5,1},{6,2},{7,3},{8,12},{9,13},{10,... | collective-permute-start | bytes 184328 | tf_op jit(solution)/shard_map/ppermute | solution.py:365
  74.8 0.7 collective-permute-start.18
  75.5 0.7 collective-permute-start.17
  76.2 1.9 %collective-permute-done.19 = f32[120,128]{1,0:T(8,128)S(1)} collective-permute-done((f32[120,128]{1,0:T(8,128)S(1)}, f32[120,128]{1,0:T(8,128)S(1)}, u32[]{:S(2)}, u32[]{:S(2)}) %collective-permute-start.19) | collective-permute-done | bytes 61472 | tf_op jit(solution)/shard_map/ppermute | solution.py:365
  78.1 1.7 %collective-permute-done.18 = f32[120,128]{1,0:T(8,128)S(1)} collective-permute-done((f32[120,128]{1,0:T(8,128)S(1)}, f32[120,128]{1,0:T(8,128)S(1)}, u32[]{:S(2)}, u32[]{:S(2)}) %collective-permute-start.18) | collective-permute-done | bytes 61472 | tf_op jit(solution)/shard_map/ppermute | solution.py:365
  79.8 0.0 collective-permute-done.17
  79.8 5.2 %shard_map.106 = (f32[184,128]{1,0:T(8,128)S(1)}, f32[96,128]{1,0:T(8,128)S(1)}, f32[280,128]{1,0:T(8,128)S(1)}, f32[280,128]{1,0:T(8,128)S(1)}, f32[4,2048]{1,0:T(4,128)S(1)}, /*index=5*/f32[8,128]{1,0:T(8,128)S(1)}) custom-call(s32[1]{0:T(128)} %bitcast.window_ref, f32[4,24,2048]{2,1,0:T(8,128)S(1)} %pad_maximum_fusion.data_ref, ...), custom_call_target="tpu_custom_call" | custom-call | tf_op jit(solution)/shard_map/pallas_call | solution.py:352
  85.0 1.5 %collective-permute-start.20 = (f32[184,128]{1,0:T(8,128)S(1)}, f32[184,128]{1,0:T(8,128)S(1)}, u32[]{:S(2)}, u32[]{:S(2)}) collective-permute-start(f32[184,128]{1,0:T(8,128)S(1)} %get-tuple-element.31), channel_id=1, source_target_pairs={{0,32},{32,0},{64,96},{96,64},{128,160},{160,128},{192,224},{224,1... | collective-permute-start | bytes 282632 | tf_op jit(solution)/shard_map/ppermute | solution.py:365
  86.5 2.1 %collective-permute-done.20 = f32[184,128]{1,0:T(8,128)S(1)} collective-permute-done((f32[184,128]{1,0:T(8,128)S(1)}, f32[184,128]{1,0:T(8,128)S(1)}, u32[]{:S(2)}, u32[]{:S(2)}) %collective-permute-start.20) | collective-permute-done | bytes 94240 | tf_op jit(solution)/shard_map/ppermute | solution.py:365
  88.6 2.9 %collective-permute-start.21 = (f32[120,128]{1,0:T(8,128)S(1)}, f32[120,128]{1,0:T(8,128)S(1)}, u32[]{:S(2)}, u32[]{:S(2)}) collective-permute-start(f32[120,128]{1,0:T(8,128)S(1)} %pad_maximum_fusion.3), channel_id=1, source_target_pairs={{0,1},{1,0},{2,3},{3,2},{4,5},{5,4},{6,7},{7,6},{8,9},{9,8},{10,11... | collective-permute-start | bytes 184328 | tf_op jit(solution)/shard_map/ppermute | solution.py:365
  91.5 0.9 collective-permute-done.21
  92.4 1.9 %collective-permute-start.24 = (f32[120,128]{1,0:T(8,128)S(1)}, f32[120,128]{1,0:T(8,128)S(1)}, u32[]{:S(2)}, u32[]{:S(2)}) collective-permute-start(f32[120,128]{1,0:T(8,128)S(1)} %fusion), channel_id=1, source_target_pairs={{0,16},{1,17},{2,18},{3,19},{4,20},{5,21},{6,22},{7,23},{8,24},{9,... | collective-permute-start | bytes 184328 | tf_op jit(solution)/shard_map/ppermute | solution.py:365
  94.3 0.9 collective-permute-start.23
  95.2 0.0 collective-permute-start.22
  95.2 1.8 %collective-permute-done.24 = f32[120,128]{1,0:T(8,128)S(1)} collective-permute-done((f32[120,128]{1,0:T(8,128)S(1)}, f32[120,128]{1,0:T(8,128)S(1)}, u32[]{:S(2)}, u32[]{:S(2)}) %collective-permute-start.24) | collective-permute-done | bytes 61472 | tf_op jit(solution)/shard_map/ppermute | solution.py:365
  97.0 1.5 %collective-permute-done.23 = f32[120,128]{1,0:T(8,128)S(1)} collective-permute-done((f32[120,128]{1,0:T(8,128)S(1)}, f32[120,128]{1,0:T(8,128)S(1)}, u32[]{:S(2)}, u32[]{:S(2)}) %collective-permute-start.23) | collective-permute-done | bytes 61472 | tf_op jit(solution)/shard_map/ppermute | solution.py:365
  98.6 0.0 collective-permute-done.22
  98.6 2.0 %collective-permute-start.27 = (f32[120,128]{1,0:T(8,128)S(1)}, f32[120,128]{1,0:T(8,128)S(1)}, u32[]{:S(2)}, u32[]{:S(2)}) collective-permute-start(f32[120,128]{1,0:T(8,128)S(1)} %add_add_fusion.1), channel_id=1, source_target_pairs={{0,4},{1,5},{2,6},{3,7},{4,0},{5,1},{6,2},{7,3},{8,12},{9,13},{10,... | collective-permute-start | bytes 184328 | tf_op jit(solution)/shard_map/ppermute | solution.py:365
  100.6 0.9 collective-permute-start.26
  101.5 0.0 collective-permute-start.25
  101.5 1.7 %collective-permute-done.27 = f32[120,128]{1,0:T(8,128)S(1)} collective-permute-done((f32[120,128]{1,0:T(8,128)S(1)}, f32[120,128]{1,0:T(8,128)S(1)}, u32[]{:S(2)}, u32[]{:S(2)}) %collective-permute-start.27) | collective-permute-done | bytes 61472 | tf_op jit(solution)/shard_map/ppermute | solution.py:365
  103.3 1.9 %collective-permute-done.26 = f32[120,128]{1,0:T(8,128)S(1)} collective-permute-done((f32[120,128]{1,0:T(8,128)S(1)}, f32[120,128]{1,0:T(8,128)S(1)}, u32[]{:S(2)}, u32[]{:S(2)}) %collective-permute-start.26) | collective-permute-done | bytes 61472 | tf_op jit(solution)/shard_map/ppermute | solution.py:365
  105.2 0.1 collective-permute-done.25
  105.3 2.5 %shard_map.107 = (f32[280,128]{1,0:T(8,128)S(1)}, f32[280,128]{1,0:T(8,128)S(1)}, f32[280,128]{1,0:T(8,128)S(1)}, f32[8,128]{1,0:T(8,128)S(1)}, f32[1,128]{1,0:T(1,128)S(1)}) custom-call(s32[1]{0:T(128)} %bitcast.window_ref, f32[4,24,2048]{2,1,0:T(8,128)S(1)} %pad_maximum_fusion.data_ref, f32[160,128]{1,0:T(8,128)S(1)} %slice.38.args_0_, ...), custom_call_target="tpu_custom_call" | custom-call | tf_op jit(solution)/shard_map/pallas_call | solution.py:352
  107.8 16.8 %all_to_all.5 = f32[64,1,128]{2,1,0:T(1,128)S(1)} all-to-all(f32[64,1,128]{2,1,0:T(1,128)S(1)} %broadcast_in_dim.9), channel_id=1, replica_groups=mesh['tm_high'=4,'tm_low'=2,'star'=32] {'tm_low','star'}, dimensions={0} | all-to-all | bytes 65536 | tf_op jit(solution)/shard_map/all_to_all | solution.py:445
  124.7 1.0 shard_map.108
  (26 shorter events, 0.3 us)
Async XLA Ops:
  3.0 24.0 %copy-start = (f32[1,24,2048]{2,1,0:T(8,128)S(1)}, f32[1,24,2048]{2,1,0:T(8,128)}, u32[]{:S(2)}) copy-start(f32[1,24,2048]{2,1,0:T(8,128)} %shard_map.103) | copy-start | bytes 589828
  3.0 15.5 %collective-permute-start.1 = (f32[1,24,2048]{2,1,0:T(8,128)}, f32[1,24,2048]{2,1,0:T(8,128)S(1)}, u32[]{:S(2)}, u32[]{:S(2)}) collective-permute-start(f32[1,24,2048]{2,1,0:T(8,128)} %shard_map.103), channel_id=1, source_target_pairs={{0,192},{32,224},{64,128},{96,160},{128,64},{160,96},{192,0},{224,... | collective-permute-start | bytes 589832 | tf_op jit(solution)/shard_map/ppermute | solution.py:365
  10.0 10.4 %collective-permute-start = (f32[1,24,2048]{2,1,0:T(8,128)}, f32[1,24,2048]{2,1,0:T(8,128)S(1)}, u32[]{:S(2)}, u32[]{:S(2)}) collective-permute-start(f32[1,24,2048]{2,1,0:T(8,128)} %shard_map.103), channel_id=1, source_target_pairs={{0,64},{32,96},{64,0},{96,32},{128,192},{160,224},{192,128},{224,1... | collective-permute-start | bytes 589832 | tf_op jit(solution)/shard_map/ppermute | solution.py:365
  18.5 4.6 %collective-permute-start.2 = (f32[1,24,1024]{2,1,0:T(8,128)S(1)}, f32[1,24,1024]{2,1,0:T(8,128)S(1)}, u32[]{:S(2)}, u32[]{:S(2)}) collective-permute-start(f32[1,24,1024]{2,1,0:T(8,128)S(1)} %slice.32), channel_id=1, source_target_pairs={{0,64},{32,96},{64,0},{96,32},{128,192},{160,224},{192,128},{224,1... | collective-permute-start | bytes 294920 | tf_op jit(solution)/shard_map/ppermute | solution.py:365
  20.3 6.7 %collective-permute-start.3 = (f32[1,24,1024]{2,1,0:T(8,128)S(1)}, f32[1,24,1024]{2,1,0:T(8,128)S(1)}, u32[]{:S(2)}, u32[]{:S(2)}) collective-permute-start(f32[1,24,1024]{2,1,0:T(8,128)S(1)} %slice.33), channel_id=1, source_target_pairs={{0,192},{32,224},{64,128},{96,160},{128,64},{160,96},{192,0},{224,... | collective-permute-start | bytes 294920 | tf_op jit(solution)/shard_map/ppermute | solution.py:365
  30.1 3.5 %collective-permute-start.4 = (f32[184,128]{1,0:T(8,128)S(1)}, f32[184,128]{1,0:T(8,128)S(1)}, u32[]{:S(2)}, u32[]{:S(2)}) collective-permute-start(f32[184,128]{1,0:T(8,128)S(1)} %get-tuple-element.24), channel_id=1, source_target_pairs={{0,32},{32,0},{64,96},{96,64},{128,160},{160,128},{192,224},{224,1... | collective-permute-start | bytes 282632 | tf_op jit(solution)/shard_map/ppermute | solution.py:365
  33.6 4.7 %collective-permute-start.5 = (f32[120,128]{1,0:T(8,128)S(1)}, f32[120,128]{1,0:T(8,128)S(1)}, u32[]{:S(2)}, u32[]{:S(2)}) collective-permute-start(f32[120,128]{1,0:T(8,128)S(1)} %pad_maximum_fusion.1), channel_id=1, source_target_pairs={{0,1},{1,0},{2,3},{3,2},{4,5},{5,4},{6,7},{7,6},{8,9},{9,8},{10,11... | collective-permute-start | bytes 184328 | tf_op jit(solution)/shard_map/ppermute | solution.py:365
  38.4 4.7 %collective-permute-start.8 = (f32[120,128]{1,0:T(8,128)S(1)}, f32[120,128]{1,0:T(8,128)S(1)}, u32[]{:S(2)}, u32[]{:S(2)}) collective-permute-start(f32[120,128]{1,0:T(8,128)S(1)} %fusion.2), channel_id=1, source_target_pairs={{0,16},{1,17},{2,18},{3,19},{4,20},{5,21},{6,22},{7,23},{8,24},{9,... | collective-permute-start | bytes 184328 | tf_op jit(solution)/shard_map/ppermute | solution.py:365
  41.2 4.3 %collective-permute-start.7 = (f32[120,128]{1,0:T(8,128)S(1)}, f32[120,128]{1,0:T(8,128)S(1)}, u32[]{:S(2)}, u32[]{:S(2)}) collective-permute-start(f32[120,128]{1,0:T(8,128)S(1)} %fusion.2), channel_id=1, source_target_pairs={{0,24},{1,25},{2,26},{3,27},{4,28},{5,29},{6,30},{7,31},{8,16},{9,... | collective-permute-start | bytes 184328 | tf_op jit(solution)/shard_map/ppermute | solution.py:365
  42.1 3.4 %collective-permute-start.6 = (f32[120,128]{1,0:T(8,128)S(1)}, f32[120,128]{1,0:T(8,128)S(1)}, u32[]{:S(2)}, u32[]{:S(2)}) collective-permute-start(f32[120,128]{1,0:T(8,128)S(1)} %fusion.2), channel_id=1, source_target_pairs={{0,8},{1,9},{2,10},{3,11},{4,12},{5,13},{6,14},{7,15},{8,0},{9,1},... | collective-permute-start | bytes 184328 | tf_op jit(solution)/shard_map/ppermute | solution.py:365
  45.5 4.7 %collective-permute-start.11 = (f32[120,128]{1,0:T(8,128)S(1)}, f32[120,128]{1,0:T(8,128)S(1)}, u32[]{:S(2)}, u32[]{:S(2)}) collective-permute-start(f32[120,128]{1,0:T(8,128)S(1)} %add_add_fusion.5), channel_id=1, source_target_pairs={{0,4},{1,5},{2,6},{3,7},{4,0},{5,1},{6,2},{7,3},{8,12},{9,13},{10,... | collective-permute-start | bytes 184328 | tf_op jit(solution)/shard_map/ppermute | solution.py:365
  48.5 4.6 %collective-permute-start.10 = (f32[120,128]{1,0:T(8,128)S(1)}, f32[120,128]{1,0:T(8,128)S(1)}, u32[]{:S(2)}, u32[]{:S(2)}) collective-permute-start(f32[120,128]{1,0:T(8,128)S(1)} %add_add_fusion.5), channel_id=1, source_target_pairs={{0,6},{1,7},{2,4},{3,5},{4,2},{5,3},{6,0},{7,1},{8,14},{9,15},{10,... | collective-permute-start | bytes 184328 | tf_op jit(solution)/shard_map/ppermute | solution.py:365
  49.3 3.8 %collective-permute-start.9 = (f32[120,128]{1,0:T(8,128)S(1)}, f32[120,128]{1,0:T(8,128)S(1)}, u32[]{:S(2)}, u32[]{:S(2)}) collective-permute-start(f32[120,128]{1,0:T(8,128)S(1)} %add_add_fusion.5), channel_id=1, source_target_pairs={{0,2},{1,3},{2,0},{3,1},{4,6},{5,7},{6,4},{7,5},{8,10},{9,11},{10,... | collective-permute-start | bytes 184328 | tf_op jit(solution)/shard_map/ppermute | solution.py:365
  58.2 3.5 %collective-permute-start.12 = (f32[184,128]{1,0:T(8,128)S(1)}, f32[184,128]{1,0:T(8,128)S(1)}, u32[]{:S(2)}, u32[]{:S(2)}) collective-permute-start(f32[184,128]{1,0:T(8,128)S(1)} %get-tuple-element.26), channel_id=1, source_target_pairs={{0,32},{32,0},{64,96},{96,64},{128,160},{160,128},{192,224},{224,1... | collective-permute-start | bytes 282632 | tf_op jit(solution)/shard_map/ppermute | solution.py:365
  61.8 5.1 %collective-permute-start.13 = (f32[120,128]{1,0:T(8,128)S(1)}, f32[120,128]{1,0:T(8,128)S(1)}, u32[]{:S(2)}, u32[]{:S(2)}) collective-permute-start(f32[120,128]{1,0:T(8,128)S(1)} %pad_maximum_fusion.2), channel_id=1, source_target_pairs={{0,1},{1,0},{2,3},{3,2},{4,5},{5,4},{6,7},{7,6},{8,9},{9,8},{10,11... | collective-permute-start | bytes 184328 | tf_op jit(solution)/shard_map/ppermute | solution.py:365
  66.9 4.7 %collective-permute-start.16 = (f32[120,128]{1,0:T(8,128)S(1)}, f32[120,128]{1,0:T(8,128)S(1)}, u32[]{:S(2)}, u32[]{:S(2)}) collective-permute-start(f32[120,128]{1,0:T(8,128)S(1)} %fusion.1), channel_id=1, source_target_pairs={{0,16},{1,17},{2,18},{3,19},{4,20},{5,21},{6,22},{7,23},{8,24},{9,... | collective-permute-start | bytes 184328 | tf_op jit(solution)/shard_map/ppermute | solution.py:365
  68.1 5.3 %collective-permute-start.15 = (f32[120,128]{1,0:T(8,128)S(1)}, f32[120,128]{1,0:T(8,128)S(1)}, u32[]{:S(2)}, u32[]{:S(2)}) collective-permute-start(f32[120,128]{1,0:T(8,128)S(1)} %fusion.1), channel_id=1, source_target_pairs={{0,24},{1,25},{2,26},{3,27},{4,28},{5,29},{6,30},{7,31},{8,16},{9,... | collective-permute-start | bytes 184328 | tf_op jit(solution)/shard_map/ppermute | solution.py:365
  69.2 4.3 %collective-permute-start.14 = (f32[120,128]{1,0:T(8,128)S(1)}, f32[120,128]{1,0:T(8,128)S(1)}, u32[]{:S(2)}, u32[]{:S(2)}) collective-permute-start(f32[120,128]{1,0:T(8,128)S(1)} %fusion.1), channel_id=1, source_target_pairs={{0,8},{1,9},{2,10},{3,11},{4,12},{5,13},{6,14},{7,15},{8,0},{9,1},... | collective-permute-start | bytes 184328 | tf_op jit(solution)/shard_map/ppermute | solution.py:365
  73.5 4.7 %collective-permute-start.19 = (f32[120,128]{1,0:T(8,128)S(1)}, f32[120,128]{1,0:T(8,128)S(1)}, u32[]{:S(2)}, u32[]{:S(2)}) collective-permute-start(f32[120,128]{1,0:T(8,128)S(1)} %add_add_fusion.3), channel_id=1, source_target_pairs={{0,4},{1,5},{2,6},{3,7},{4,0},{5,1},{6,2},{7,3},{8,12},{9,13},{10,... | collective-permute-start | bytes 184328 | tf_op jit(solution)/shard_map/ppermute | solution.py:365
  74.8 5.0 %collective-permute-start.18 = (f32[120,128]{1,0:T(8,128)S(1)}, f32[120,128]{1,0:T(8,128)S(1)}, u32[]{:S(2)}, u32[]{:S(2)}) collective-permute-start(f32[120,128]{1,0:T(8,128)S(1)} %add_add_fusion.3), channel_id=1, source_target_pairs={{0,6},{1,7},{2,4},{3,5},{4,2},{5,3},{6,0},{7,1},{8,14},{9,15},{10,... | collective-permute-start | bytes 184328 | tf_op jit(solution)/shard_map/ppermute | solution.py:365
  75.5 4.3 %collective-permute-start.17 = (f32[120,128]{1,0:T(8,128)S(1)}, f32[120,128]{1,0:T(8,128)S(1)}, u32[]{:S(2)}, u32[]{:S(2)}) collective-permute-start(f32[120,128]{1,0:T(8,128)S(1)} %add_add_fusion.3), channel_id=1, source_target_pairs={{0,2},{1,3},{2,0},{3,1},{4,6},{5,7},{6,4},{7,5},{8,10},{9,11},{10,... | collective-permute-start | bytes 184328 | tf_op jit(solution)/shard_map/ppermute | solution.py:365
  85.0 3.5 %collective-permute-start.20 = (f32[184,128]{1,0:T(8,128)S(1)}, f32[184,128]{1,0:T(8,128)S(1)}, u32[]{:S(2)}, u32[]{:S(2)}) collective-permute-start(f32[184,128]{1,0:T(8,128)S(1)} %get-tuple-element.31), channel_id=1, source_target_pairs={{0,32},{32,0},{64,96},{96,64},{128,160},{160,128},{192,224},{224,1... | collective-permute-start | bytes 282632 | tf_op jit(solution)/shard_map/ppermute | solution.py:365
  88.6 3.8 %collective-permute-start.21 = (f32[120,128]{1,0:T(8,128)S(1)}, f32[120,128]{1,0:T(8,128)S(1)}, u32[]{:S(2)}, u32[]{:S(2)}) collective-permute-start(f32[120,128]{1,0:T(8,128)S(1)} %pad_maximum_fusion.3), channel_id=1, source_target_pairs={{0,1},{1,0},{2,3},{3,2},{4,5},{5,4},{6,7},{7,6},{8,9},{9,8},{10,11... | collective-permute-start | bytes 184328 | tf_op jit(solution)/shard_map/ppermute | solution.py:365
  92.4 4.7 %collective-permute-start.24 = (f32[120,128]{1,0:T(8,128)S(1)}, f32[120,128]{1,0:T(8,128)S(1)}, u32[]{:S(2)}, u32[]{:S(2)}) collective-permute-start(f32[120,128]{1,0:T(8,128)S(1)} %fusion), channel_id=1, source_target_pairs={{0,16},{1,17},{2,18},{3,19},{4,20},{5,21},{6,22},{7,23},{8,24},{9,... | collective-permute-start | bytes 184328 | tf_op jit(solution)/shard_map/ppermute | solution.py:365
  94.3 4.3 %collective-permute-start.23 = (f32[120,128]{1,0:T(8,128)S(1)}, f32[120,128]{1,0:T(8,128)S(1)}, u32[]{:S(2)}, u32[]{:S(2)}) collective-permute-start(f32[120,128]{1,0:T(8,128)S(1)} %fusion), channel_id=1, source_target_pairs={{0,24},{1,25},{2,26},{3,27},{4,28},{5,29},{6,30},{7,31},{8,16},{9,... | collective-permute-start | bytes 184328 | tf_op jit(solution)/shard_map/ppermute | solution.py:365
  95.2 3.3 %collective-permute-start.22 = (f32[120,128]{1,0:T(8,128)S(1)}, f32[120,128]{1,0:T(8,128)S(1)}, u32[]{:S(2)}, u32[]{:S(2)}) collective-permute-start(f32[120,128]{1,0:T(8,128)S(1)} %fusion), channel_id=1, source_target_pairs={{0,8},{1,9},{2,10},{3,11},{4,12},{5,13},{6,14},{7,15},{8,0},{9,1},... | collective-permute-start | bytes 184328 | tf_op jit(solution)/shard_map/ppermute | solution.py:365
  98.6 4.7 %collective-permute-start.27 = (f32[120,128]{1,0:T(8,128)S(1)}, f32[120,128]{1,0:T(8,128)S(1)}, u32[]{:S(2)}, u32[]{:S(2)}) collective-permute-start(f32[120,128]{1,0:T(8,128)S(1)} %add_add_fusion.1), channel_id=1, source_target_pairs={{0,4},{1,5},{2,6},{3,7},{4,0},{5,1},{6,2},{7,3},{8,12},{9,13},{10,... | collective-permute-start | bytes 184328 | tf_op jit(solution)/shard_map/ppermute | solution.py:365
  100.6 4.6 %collective-permute-start.26 = (f32[120,128]{1,0:T(8,128)S(1)}, f32[120,128]{1,0:T(8,128)S(1)}, u32[]{:S(2)}, u32[]{:S(2)}) collective-permute-start(f32[120,128]{1,0:T(8,128)S(1)} %add_add_fusion.1), channel_id=1, source_target_pairs={{0,6},{1,7},{2,4},{3,5},{4,2},{5,3},{6,0},{7,1},{8,14},{9,15},{10,... | collective-permute-start | bytes 184328 | tf_op jit(solution)/shard_map/ppermute | solution.py:365
  101.5 3.8 %collective-permute-start.25 = (f32[120,128]{1,0:T(8,128)S(1)}, f32[120,128]{1,0:T(8,128)S(1)}, u32[]{:S(2)}, u32[]{:S(2)}) collective-permute-start(f32[120,128]{1,0:T(8,128)S(1)} %add_add_fusion.1), channel_id=1, source_target_pairs={{0,2},{1,3},{2,0},{3,1},{4,6},{5,7},{6,4},{7,5},{8,10},{9,11},{10,... | collective-permute-start | bytes 184328 | tf_op jit(solution)/shard_map/ppermute | solution.py:365

commit v3 on v2

--- a/solution.py
+++ b/solution.py
@@ -152,13 +152,13 @@
     return jnp.concatenate(knots, axis=0), bounds
 
 
-def set_scalars(ref, base, scalars):
+def set_scalars(rest_ref, scalars):
     rows, lanes = iota((8, LO), 0), iota((8, LO), 1)
-    block = ref[base:]
+    block = rest_ref[N_C : N_C + N_B]
     for i, scalar in enumerate(scalars):
         here = jnp.logical_and(rows == i, lanes == SCALAR_LANE)
         block = jnp.where(here, jnp.broadcast_to(scalar, (8, LO)), block)
-    ref[base:] = block
+    rest_ref[N_C : N_C + N_B] = block
 
 
 def get_scalars(rest_ref):
@@ -216,10 +216,31 @@
     data_ref[0, RIGHT + 1 :] = jnp.zeros((PACKED - RIGHT - 1, ROWS), F32)
 
 
-def gather_kernel(window_ref, data_ref, *args):
-    wide_ref, knot_ref, star_ref, cal_ref = args
+def clear(refs):
+    for ref in refs:
+        ref[...] = jnp.zeros(ref.shape, F32)
+
+
+def add_sums(data_ref, slot, hots, row, window, member, rest_ref, cal_ref):
+    spread, cals = adjoint(data_ref, slot, hots, row)
+    cal_ref[...] += cals
+    knots, bounds = knot_sums(fold(spread), window_of(window, member))
+    at = N_C + N_B + N_K * member
+    rest_ref[at : at + N_K] = knots
+    rest_ref[N_C : N_C + N_B] += bounds
+
+
+def table_of(rows):
+    return jnp.concatenate(split(rows), axis=1)
+
+
+def knot_table(vec_ref, window, member):
+    return table_of(shifted_knots(vec_ref, window_of(window, member), member))
+
+
+def right_kernel(window_ref, data_ref, rest_ref, cal_ref):
     window = window_ref[0]
-    clear((wide_ref, star_ref, cal_ref))
+    clear((rest_ref, cal_ref))
     norm, size = 0.0, 0.0
     for member in range(GROUP):
         slot = member_of(window) ^ member
@@ -227,98 +248,119 @@
         coefs = data_ref[slot, :INDEX]
         norm += total(row * row)
         size += total(jnp.sum(coefs * coefs, axis=0, keepdims=True))
-        hots = hots_of(data_ref, slot, (0, 1, 2))
-        add_sums(data_ref, slot, hots, row, window, member, args)
-    finish_sums(args)
-    set_scalars(wide_ref, N_S + N_C, [norm, size])
-
-
-def clear(refs):
-    for ref in refs:
-        ref[...] = jnp.zeros(ref.shape, F32)
-
-
-def add_sums(data_ref, slot, hots, row, window, member, sums):
-    wide_ref, knot_ref, star_ref, cal_ref = sums
-    stars, spread, cals = adjoint(data_ref, slot, hots, row)
-    star_ref[...] += stars
-    cal_ref[...] += cals
-    knots, bounds = knot_sums(fold(spread), window_of(window, member))
-    knot_ref[N_K * member : N_K * member + N_K] = knots
-    wide_ref[N_S + N_C :] += bounds
-
-
-def finish_sums(sums):
-    wide_ref, _, star_ref, cal_ref = sums
-    wide_ref[:N_S] = fold(star_ref[...])
-    wide_ref[N_S : N_S + N_C] = fold(cal_ref[...])
-
-
-def apply(window, vec_ref, data_ref, scale, row_ref, sums=None):
-    vec = vec_ref[:N_Z]
-    star_table = jnp.concatenate(split(vec[:N_S]), axis=1)
-    cal_table = jnp.concatenate(split(vec[N_S : N_S + N_C]), axis=1)
-    if sums is not None:
-        clear((sums[0], sums[2], sums[3]))
-    for member in range(GROUP):
-        slot = member_of(window) ^ member
-        knots = shifted_knots(vec_ref, window_of(window, member), member)
-        tables = (star_table, jnp.concatenate(split(knots), axis=1), cal_table)
-        hots = hots_of(data_ref, slot, (0, 1, 2))
-        row = forward(data_ref, slot, hots, tables) * scale
-        row_ref[member : member + 1] = row
-        if sums is not None:
-            add_sums(data_ref, slot, hots, row * scale, window, member, sums)
-    if sums is not None:
-        finish_sums(sums)
-
-
-def first_kernel(window_ref, data_ref, stars_ref, rest_ref, *args):
-    wide_ref, knot_ref, grad_ref, row_ref, kept_ref, star_ref, cal_ref = args
+        hots = hots_of(data_ref, slot, (1, 2))
+        add_sums(data_ref, slot, hots, row, window, member, rest_ref, cal_ref)
+    rest_ref[:N_C] = fold(cal_ref[...])
+    set_scalars(rest_ref, [norm, size])
+
+
+def right_stars_kernel(window_ref, data_ref, out_ref, star_ref):
+    clear((star_ref,))
+    for member in range(GROUP):
+        slot = member_of(window_ref[0]) ^ member
+        row = data_ref[slot, RIGHT : RIGHT + 1]
+        star_ref[...] += adjoint(data_ref, slot, hots_of(data_ref, slot, (0,)), row)[0]
+    out_ref[...] = fold(star_ref[...])
+
+
+def stars_kernel(window_ref, data_ref, row_ref, kept_ref, out_ref, star_ref):
+    clear((star_ref,))
+    inverse = kept(kept_ref)[0]
+    for member in range(GROUP):
+        slot = member_of(window_ref[0]) ^ member
+        row = row_ref[member : member + 1] * inverse
+        star_ref[...] += adjoint(data_ref, slot, hots_of(data_ref, slot, (0,)), row)[0]
+    out_ref[...] = fold(star_ref[...])
+
+
+def taken_kernel(window_ref, data_ref, stars_ref, kept_ref, out_ref):
+    inverse = kept(kept_ref)[0]
+    table = table_of(stars_ref[...])
+    for member in range(GROUP):
+        slot = member_of(window_ref[0]) ^ member
+        hots = hots_of(data_ref, slot, (0,))
+        out_ref[member : member + 1] = forward(data_ref, slot, hots, (table,)) * inverse
+
+
+def first_kernel(window_ref, data_ref, stars_ref, rest_in_ref, *args):
+    rest_ref, grad_ref, row_ref, kept_ref, cal_ref = args
     window = window_ref[0]
-    norm, size, _ = get_scalars(rest_ref)
+    norm, size, _ = get_scalars(rest_in_ref)
     inverse, length = lax.rsqrt(size), jnp.sqrt(norm)
-    grad = read_sums(stars_ref, rest_ref) * inverse / length
+    grad = read_sums(stars_ref, rest_in_ref) * inverse / length
     grad_ref[...] = grad
     keep([inverse, length], kept_ref)
-    apply(window, grad_ref, data_ref, inverse, row_ref, (wide_ref, knot_ref, star_ref, cal_ref))
+    clear((rest_ref, cal_ref))
+    star_table, cal_table = table_of(grad[:N_S]), table_of(grad[N_S : N_S + N_C])
+    for member in range(GROUP):
+        slot = member_of(window) ^ member
+        hots = hots_of(data_ref, slot, (0, 1, 2))
+        tables = (star_table, knot_table(grad_ref, window, member), cal_table)
+        row = forward(data_ref, slot, hots, tables) * inverse
+        row_ref[member : member + 1] = row
+        add_sums(data_ref, slot, hots[1:], row * inverse, window, member, rest_ref, cal_ref)
+    rest_ref[:N_C] = fold(cal_ref[...])
     row = row_ref[...]
-    set_scalars(wide_ref, N_S + N_C, [square(grad), total(row * row)])
-
-
-def second_kernel(window_ref, data_ref, stars_ref, rest_ref, grad_ref, q_ref, old_ref, *args):
-    wide_ref, knot_ref, new_ref, image_ref, row_ref, kept_ref, star_ref, cal_ref = args
+    set_scalars(rest_ref, [square(grad), total(row * row)])
+
+
+def second_kernel(window_ref, data_ref, *args):
+    stars_ref, rest_in_ref, taken_ref, grad_ref, q_ref, old_ref = args[:6]
+    rest_ref, new_ref, image_ref, mapped_ref, row_ref, kept_ref, cal_ref = args[6:]
+    window = window_ref[0]
     inverse, length = kept(old_ref)[:2]
-    gamma, delta, _ = get_scalars(rest_ref)
-    image = read_sums(stars_ref, rest_ref)
+    gamma, delta, _ = get_scalars(rest_in_ref)
+    step = gamma / delta
+    image = read_sums(stars_ref, rest_in_ref)
     image_ref[...] = image
-    grad = grad_ref[...] - (gamma / delta) * image
+    grad = grad_ref[...] - step * image
     new_ref[...] = grad
     keep([inverse, length, gamma, delta], kept_ref)
-    sums = (wide_ref, knot_ref, star_ref, cal_ref)
-    apply(window_ref[0], new_ref, data_ref, inverse, row_ref, sums)
+    clear((rest_ref, cal_ref))
+    cal_table = table_of(image[N_S : N_S + N_C])
+    for member in range(GROUP):
+        slot = member_of(window) ^ member
+        own = slice(member, member + 1)
+        hots = hots_of(data_ref, slot, (1, 2))
+        tables = (knot_table(image_ref, window, member), cal_table)
+        mapped = taken_ref[own] + forward(data_ref, slot, hots, tables) * inverse
+        mapped_ref[own] = mapped
+        row = q_ref[own] - step * mapped
+        row_ref[own] = row
+        add_sums(data_ref, slot, hots, row * inverse, window, member, rest_ref, cal_ref)
+    rest_ref[:N_C] = fold(cal_ref[...])
     row = row_ref[...]
-    set_scalars(wide_ref, N_S + N_C, [square(grad), total(row * row), total(row * q_ref[...])])
+    set_scalars(rest_ref, [square(grad), total(row * row), total(row * q_ref[...])])
 
 
 def third_kernel(window_ref, data_ref, *args):
-    stars_ref, rest_ref, first_ref, grad_ref, image_ref, q_ref, row_ref, old_ref = args[:8]
-    new_ref, x_ref, direction_ref, kept_ref, scalar_ref, work_ref = args[8:]
+    stars_ref, rest_in_ref, taken_ref, first_ref, grad_ref, image_ref, mapped_ref = args[:7]
+    q_ref, row_ref, old_ref = args[7:10]
+    new_ref, x_ref, direction_ref, kept_ref, scalar_ref, work_ref, raw_ref = args[10:]
+    window = window_ref[0]
     inverse, length, gamma0, delta0 = kept(old_ref)[:4]
-    gamma1, square1, cross1 = get_scalars(rest_ref)
+    gamma1, square1, cross1 = get_scalars(rest_in_ref)
     beta = gamma1 / gamma0
     first, grad = first_ref[...], grad_ref[...]
     direction = grad + beta * first
     q = row_ref[...] + beta * q_ref[...]
     delta1 = square1 + 2.0 * beta * cross1 + beta * beta * delta0
-    image = read_sums(stars_ref, rest_ref) + beta * image_ref[...]
+    raw = read_sums(stars_ref, rest_in_ref)
+    raw_ref[...] = raw
     step = gamma1 / delta1
     x_ref[...] = (gamma0 / delta0) * first + step * direction
     direction_ref[...] = direction
-    grad = grad - step * image
+    grad = grad - step * (raw + beta * image_ref[...])
     new_ref[...] = grad
     keep([inverse, length, gamma1, delta1], kept_ref)
-    apply(window_ref[0], new_ref, data_ref, inverse, work_ref)
+    cal_table = table_of(raw[N_S : N_S + N_C])
+    for member in range(GROUP):
+        slot = member_of(window) ^ member
+        own = slice(member, member + 1)
+        hots = hots_of(data_ref, slot, (1, 2))
+        tables = (knot_table(raw_ref, window, member), cal_table)
+        mapped = taken_ref[own] + forward(data_ref, slot, hots, tables) * inverse
+        work_ref[own] = row_ref[own] - step * (mapped + beta * mapped_ref[own])
     row = work_ref[...]
     lane = iota((1, LO), 1)
     scalar_ref[...] = (
@@ -356,6 +398,7 @@
         + [pl.BlockSpec(memory_space=space)] * len(vmem),
         out_specs=[pl.BlockSpec(memory_space=pltpu.VMEM)] * len(outs),
         scratch_shapes=list(scratch),
+        cost_estimate=pl.CostEstimate(flops=1500000000, bytes_accessed=1000000, transcendentals=0),
         compiler_params=pltpu.CompilerParams(vmem_limit_bytes=mebibytes * 1024 * 1024),
     )(*smem, *vmem)
 
@@ -372,12 +415,6 @@
     return (value + arrived[0]) + (arrived[1] + arrived[2])
 
 
-def over_star(rest):
-    for bits in ((1,), (8, 24, 16), (2, 6, 4)):
-        rest = add_swapped(rest, "star", bits)
-    return rest
-
-
 def share(data):
     near, wrap = swap(data, TM, 2), swap(data, TM, 6)
     half = ROWS // 2
@@ -385,9 +422,15 @@
     return jnp.concatenate([data, near, jnp.concatenate(far, axis=2), wrap], axis=0)
 
 
-def reduce(wide, knots):
-    wide = add_swapped(wide, TM, REST)
-    return wide[:N_S], over_star(jnp.concatenate([wide[N_S:], knots], axis=0))
+def reduce(rest, add_stars, take_stars=None):
+    bounded = add_swapped(rest[: N_C + N_B], TM, REST)
+    bounded, stars = lax.optimization_barrier((bounded, add_stars()))
+    stars = add_swapped(stars, TM, REST)
+    rest = jnp.concatenate([bounded, rest[N_C + N_B :]], axis=0)
+    rest = add_swapped(add_swapped(rest, "star", (1,)), "star", (8, 24, 16))
+    rest, stars = lax.optimization_barrier((rest, stars))
+    taken = () if take_stars is None else (take_stars(stars),)
+    return (stars, add_swapped(rest, "star", (2, 6, 4))) + taken
 
 
 def shards(star_coef, att_coef, cal_coef, observed, star_index, knot_index, cal_index, valid_blocks):
@@ -401,10 +444,9 @@
         knot_index.reshape(1, ROWS),
         cal_index.reshape(1, ROWS),
     )
-    wide_shape, vec_shape, small = (N_Z, LO), (N_ALL, LO), (8, LO)
-    row_shape = (GROUP, ROWS)
-    sums = (wide_shape, (N_K * GROUP, LO))
-    scratch = [pltpu.VMEM((2 * N_S, LO), F32), pltpu.VMEM((2 * N_C, LO), F32)]
+    vec_shape, small, row_shape = (N_ALL, LO), (8, LO), (GROUP, ROWS)
+    rest_shape = (N_ALL - N_S, LO)
+    star_scratch, cal_scratch = [pltpu.VMEM((2 * N_S, LO), F32)], [pltpu.VMEM((2 * N_C, LO), F32)]
     (data,) = call(
         start_kernel,
         (valid_blocks,),
@@ -415,30 +457,35 @@
         60,
     )
     data = share(data)
-    wide, knots = call(gather_kernel, (window,), (data,), sums, scratch)
-    arrived = reduce(wide, knots)
-    wide, knots, grad0, row0, scalars = call(
-        first_kernel,
-        (window,),
-        (data,) + arrived,
-        sums + (vec_shape, row_shape, small),
-        scratch,
-    )
-    arrived = reduce(wide, knots)
-    wide, knots, grad1, image0, row1, scalars = call(
+
+    def star_sums(row, kept_scalars):
+        return call(stars_kernel, (window,), (data, row, kept_scalars), ((N_S, LO),), star_scratch)[0]
+
+    def taken(stars, kept_scalars):
+        return call(taken_kernel, (window,), (data, stars, kept_scalars), (row_shape,))[0]
+
+    (rest,) = call(right_kernel, (window,), (data,), (rest_shape,), cal_scratch)
+    arrived = reduce(
+        rest, lambda: call(right_stars_kernel, (window,), (data,), ((N_S, LO),), star_scratch)[0]
+    )
+    rest, grad0, row0, scalars0 = call(
+        first_kernel, (window,), (data,) + arrived, (rest_shape, vec_shape, row_shape, small), cal_scratch
+    )
+    arrived = reduce(rest, lambda: star_sums(row0, scalars0), lambda stars: taken(stars, scalars0))
+    rest, grad1, image0, mapped0, row1, scalars1 = call(
         second_kernel,
         (window,),
-        (data,) + arrived + (grad0, row0, scalars),
-        sums + (vec_shape, vec_shape, row_shape, small),
-        scratch,
-    )
-    arrived = reduce(wide, knots)
+        (data,) + arrived + (grad0, row0, scalars0),
+        (rest_shape, vec_shape, vec_shape, row_shape, row_shape, small),
+        cal_scratch,
+    )
+    arrived = reduce(rest, lambda: star_sums(row1, scalars1), lambda stars: taken(stars, scalars1))
     grad2, x, direction, scalars, partial = call(
         third_kernel,
         (window,),
-        (data,) + arrived + (grad0, grad1, image0, row0, row1, scalars),
+        (data,) + arrived + (grad0, grad1, image0, mapped0, row0, row1, scalars1),
         (vec_shape, vec_shape, vec_shape, small, (1, LO)),
-        [pltpu.VMEM(row_shape, F32)],
+        [pltpu.VMEM(row_shape, F32), pltpu.VMEM(vec_shape, F32)],
     )
     axes = ("tm_low", "star")
     count = lax.axis_size(axes)

time: 126 us -> 118 us (0.937)
  waiting for transfers between devices: 43.1 us -> 32.2 us
  starting transfers between devices: 45.4 us -> 47.5 us
  Pallas kernels: 18.5 us -> 20.4 us
    ppermute x28 -> x31, waiting for transfers between devices: 43.1 us -> 32.2 us  [swap(): return lax.ppermute(value, axis, [(i, i ^ bits) for i in range(count)])]
    ppermute x28 -> x31, starting transfers between devices: 45.4 us -> 47.5 us  [swap(): return lax.ppermute(value, axis, [(i, i ^ bits) for i in range(count)])]
    pallas_call x6 -> x11, Pallas kernels: 18.5 us -> 20.4 us  [call(): pl.pallas_call(kernel, out_shape=[jax.ShapeDtypeStruct(shape, F32) for sh...]
  transfers between devices with their start and end apart: 28 -> 31, of which waited for: 21 -> 20; matrix products, arithmetic and copies ran while one was open for 0% -> 0% of each run, Pallas kernels for 0% -> 6%
where the time goes in v3:
time: 118 us
  starting transfers between devices  47.5 us (40%)
  waiting for transfers between devices  32.2 us (27%)
  Pallas kernels  20.4 us (17%)
  blocking collectives  16.3 us (14%)
  between operations  1.45 us (1%)
    ppermute x31, starting transfers between devices, swap(): return lax.ppermute(value, axis, [(i, i ^ bits) for i in range(count)])  47.5 us
    ppermute x31, waiting for transfers between devices, swap(): return lax.ppermute(value, axis, [(i, i ^ bits) for i in range(count)])  32.2 us
    pallas_call x11, Pallas kernels, call(): pl.pallas_call(kernel, out_shape=[jax.ShapeDtypeStruct(shape, F32) for sh...  20.4 us
    all_to_all x1, blocking collectives, shards(): lax.all_to_all(jnp.broadcast_to(partial[None], (count, 1, LO)), axes, 0, 0)  16.3 us
  transfers between devices with their start and end apart: 31, of which 20 were waited for; matrix products, arithmetic and copies ran while one was open for 0% of the time, Pallas kernels for 6%

profile of v3, /device:TPU:1, one launch (start us, length us, event | category | flops | bytes accessed | tf_op | source)
XLA Modules:
  0.0 118.3 jit_solution(11233910141996166371)
XLA Ops:
  1.3 1.7 %shard_map.103 = f32[1,24,2048]{2,1,0:T(8,128)} custom-call(s32[1,1]{1,0:T(1,128)S(6)} %copy.11.blocks_ref, f32[5,2048]{1,0:T(8,128)} %args_0_.4, f32[12,2048]{1,0:T(8,128)} %args_1_.4, f32[1,2048]{1,0:T(1,128)} %bitcast.11, f32[1,2048]{1,0:T(1,128)} %bitcast.12, s32[1,2048]{1,0:T(1,128)} %bitcast.13, s32[1,2048]{1,0:T(1,128)} %bitcast.14, s32[1,2048]{1,0:T(1,128)} %bitcast.15), custom_call_target="tpu_custom_call" | custom-call | flops 1500000000 | bytes 1000000 | tf_op jit(solution)/shard_map/pallas_call | solution.py:394
  3.0 6.9 %collective-permute-start.1 = (f32[1,24,2048]{2,1,0:T(8,128)}, f32[1,24,2048]{2,1,0:T(8,128)S(1)}, u32[]{:S(2)}, u32[]{:S(2)}) collective-permute-start(f32[1,24,2048]{2,1,0:T(8,128)} %shard_map.103), channel_id=1, source_target_pairs={{0,192},{32,224},{64,128},{96,160},{128,64},{160,96},{192,0},{224,... | collective-permute-start | bytes 589832 | tf_op jit(solution)/shard_map/ppermute | solution.py:408
  10.0 1.2 collective-permute-start
  11.1 7.4 %collective-permute-done.1 = f32[1,24,2048]{2,1,0:T(8,128)S(1)} collective-permute-done((f32[1,24,2048]{2,1,0:T(8,128)}, f32[1,24,2048]{2,1,0:T(8,128)S(1)}, u32[]{:S(2)}, u32[]{:S(2)}) %collective-permute-start.1) | collective-permute-done | bytes 196640 | tf_op jit(solution)/shard_map/ppermute | solution.py:408
  18.5 1.8 %collective-permute-start.2 = (f32[1,24,1024]{2,1,0:T(8,128)S(1)}, f32[1,24,1024]{2,1,0:T(8,128)S(1)}, u32[]{:S(2)}, u32[]{:S(2)}) collective-permute-start(f32[1,24,1024]{2,1,0:T(8,128)S(1)} %slice.32), channel_id=1, source_target_pairs={{0,64},{32,96},{64,0},{96,32},{128,192},{160,224},{192,128},{224,1... | collective-permute-start | bytes 294920 | tf_op jit(solution)/shard_map/ppermute | solution.py:408
  20.3 2.7 %collective-permute-start.3 = (f32[1,24,1024]{2,1,0:T(8,128)S(1)}, f32[1,24,1024]{2,1,0:T(8,128)S(1)}, u32[]{:S(2)}, u32[]{:S(2)}) collective-permute-start(f32[1,24,1024]{2,1,0:T(8,128)S(1)} %slice.33), channel_id=1, source_target_pairs={{0,192},{32,224},{64,128},{96,160},{128,64},{160,96},{192,0},{224,... | collective-permute-start | bytes 294920 | tf_op jit(solution)/shard_map/ppermute | solution.py:408
  23.1 4.0 %collective-permute-done.3 = f32[1,24,1024]{2,1,0:T(8,128)S(1)} collective-permute-done((f32[1,24,1024]{2,1,0:T(8,128)S(1)}, f32[1,24,1024]{2,1,0:T(8,128)S(1)}, u32[]{:S(2)}, u32[]{:S(2)}) %collective-permute-start.3) | collective-permute-done | bytes 98336 | tf_op jit(solution)/shard_map/ppermute | solution.py:408
  27.0 0.1 pad_maximum_fusion.data_ref
  27.1 1.9 %shard_map.104 = f32[120,128]{1,0:T(8,128)S(1)} custom-call(s32[1]{0:T(128)} %bitcast.window_ref, f32[4,24,2048]{2,1,0:T(8,128)S(1)} %pad_maximum_fusion.data_ref), custom_call_target="tpu_custom_call" | custom-call | flops 1500000000 | bytes 1000000 | tf_op jit(solution)/shard_map/pallas_call | solution.py:394
  29.1 0.2 collective-permute-start.4
  29.3 1.5 %shard_map.105 = f32[160,128]{1,0:T(8,128)S(1)} custom-call(s32[1]{0:T(128)} %bitcast.window_ref, f32[4,24,2048]{2,1,0:T(8,128)S(1)} %pad_maximum_fusion.data_ref), custom_call_target="tpu_custom_call" | custom-call | flops 1500000000 | bytes 1000000 | tf_op jit(solution)/shard_map/pallas_call | solution.py:394
  30.8 0.9 collective-permute-done.4
  31.7 3.8 %collective-permute-start.5 = (f32[120,128]{1,0:T(8,128)S(1)}, f32[120,128]{1,0:T(8,128)S(1)}, u32[]{:S(2)}, u32[]{:S(2)}) collective-permute-start(f32[120,128]{1,0:T(8,128)S(1)} %pad_maximum_fusion.1), channel_id=1, source_target_pairs={{0,1},{1,0},{2,3},{3,2},{4,5},{5,4},{6,7},{7,6},{8,9},{9,8},{10,11... | collective-permute-start | bytes 184328 | tf_op jit(solution)/shard_map/ppermute | solution.py:408
  35.5 1.4 %collective-permute-start.9 = (f32[160,128]{1,0:T(8,128)S(1)}, f32[160,128]{1,0:T(8,128)S(1)}, u32[]{:S(2)}, u32[]{:S(2)}) collective-permute-start(f32[160,128]{1,0:T(8,128)S(1)} %shard_map.105), channel_id=1, source_target_pairs={{0,32},{32,0},{64,96},{96,64},{128,160},{160,128},{192,224},{224,1... | collective-permute-start | bytes 245768 | tf_op jit(solution)/shard_map/ppermute | solution.py:408
  36.9 2.8 %collective-permute-start.8 = (f32[120,128]{1,0:T(8,128)S(1)}, f32[120,128]{1,0:T(8,128)S(1)}, u32[]{:S(2)}, u32[]{:S(2)}) collective-permute-start(f32[120,128]{1,0:T(8,128)S(1)} %fusion.2), channel_id=1, source_target_pairs={{0,16},{1,17},{2,18},{3,19},{4,20},{5,21},{6,22},{7,23},{8,24},{9,... | collective-permute-start | bytes 184328 | tf_op jit(solution)/shard_map/ppermute | solution.py:408
  39.8 0.9 collective-permute-start.7
  40.7 0.9 collective-permute-done.8
  41.6 2.5 %collective-permute-done.7 = f32[120,128]{1,0:T(8,128)S(1)} collective-permute-done((f32[120,128]{1,0:T(8,128)S(1)}, f32[120,128]{1,0:T(8,128)S(1)}, u32[]{:S(2)}, u32[]{:S(2)}) %collective-permute-start.7) | collective-permute-done | bytes 61472 | tf_op jit(solution)/shard_map/ppermute | solution.py:408
  44.1 3.0 %collective-permute-start.12 = (f32[120,128]{1,0:T(8,128)S(1)}, f32[120,128]{1,0:T(8,128)S(1)}, u32[]{:S(2)}, u32[]{:S(2)}) collective-permute-start(f32[120,128]{1,0:T(8,128)S(1)} %add_add_fusion.5), channel_id=1, source_target_pairs={{0,4},{1,5},{2,6},{3,7},{4,0},{5,1},{6,2},{7,3},{8,12},{9,13},{10,... | collective-permute-start | bytes 184328 | tf_op jit(solution)/shard_map/ppermute | solution.py:408
  47.1 0.8 collective-permute-start.11
  47.9 0.0 collective-permute-start.10
  47.9 0.9 collective-permute-done.12
  48.7 2.9 %collective-permute-done.11 = f32[120,128]{1,0:T(8,128)S(1)} collective-permute-done((f32[120,128]{1,0:T(8,128)S(1)}, f32[120,128]{1,0:T(8,128)S(1)}, u32[]{:S(2)}, u32[]{:S(2)}) %collective-permute-start.11) | collective-permute-done | bytes 61472 | tf_op jit(solution)/shard_map/ppermute | solution.py:408
  51.7 4.2 %shard_map.106 = (f32[120,128]{1,0:T(8,128)S(1)}, f32[280,128]{1,0:T(8,128)S(1)}, f32[4,2048]{1,0:T(4,128)S(1)}, f32[8,128]{1,0:T(8,128)S(1)}) custom-call(s32[1]{0:T(128)} %bitcast.window_ref, f32[4,24,2048]{2,1,0:T(8,128)S(1)} %pad_maximum_fusion.data_ref, f32[160,128]{1,0:T(8,128)S(1)} %add.90.stars_ref, f32[120,128]{1,0:T(8,128)S(1)} %add_add_fusion.4.rest_in_ref), custom_call_target="tpu_custom_call" | custom-call | flops 1500000000 | bytes 1000000 | tf_op jit(solution)/shard_map/pallas_call | solution.py:394
  55.9 0.9 collective-permute-start.13
  56.8 1.6 %shard_map.107 = f32[160,128]{1,0:T(8,128)S(1)} custom-call(s32[1]{0:T(128)} %bitcast.window_ref, f32[4,24,2048]{2,1,0:T(8,128)S(1)} %pad_maximum_fusion.data_ref, f32[4,2048]{1,0:T(4,128)S(1)} %get-tuple-element.38.row_ref.args_4_.args_7_, f32[8,128]{1,0:T(8,128)S(1)} %get-tuple-element.39.kept_ref.args_5_), custom_call_target="tpu_custom_call" | custom-call | flops 1500000000 | bytes 1000000 | tf_op jit(solution)/shard_map/pallas_call | solution.py:394
  58.4 0.1 collective-permute-done.13
  58.5 4.2 %collective-permute-start.14 = (f32[120,128]{1,0:T(8,128)S(1)}, f32[120,128]{1,0:T(8,128)S(1)}, u32[]{:S(2)}, u32[]{:S(2)}) collective-permute-start(f32[120,128]{1,0:T(8,128)S(1)} %pad_maximum_fusion.2), channel_id=1, source_target_pairs={{0,1},{1,0},{2,3},{3,2},{4,5},{5,4},{6,7},{7,6},{8,9},{9,8},{10,11... | collective-permute-start | bytes 184328 | tf_op jit(solution)/shard_map/ppermute | solution.py:408
  62.7 0.9 collective-permute-start.18
  63.6 0.0 collective-permute-done.14
  63.6 1.3 %collective-permute-start.17 = (f32[120,128]{1,0:T(8,128)S(1)}, f32[120,128]{1,0:T(8,128)S(1)}, u32[]{:S(2)}, u32[]{:S(2)}) collective-permute-start(f32[120,128]{1,0:T(8,128)S(1)} %fusion.1), channel_id=1, source_target_pairs={{0,16},{1,17},{2,18},{3,19},{4,20},{5,21},{6,22},{7,23},{8,24},{9,... | collective-permute-start | bytes 184328 | tf_op jit(solution)/shard_map/ppermute | solution.py:408
  64.8 1.0 collective-permute-start.16
  65.9 0.4 collective-permute-start.15
  66.3 0.4 collective-permute-done.18
  66.7 1.5 %collective-permute-done.17 = f32[120,128]{1,0:T(8,128)S(1)} collective-permute-done((f32[120,128]{1,0:T(8,128)S(1)}, f32[120,128]{1,0:T(8,128)S(1)}, u32[]{:S(2)}, u32[]{:S(2)}) %collective-permute-start.17) | collective-permute-done | bytes 61472 | tf_op jit(solution)/shard_map/ppermute | solution.py:408
  68.2 1.9 %collective-permute-done.16 = f32[120,128]{1,0:T(8,128)S(1)} collective-permute-done((f32[120,128]{1,0:T(8,128)S(1)}, f32[120,128]{1,0:T(8,128)S(1)}, u32[]{:S(2)}, u32[]{:S(2)}) %collective-permute-start.16) | collective-permute-done | bytes 61472 | tf_op jit(solution)/shard_map/ppermute | solution.py:408
  70.2 1.3 %collective-permute-start.21 = (f32[120,128]{1,0:T(8,128)S(1)}, f32[120,128]{1,0:T(8,128)S(1)}, u32[]{:S(2)}, u32[]{:S(2)}) collective-permute-start(f32[120,128]{1,0:T(8,128)S(1)} %add_add_fusion.3), channel_id=1, source_target_pairs={{0,4},{1,5},{2,6},{3,7},{4,0},{5,1},{6,2},{7,3},{8,12},{9,13},{10,... | collective-permute-start | bytes 184328 | tf_op jit(solution)/shard_map/ppermute | solution.py:408
  71.5 0.7 collective-permute-start.20
  72.2 0.7 collective-permute-start.19
  72.9 0.9 shard_map.108.args_2_
  73.9 1.0 collective-permute-done.21
  74.8 1.7 %collective-permute-done.20 = f32[120,128]{1,0:T(8,128)S(1)} collective-permute-done((f32[120,128]{1,0:T(8,128)S(1)}, f32[120,128]{1,0:T(8,128)S(1)}, u32[]{:S(2)}, u32[]{:S(2)}) %collective-permute-start.20) | collective-permute-done | bytes 61472 | tf_op jit(solution)/shard_map/ppermute | solution.py:408
  76.5 3.4 %shard_map.109 = (f32[120,128]{1,0:T(8,128)S(1)}, f32[280,128]{1,0:T(8,128)S(1)}, f32[280,128]{1,0:T(8,128)S(1)}, f32[4,2048]{1,0:T(4,128)S(1)}, f32[4,2048]{1,0:T(4,128)S(1)}, /*index=5*/f32[8,128]{1,0:T(8,128)S(1)}) custom-call(s32[1]{0:T(128)} %bitcast.window_ref, f32[4,24,2048]{2,1,0:T(8,128)S(1)} %pad_maximum_fusion.data_ref, ...), custom_call_target="tpu_custom_call" | custom-call | flops 1500000000 | bytes 1000000 | tf_op jit(solution)/shard_map/pallas_call | solution.py:394
  79.9 0.9 collective-permute-start.22
  80.9 1.6 %shard_map.110 = f32[160,128]{1,0:T(8,128)S(1)} custom-call(s32[1]{0:T(128)} %bitcast.window_ref, f32[4,24,2048]{2,1,0:T(8,128)S(1)} %pad_maximum_fusion.data_ref, f32[4,2048]{1,0:T(4,128)S(1)} %get-tuple-element.46.row_ref.args_8_, f32[8,128]{1,0:T(8,128)S(1)} %get-tuple-element.47.kept_ref.args_9_), custom_call_target="tpu_custom_call" | custom-call | flops 1500000000 | bytes 1000000 | tf_op jit(solution)/shard_map/pallas_call | solution.py:394
  82.4 0.1 collective-permute-done.22
  82.6 2.9 %collective-permute-start.23 = (f32[120,128]{1,0:T(8,128)S(1)}, f32[120,128]{1,0:T(8,128)S(1)}, u32[]{:S(2)}, u32[]{:S(2)}) collective-permute-start(f32[120,128]{1,0:T(8,128)S(1)} %pad_maximum_fusion.3), channel_id=1, source_target_pairs={{0,1},{1,0},{2,3},{3,2},{4,5},{5,4},{6,7},{7,6},{8,9},{9,8},{10,11... | collective-permute-start | bytes 184328 | tf_op jit(solution)/shard_map/ppermute | solution.py:408
  85.4 0.9 collective-permute-start.27
  86.3 0.0 collective-permute-done.23
  86.3 1.9 %collective-permute-start.26 = (f32[120,128]{1,0:T(8,128)S(1)}, f32[120,128]{1,0:T(8,128)S(1)}, u32[]{:S(2)}, u32[]{:S(2)}) collective-permute-start(f32[120,128]{1,0:T(8,128)S(1)} %fusion), channel_id=1, source_target_pairs={{0,16},{1,17},{2,18},{3,19},{4,20},{5,21},{6,22},{7,23},{8,24},{9,... | collective-permute-start | bytes 184328 | tf_op jit(solution)/shard_map/ppermute | solution.py:408
  88.3 0.9 collective-permute-start.25
  89.2 0.2 collective-permute-done.27
  89.5 1.5 %collective-permute-done.26 = f32[120,128]{1,0:T(8,128)S(1)} collective-permute-done((f32[120,128]{1,0:T(8,128)S(1)}, f32[120,128]{1,0:T(8,128)S(1)}, u32[]{:S(2)}, u32[]{:S(2)}) %collective-permute-start.26) | collective-permute-done | bytes 61472 | tf_op jit(solution)/shard_map/ppermute | solution.py:408
  91.0 1.6 %collective-permute-done.25 = f32[120,128]{1,0:T(8,128)S(1)} collective-permute-done((f32[120,128]{1,0:T(8,128)S(1)}, f32[120,128]{1,0:T(8,128)S(1)}, u32[]{:S(2)}, u32[]{:S(2)}) %collective-permute-start.25) | collective-permute-done | bytes 61472 | tf_op jit(solution)/shard_map/ppermute | solution.py:408
  92.6 2.0 %collective-permute-start.30 = (f32[120,128]{1,0:T(8,128)S(1)}, f32[120,128]{1,0:T(8,128)S(1)}, u32[]{:S(2)}, u32[]{:S(2)}) collective-permute-start(f32[120,128]{1,0:T(8,128)S(1)} %add_add_fusion.1), channel_id=1, source_target_pairs={{0,4},{1,5},{2,6},{3,7},{4,0},{5,1},{6,2},{7,3},{8,12},{9,13},{10,... | collective-permute-start | bytes 184328 | tf_op jit(solution)/shard_map/ppermute | solution.py:408
  94.6 0.9 collective-permute-start.29
  95.5 0.0 collective-permute-start.28
  95.5 1.0 shard_map.111.args_2_
  96.5 0.8 collective-permute-done.30
  97.2 1.9 %collective-permute-done.29 = f32[120,128]{1,0:T(8,128)S(1)} collective-permute-done((f32[120,128]{1,0:T(8,128)S(1)}, f32[120,128]{1,0:T(8,128)S(1)}, u32[]{:S(2)}, u32[]{:S(2)}) %collective-permute-start.29) | collective-permute-done | bytes 61472 | tf_op jit(solution)/shard_map/ppermute | solution.py:408
  99.2 0.1 collective-permute-done.28
  99.3 1.7 %shard_map.112 = (f32[280,128]{1,0:T(8,128)S(1)}, f32[280,128]{1,0:T(8,128)S(1)}, f32[280,128]{1,0:T(8,128)S(1)}, f32[8,128]{1,0:T(8,128)S(1)}, f32[1,128]{1,0:T(1,128)S(1)}) custom-call(s32[1]{0:T(128)} %bitcast.window_ref, f32[4,24,2048]{2,1,0:T(8,128)S(1)} %pad_maximum_fusion.data_ref, f32[160,128]{1,0:T(8,128)S(1)} %add.108.stars_ref.args_0_, ...), custom_call_target="tpu_custom_call" | custom-call | flops 1500000000 | bytes 1000000 | tf_op jit(solution)/shard_map/pallas_call | solution.py:394
  101.0 16.3 %all_to_all.5 = f32[64,1,128]{2,1,0:T(1,128)S(1)} all-to-all(f32[64,1,128]{2,1,0:T(1,128)S(1)} %broadcast_in_dim.9), channel_id=1, replica_groups=mesh['tm_high'=4,'tm_low'=2,'star'=32] {'tm_low','star'}, dimensions={0} | all-to-all | bytes 65536 | tf_op jit(solution)/shard_map/all_to_all | solution.py:492
  117.3 1.0 shard_map.113
  (40 shorter events, 0.3 us)
Async XLA Ops:
  3.0 24.0 %copy-start = (f32[1,24,2048]{2,1,0:T(8,128)S(1)}, f32[1,24,2048]{2,1,0:T(8,128)}, u32[]{:S(2)}) copy-start(f32[1,24,2048]{2,1,0:T(8,128)} %shard_map.103) | copy-start | bytes 589828
  3.0 15.5 %collective-permute-start.1 = (f32[1,24,2048]{2,1,0:T(8,128)}, f32[1,24,2048]{2,1,0:T(8,128)S(1)}, u32[]{:S(2)}, u32[]{:S(2)}) collective-permute-start(f32[1,24,2048]{2,1,0:T(8,128)} %shard_map.103), channel_id=1, source_target_pairs={{0,192},{32,224},{64,128},{96,160},{128,64},{160,96},{192,0},{224,... | collective-permute-start | bytes 589832 | tf_op jit(solution)/shard_map/ppermute | solution.py:408
  10.0 10.4 %collective-permute-start = (f32[1,24,2048]{2,1,0:T(8,128)}, f32[1,24,2048]{2,1,0:T(8,128)S(1)}, u32[]{:S(2)}, u32[]{:S(2)}) collective-permute-start(f32[1,24,2048]{2,1,0:T(8,128)} %shard_map.103), channel_id=1, source_target_pairs={{0,64},{32,96},{64,0},{96,32},{128,192},{160,224},{192,128},{224,1... | collective-permute-start | bytes 589832 | tf_op jit(solution)/shard_map/ppermute | solution.py:408
  18.5 4.6 %collective-permute-start.2 = (f32[1,24,1024]{2,1,0:T(8,128)S(1)}, f32[1,24,1024]{2,1,0:T(8,128)S(1)}, u32[]{:S(2)}, u32[]{:S(2)}) collective-permute-start(f32[1,24,1024]{2,1,0:T(8,128)S(1)} %slice.32), channel_id=1, source_target_pairs={{0,64},{32,96},{64,0},{96,32},{128,192},{160,224},{192,128},{224,1... | collective-permute-start | bytes 294920 | tf_op jit(solution)/shard_map/ppermute | solution.py:408
  20.3 6.7 %collective-permute-start.3 = (f32[1,24,1024]{2,1,0:T(8,128)S(1)}, f32[1,24,1024]{2,1,0:T(8,128)S(1)}, u32[]{:S(2)}, u32[]{:S(2)}) collective-permute-start(f32[1,24,1024]{2,1,0:T(8,128)S(1)} %slice.33), channel_id=1, source_target_pairs={{0,192},{32,224},{64,128},{96,160},{128,64},{160,96},{192,0},{224,... | collective-permute-start | bytes 294920 | tf_op jit(solution)/shard_map/ppermute | solution.py:408
  29.1 2.6 %collective-permute-start.4 = (f32[24,128]{1,0:T(8,128)S(1)}, f32[24,128]{1,0:T(8,128)S(1)}, u32[]{:S(2)}, u32[]{:S(2)}) collective-permute-start(f32[24,128]{1,0:T(8,128)S(1)} %slice.34), channel_id=1, source_target_pairs={{0,32},{32,0},{64,96},{96,64},{128,160},{160,128},{192,224},{224,1... | collective-permute-start | bytes 36872 | tf_op jit(solution)/shard_map/ppermute | solution.py:408
  31.7 5.2 %collective-permute-start.5 = (f32[120,128]{1,0:T(8,128)S(1)}, f32[120,128]{1,0:T(8,128)S(1)}, u32[]{:S(2)}, u32[]{:S(2)}) collective-permute-start(f32[120,128]{1,0:T(8,128)S(1)} %pad_maximum_fusion.1), channel_id=1, source_target_pairs={{0,1},{1,0},{2,3},{3,2},{4,5},{5,4},{6,7},{7,6},{8,9},{9,8},{10,11... | collective-permute-start | bytes 184328 | tf_op jit(solution)/shard_map/ppermute | solution.py:408
  35.5 5.1 %collective-permute-start.9 = (f32[160,128]{1,0:T(8,128)S(1)}, f32[160,128]{1,0:T(8,128)S(1)}, u32[]{:S(2)}, u32[]{:S(2)}) collective-permute-start(f32[160,128]{1,0:T(8,128)S(1)} %shard_map.105), channel_id=1, source_target_pairs={{0,32},{32,0},{64,96},{96,64},{128,160},{160,128},{192,224},{224,1... | collective-permute-start | bytes 245768 | tf_op jit(solution)/shard_map/ppermute | solution.py:408
  36.9 4.7 %collective-permute-start.8 = (f32[120,128]{1,0:T(8,128)S(1)}, f32[120,128]{1,0:T(8,128)S(1)}, u32[]{:S(2)}, u32[]{:S(2)}) collective-permute-start(f32[120,128]{1,0:T(8,128)S(1)} %fusion.2), channel_id=1, source_target_pairs={{0,16},{1,17},{2,18},{3,19},{4,20},{5,21},{6,22},{7,23},{8,24},{9,... | collective-permute-start | bytes 184328 | tf_op jit(solution)/shard_map/ppermute | solution.py:408
  39.8 4.3 %collective-permute-start.7 = (f32[120,128]{1,0:T(8,128)S(1)}, f32[120,128]{1,0:T(8,128)S(1)}, u32[]{:S(2)}, u32[]{:S(2)}) collective-permute-start(f32[120,128]{1,0:T(8,128)S(1)} %fusion.2), channel_id=1, source_target_pairs={{0,24},{1,25},{2,26},{3,27},{4,28},{5,29},{6,30},{7,31},{8,16},{9,... | collective-permute-start | bytes 184328 | tf_op jit(solution)/shard_map/ppermute | solution.py:408
  40.6 3.4 %collective-permute-start.6 = (f32[120,128]{1,0:T(8,128)S(1)}, f32[120,128]{1,0:T(8,128)S(1)}, u32[]{:S(2)}, u32[]{:S(2)}) collective-permute-start(f32[120,128]{1,0:T(8,128)S(1)} %fusion.2), channel_id=1, source_target_pairs={{0,8},{1,9},{2,10},{3,11},{4,12},{5,13},{6,14},{7,15},{8,0},{9,1},... | collective-permute-start | bytes 184328 | tf_op jit(solution)/shard_map/ppermute | solution.py:408
  44.1 4.7 %collective-permute-start.12 = (f32[120,128]{1,0:T(8,128)S(1)}, f32[120,128]{1,0:T(8,128)S(1)}, u32[]{:S(2)}, u32[]{:S(2)}) collective-permute-start(f32[120,128]{1,0:T(8,128)S(1)} %add_add_fusion.5), channel_id=1, source_target_pairs={{0,4},{1,5},{2,6},{3,7},{4,0},{5,1},{6,2},{7,3},{8,12},{9,13},{10,... | collective-permute-start | bytes 184328 | tf_op jit(solution)/shard_map/ppermute | solution.py:408
  47.1 4.6 %collective-permute-start.11 = (f32[120,128]{1,0:T(8,128)S(1)}, f32[120,128]{1,0:T(8,128)S(1)}, u32[]{:S(2)}, u32[]{:S(2)}) collective-permute-start(f32[120,128]{1,0:T(8,128)S(1)} %add_add_fusion.5), channel_id=1, source_target_pairs={{0,6},{1,7},{2,4},{3,5},{4,2},{5,3},{6,0},{7,1},{8,14},{9,15},{10,... | collective-permute-start | bytes 184328 | tf_op jit(solution)/shard_map/ppermute | solution.py:408
  47.9 3.8 %collective-permute-start.10 = (f32[120,128]{1,0:T(8,128)S(1)}, f32[120,128]{1,0:T(8,128)S(1)}, u32[]{:S(2)}, u32[]{:S(2)}) collective-permute-start(f32[120,128]{1,0:T(8,128)S(1)} %add_add_fusion.5), channel_id=1, source_target_pairs={{0,2},{1,3},{2,0},{3,1},{4,6},{5,7},{6,4},{7,5},{8,10},{9,11},{10,... | collective-permute-start | bytes 184328 | tf_op jit(solution)/shard_map/ppermute | solution.py:408
  55.9 2.6 %collective-permute-start.13 = (f32[24,128]{1,0:T(8,128)S(1)}, f32[24,128]{1,0:T(8,128)S(1)}, u32[]{:S(2)}, u32[]{:S(2)}) collective-permute-start(f32[24,128]{1,0:T(8,128)S(1)} %slice.28), channel_id=1, source_target_pairs={{0,32},{32,0},{64,96},{96,64},{128,160},{160,128},{192,224},{224,1... | collective-permute-start | bytes 36872 | tf_op jit(solution)/shard_map/ppermute | solution.py:408
  58.5 5.1 %collective-permute-start.14 = (f32[120,128]{1,0:T(8,128)S(1)}, f32[120,128]{1,0:T(8,128)S(1)}, u32[]{:S(2)}, u32[]{:S(2)}) collective-permute-start(f32[120,128]{1,0:T(8,128)S(1)} %pad_maximum_fusion.2), channel_id=1, source_target_pairs={{0,1},{1,0},{2,3},{3,2},{4,5},{5,4},{6,7},{7,6},{8,9},{9,8},{10,11... | collective-permute-start | bytes 184328 | tf_op jit(solution)/shard_map/ppermute | solution.py:408
  62.7 4.0 %collective-permute-start.18 = (f32[160,128]{1,0:T(8,128)S(1)}, f32[160,128]{1,0:T(8,128)S(1)}, u32[]{:S(2)}, u32[]{:S(2)}) collective-permute-start(f32[160,128]{1,0:T(8,128)S(1)} %shard_map.107), channel_id=1, source_target_pairs={{0,32},{32,0},{64,96},{96,64},{128,160},{160,128},{192,224},{224,1... | collective-permute-start | bytes 245768 | tf_op jit(solution)/shard_map/ppermute | solution.py:408
  63.6 4.7 %collective-permute-start.17 = (f32[120,128]{1,0:T(8,128)S(1)}, f32[120,128]{1,0:T(8,128)S(1)}, u32[]{:S(2)}, u32[]{:S(2)}) collective-permute-start(f32[120,128]{1,0:T(8,128)S(1)} %fusion.1), channel_id=1, source_target_pairs={{0,16},{1,17},{2,18},{3,19},{4,20},{5,21},{6,22},{7,23},{8,24},{9,... | collective-permute-start | bytes 184328 | tf_op jit(solution)/shard_map/ppermute | solution.py:408
  64.8 5.3 %collective-permute-start.16 = (f32[120,128]{1,0:T(8,128)S(1)}, f32[120,128]{1,0:T(8,128)S(1)}, u32[]{:S(2)}, u32[]{:S(2)}) collective-permute-start(f32[120,128]{1,0:T(8,128)S(1)} %fusion.1), channel_id=1, source_target_pairs={{0,24},{1,25},{2,26},{3,27},{4,28},{5,29},{6,30},{7,31},{8,16},{9,... | collective-permute-start | bytes 184328 | tf_op jit(solution)/shard_map/ppermute | solution.py:408
  65.9 4.3 %collective-permute-start.15 = (f32[120,128]{1,0:T(8,128)S(1)}, f32[120,128]{1,0:T(8,128)S(1)}, u32[]{:S(2)}, u32[]{:S(2)}) collective-permute-start(f32[120,128]{1,0:T(8,128)S(1)} %fusion.1), channel_id=1, source_target_pairs={{0,8},{1,9},{2,10},{3,11},{4,12},{5,13},{6,14},{7,15},{8,0},{9,1},... | collective-permute-start | bytes 184328 | tf_op jit(solution)/shard_map/ppermute | solution.py:408
  70.2 4.7 %collective-permute-start.21 = (f32[120,128]{1,0:T(8,128)S(1)}, f32[120,128]{1,0:T(8,128)S(1)}, u32[]{:S(2)}, u32[]{:S(2)}) collective-permute-start(f32[120,128]{1,0:T(8,128)S(1)} %add_add_fusion.3), channel_id=1, source_target_pairs={{0,4},{1,5},{2,6},{3,7},{4,0},{5,1},{6,2},{7,3},{8,12},{9,13},{10,... | collective-permute-start | bytes 184328 | tf_op jit(solution)/shard_map/ppermute | solution.py:408
  71.5 5.0 %collective-permute-start.20 = (f32[120,128]{1,0:T(8,128)S(1)}, f32[120,128]{1,0:T(8,128)S(1)}, u32[]{:S(2)}, u32[]{:S(2)}) collective-permute-start(f32[120,128]{1,0:T(8,128)S(1)} %add_add_fusion.3), channel_id=1, source_target_pairs={{0,6},{1,7},{2,4},{3,5},{4,2},{5,3},{6,0},{7,1},{8,14},{9,15},{10,... | collective-permute-start | bytes 184328 | tf_op jit(solution)/shard_map/ppermute | solution.py:408
  72.2 4.3 %collective-permute-start.19 = (f32[120,128]{1,0:T(8,128)S(1)}, f32[120,128]{1,0:T(8,128)S(1)}, u32[]{:S(2)}, u32[]{:S(2)}) collective-permute-start(f32[120,128]{1,0:T(8,128)S(1)} %add_add_fusion.3), channel_id=1, source_target_pairs={{0,2},{1,3},{2,0},{3,1},{4,6},{5,7},{6,4},{7,5},{8,10},{9,11},{10,... | collective-permute-start | bytes 184328 | tf_op jit(solution)/shard_map/ppermute | solution.py:408
  79.9 2.6 %collective-permute-start.22 = (f32[24,128]{1,0:T(8,128)S(1)}, f32[24,128]{1,0:T(8,128)S(1)}, u32[]{:S(2)}, u32[]{:S(2)}) collective-permute-start(f32[24,128]{1,0:T(8,128)S(1)} %slice.30), channel_id=1, source_target_pairs={{0,32},{32,0},{64,96},{96,64},{128,160},{160,128},{192,224},{224,1... | collective-permute-start | bytes 36872 | tf_op jit(solution)/shard_map/ppermute | solution.py:408
  82.6 3.8 %collective-permute-start.23 = (f32[120,128]{1,0:T(8,128)S(1)}, f32[120,128]{1,0:T(8,128)S(1)}, u32[]{:S(2)}, u32[]{:S(2)}) collective-permute-start(f32[120,128]{1,0:T(8,128)S(1)} %pad_maximum_fusion.3), channel_id=1, source_target_pairs={{0,1},{1,0},{2,3},{3,2},{4,5},{5,4},{6,7},{7,6},{8,9},{9,8},{10,11... | collective-permute-start | bytes 184328 | tf_op jit(solution)/shard_map/ppermute | solution.py:408
  85.4 4.0 %collective-permute-start.27 = (f32[160,128]{1,0:T(8,128)S(1)}, f32[160,128]{1,0:T(8,128)S(1)}, u32[]{:S(2)}, u32[]{:S(2)}) collective-permute-start(f32[160,128]{1,0:T(8,128)S(1)} %shard_map.110), channel_id=1, source_target_pairs={{0,32},{32,0},{64,96},{96,64},{128,160},{160,128},{192,224},{224,1... | collective-permute-start | bytes 245768 | tf_op jit(solution)/shard_map/ppermute | solution.py:408
  86.3 4.7 %collective-permute-start.26 = (f32[120,128]{1,0:T(8,128)S(1)}, f32[120,128]{1,0:T(8,128)S(1)}, u32[]{:S(2)}, u32[]{:S(2)}) collective-permute-start(f32[120,128]{1,0:T(8,128)S(1)} %fusion), channel_id=1, source_target_pairs={{0,16},{1,17},{2,18},{3,19},{4,20},{5,21},{6,22},{7,23},{8,24},{9,... | collective-permute-start | bytes 184328 | tf_op jit(solution)/shard_map/ppermute | solution.py:408
  88.3 4.3 %collective-permute-start.25 = (f32[120,128]{1,0:T(8,128)S(1)}, f32[120,128]{1,0:T(8,128)S(1)}, u32[]{:S(2)}, u32[]{:S(2)}) collective-permute-start(f32[120,128]{1,0:T(8,128)S(1)} %fusion), channel_id=1, source_target_pairs={{0,24},{1,25},{2,26},{3,27},{4,28},{5,29},{6,30},{7,31},{8,16},{9,... | collective-permute-start | bytes 184328 | tf_op jit(solution)/shard_map/ppermute | solution.py:408
  89.2 3.4 %collective-permute-start.24 = (f32[120,128]{1,0:T(8,128)S(1)}, f32[120,128]{1,0:T(8,128)S(1)}, u32[]{:S(2)}, u32[]{:S(2)}) collective-permute-start(f32[120,128]{1,0:T(8,128)S(1)} %fusion), channel_id=1, source_target_pairs={{0,8},{1,9},{2,10},{3,11},{4,12},{5,13},{6,14},{7,15},{8,0},{9,1},... | collective-permute-start | bytes 184328 | tf_op jit(solution)/shard_map/ppermute | solution.py:408
  92.6 4.7 %collective-permute-start.30 = (f32[120,128]{1,0:T(8,128)S(1)}, f32[120,128]{1,0:T(8,128)S(1)}, u32[]{:S(2)}, u32[]{:S(2)}) collective-permute-start(f32[120,128]{1,0:T(8,128)S(1)} %add_add_fusion.1), channel_id=1, source_target_pairs={{0,4},{1,5},{2,6},{3,7},{4,0},{5,1},{6,2},{7,3},{8,12},{9,13},{10,... | collective-permute-start | bytes 184328 | tf_op jit(solution)/shard_map/ppermute | solution.py:408
  94.6 4.6 %collective-permute-start.29 = (f32[120,128]{1,0:T(8,128)S(1)}, f32[120,128]{1,0:T(8,128)S(1)}, u32[]{:S(2)}, u32[]{:S(2)}) collective-permute-start(f32[120,128]{1,0:T(8,128)S(1)} %add_add_fusion.1), channel_id=1, source_target_pairs={{0,6},{1,7},{2,4},{3,5},{4,2},{5,3},{6,0},{7,1},{8,14},{9,15},{10,... | collective-permute-start | bytes 184328 | tf_op jit(solution)/shard_map/ppermute | solution.py:408
  95.5 3.8 %collective-permute-start.28 = (f32[120,128]{1,0:T(8,128)S(1)}, f32[120,128]{1,0:T(8,128)S(1)}, u32[]{:S(2)}, u32[]{:S(2)}) collective-permute-start(f32[120,128]{1,0:T(8,128)S(1)} %add_add_fusion.1), channel_id=1, source_target_pairs={{0,2},{1,3},{2,0},{3,1},{4,6},{5,7},{6,4},{7,5},{8,10},{9,11},{10,... | collective-permute-start | bytes 184328 | tf_op jit(solution)/shard_map/ppermute | solution.py:408

commit v4 on v3

--- a/solution.py
+++ b/solution.py
@@ -7,6 +7,7 @@
 from jax.sharding import PartitionSpec as P
 
 ROWS = 2048
+HALF = ROWS // 2
 LO = 128
 MASKS = (0, 2, 4, 6)
 REST = (1,)
@@ -85,7 +86,7 @@
 
 
 def hots_of(data_ref, slot, kinds):
-    places = iota((LO, ROWS), 0).astype(F32).astype(BF16)
+    places = iota((LO, data_ref.shape[2]), 0).astype(F32).astype(BF16)
     hots = []
     for kind in kinds:
         index = data_ref[slot, INDEX + kind : INDEX + kind + 1].astype(jnp.int32)
@@ -196,7 +197,7 @@
 
 
 def start_kernel(blocks_ref, *args):
-    sources, data_ref, scratch = args[:7], args[7], args[8:]
+    sources, halves, scratch = args[:7], args[7:9], args[9:]
     held, semaphore = scratch[:7], scratch[7]
     copies = [
         pltpu.make_async_copy(source, target, semaphore.at[i])
@@ -207,13 +208,16 @@
     for copy in copies:
         copy.wait()
     live = jnp.where(iota((1, ROWS), 1) < 128 * blocks_ref[0, 0], 1.0, 0.0)
-    data_ref[0, STAR : STAR + 5] = held[0][...] * live
-    data_ref[0, ATT : ATT + 12] = held[1][...] * live
-    data_ref[0, CAL : CAL + 1] = held[2][...] * live
-    for which in range(3):
-        data_ref[0, INDEX + which : INDEX + which + 1] = held[4 + which][...].astype(F32)
-    data_ref[0, RIGHT : RIGHT + 1] = held[3][...] * live
-    data_ref[0, RIGHT + 1 :] = jnp.zeros((PACKED - RIGHT - 1, ROWS), F32)
+    for half, data_ref in enumerate(halves):
+        columns = slice(HALF * half, HALF * half + HALF)
+        here = live[:, columns]
+        data_ref[0, STAR : STAR + 5] = held[0][:, columns] * here
+        data_ref[0, ATT : ATT + 12] = held[1][:, columns] * here
+        data_ref[0, CAL : CAL + 1] = held[2][:, columns] * here
+        for which in range(3):
+            data_ref[0, INDEX + which : INDEX + which + 1] = held[4 + which][:, columns].astype(F32)
+        data_ref[0, RIGHT : RIGHT + 1] = held[3][:, columns] * here
+        data_ref[0, RIGHT + 1 :] = jnp.zeros((PACKED - RIGHT - 1, HALF), F32)
 
 
 def clear(refs):
@@ -282,7 +286,19 @@
         out_ref[member : member + 1] = forward(data_ref, slot, hots, (table,)) * inverse
 
 
-def first_kernel(window_ref, data_ref, stars_ref, rest_in_ref, *args):
+def first_taken_kernel(window_ref, data_ref, stars_ref, out_ref, biggest_ref):
+    stars = stars_ref[...]
+    biggest = jnp.max(jnp.max(jnp.abs(stars), axis=1, keepdims=True), axis=0, keepdims=True)
+    biggest = jnp.where(biggest > 0.0, biggest, 1.0)
+    biggest_ref[...] = jnp.broadcast_to(biggest, (8, LO))
+    table = table_of(stars / biggest)
+    for member in range(GROUP):
+        slot = member_of(window_ref[0]) ^ member
+        hots = hots_of(data_ref, slot, (0,))
+        out_ref[member : member + 1] = forward(data_ref, slot, hots, (table,))
+
+
+def first_kernel(window_ref, data_ref, stars_ref, rest_in_ref, taken_ref, biggest_ref, *args):
     rest_ref, grad_ref, row_ref, kept_ref, cal_ref = args
     window = window_ref[0]
     norm, size, _ = get_scalars(rest_in_ref)
@@ -291,14 +307,16 @@
     grad_ref[...] = grad
     keep([inverse, length], kept_ref)
     clear((rest_ref, cal_ref))
-    star_table, cal_table = table_of(grad[:N_S]), table_of(grad[N_S : N_S + N_C])
+    cal_table = table_of(grad[N_S : N_S + N_C])
+    share = biggest_ref[0:1, 0:1] * inverse / length
     for member in range(GROUP):
         slot = member_of(window) ^ member
-        hots = hots_of(data_ref, slot, (0, 1, 2))
-        tables = (star_table, knot_table(grad_ref, window, member), cal_table)
-        row = forward(data_ref, slot, hots, tables) * inverse
-        row_ref[member : member + 1] = row
-        add_sums(data_ref, slot, hots[1:], row * inverse, window, member, rest_ref, cal_ref)
+        own = slice(member, member + 1)
+        hots = hots_of(data_ref, slot, (1, 2))
+        tables = (knot_table(grad_ref, window, member), cal_table)
+        row = (taken_ref[own] * share + forward(data_ref, slot, hots, tables)) * inverse
+        row_ref[own] = row
+        add_sums(data_ref, slot, hots, row * inverse, window, member, rest_ref, cal_ref)
     rest_ref[:N_C] = fold(cal_ref[...])
     row = row_ref[...]
     set_scalars(rest_ref, [square(grad), total(row * row)])
@@ -415,22 +433,27 @@
     return (value + arrived[0]) + (arrived[1] + arrived[2])
 
 
-def share(data):
-    near, wrap = swap(data, TM, 2), swap(data, TM, 6)
-    half = ROWS // 2
-    far = [swap(wrap[..., :half], TM, 2), swap(near[..., half:], TM, 6)]
-    return jnp.concatenate([data, near, jnp.concatenate(far, axis=2), wrap], axis=0)
-
-
-def reduce(rest, add_stars, take_stars=None):
+def share(left, right):
+    near_right, wrap_left = swap(right, TM, 2), swap(left, TM, 6)
+    near_left, wrap_right = swap(left, TM, 2), swap(right, TM, 6)
+    far_left, far_right = swap(wrap_left, TM, 2), swap(near_right, TM, 6)
+    return (
+        (left, right),
+        (near_left, near_right),
+        (far_left, far_right),
+        (wrap_left, wrap_right),
+    )
+
+
+def reduce(rest, add_stars, take_stars):
     bounded = add_swapped(rest[: N_C + N_B], TM, REST)
     bounded, stars = lax.optimization_barrier((bounded, add_stars()))
     stars = add_swapped(stars, TM, REST)
     rest = jnp.concatenate([bounded, rest[N_C + N_B :]], axis=0)
     rest = add_swapped(add_swapped(rest, "star", (1,)), "star", (8, 24, 16))
     rest, stars = lax.optimization_barrier((rest, stars))
-    taken = () if take_stars is None else (take_stars(stars),)
-    return (stars, add_swapped(rest, "star", (2, 6, 4))) + taken
+    taken = take_stars(stars)
+    return [stars, add_swapped(rest, "star", (2, 6, 4)), *taken]
 
 
 def shards(star_coef, att_coef, cal_coef, observed, star_index, knot_index, cal_index, valid_blocks):
@@ -447,35 +470,38 @@
     vec_shape, small, row_shape = (N_ALL, LO), (8, LO), (GROUP, ROWS)
     rest_shape = (N_ALL - N_S, LO)
     star_scratch, cal_scratch = [pltpu.VMEM((2 * N_S, LO), F32)], [pltpu.VMEM((2 * N_C, LO), F32)]
-    (data,) = call(
+    halves = call(
         start_kernel,
         (valid_blocks,),
         arrays,
-        ((1, PACKED, ROWS),),
+        ((1, PACKED, HALF),) * 2,
         [pltpu.VMEM(item.shape, item.dtype) for item in arrays] + [pltpu.SemaphoreType.DMA((7,))],
         pltpu.HBM,
         60,
     )
-    data = share(data)
+    shared = share(*halves)
+    data = jnp.concatenate([jnp.concatenate(pair, axis=2) for pair in shared], axis=0)
 
     def star_sums(row, kept_scalars):
         return call(stars_kernel, (window,), (data, row, kept_scalars), ((N_S, LO),), star_scratch)[0]
 
     def taken(stars, kept_scalars):
-        return call(taken_kernel, (window,), (data, stars, kept_scalars), (row_shape,))[0]
+        return call(taken_kernel, (window,), (data, stars, kept_scalars), (row_shape,))
 
     (rest,) = call(right_kernel, (window,), (data,), (rest_shape,), cal_scratch)
     arrived = reduce(
-        rest, lambda: call(right_stars_kernel, (window,), (data,), ((N_S, LO),), star_scratch)[0]
+        rest,
+        lambda: call(right_stars_kernel, (window,), (data,), ((N_S, LO),), star_scratch)[0],
+        lambda stars: call(first_taken_kernel, (window,), (data, stars), (row_shape, small)),
     )
     rest, grad0, row0, scalars0 = call(
-        first_kernel, (window,), (data,) + arrived, (rest_shape, vec_shape, row_shape, small), cal_scratch
+        first_kernel, (window,), [data] + arrived, (rest_shape, vec_shape, row_shape, small), cal_scratch
     )
     arrived = reduce(rest, lambda: star_sums(row0, scalars0), lambda stars: taken(stars, scalars0))
     rest, grad1, image0, mapped0, row1, scalars1 = call(
         second_kernel,
         (window,),
-        (data,) + arrived + (grad0, row0, scalars0),
+        [data] + arrived + [grad0, row0, scalars0],
         (rest_shape, vec_shape, vec_shape, row_shape, row_shape, small),
         cal_scratch,
     )
@@ -483,7 +509,7 @@
     grad2, x, direction, scalars, partial = call(
         third_kernel,
         (window,),
-        (data,) + arrived + (grad0, grad1, image0, mapped0, row0, row1, scalars1),
+        [data] + arrived + [grad0, grad1, image0, mapped0, row0, row1, scalars1],
         (vec_shape, vec_shape, vec_shape, small, (1, LO)),
         [pltpu.VMEM(row_shape, F32), pltpu.VMEM(vec_shape, F32)],
     )

time: 118 us -> 117 us (level)
  waiting for transfers between devices: 32.2 us -> 30.6 us
    ppermute x31 -> x33, waiting for transfers between devices: 32.2 us -> 30.6 us  [swap(): return lax.ppermute(value, axis, [(i, i ^ bits) for i in range(count)])]
    ppermute x31 -> x33, starting transfers between devices: 47.5 us -> 46.4 us  [swap(): return lax.ppermute(value, axis, [(i, i ^ bits) for i in range(count)])]
    pallas_call x11 -> x12, Pallas kernels: 20.4 us -> 20.6 us  [call(): pl.pallas_call(kernel, out_shape=[jax.ShapeDtypeStruct(shape, F32) for sh...]
  transfers between devices with their start and end apart: 31 -> 33, of which waited for: 20 -> 24; matrix products, arithmetic and copies ran while one was open for 0% -> 0% of each run, Pallas kernels for 6% -> 6%
where the time goes in v4:
time: 117 us; the launch traced here: 116 us
  starting transfers between devices  46.4 us (40%)
  waiting for transfers between devices  30.6 us (26%)
  Pallas kernels  20.6 us (18%)
  blocking collectives  16.1 us (14%)
  between operations  1.45 us (1%)
  other arithmetic  1.2 us (1%)
    ppermute x33, starting transfers between devices, swap(): return lax.ppermute(value, axis, [(i, i ^ bits) for i in range(count)])  46.4 us
    ppermute x33, waiting for transfers between devices, swap(): return lax.ppermute(value, axis, [(i, i ^ bits) for i in range(count)])  30.6 us
    pallas_call x12, Pallas kernels, call(): pl.pallas_call(kernel, out_shape=[jax.ShapeDtypeStruct(shape, F32) for sh...  20.6 us
    all_to_all x1, blocking collectives, shards(): lax.all_to_all(jnp.broadcast_to(partial[None], (count, 1, LO)), axes, 0, 0)  16.1 us
  transfers between devices with their start and end apart: 33, of which 24 were waited for; matrix products, arithmetic and copies ran while one was open for 0% of the time, Pallas kernels for 6%

profile of v4, /device:TPU:1, one launch (start us, length us, event | category | flops | bytes accessed | tf_op | source)
XLA Modules:
  0.0 116.4 jit_solution(9474407284861637795)
XLA Ops:
  1.3 1.7 %shard_map.103 = (f32[1,24,1024]{2,1,0:T(8,128)}, f32[1,24,1024]{2,1,0:T(8,128)}) custom-call(s32[1,1]{1,0:T(1,128)S(6)} %copy.11.blocks_ref, f32[5,2048]{1,0:T(8,128)} %args_0_.4, f32[12,2048]{1,0:T(8,128)} %args_1_.4, f32[1,2048]{1,0:T(1,128)} %bitcast.11, f32[1,2048]{1,0:T(1,128)} %bitcast.12, s32[1,2048]{1,0:T(1,128)} %bitcast.13, s32[1,2048]{1,0:T(1,128)} %bitcast.14, ...), custom_call_target="tpu_custom_call" | custom-call | flops 1500000000 | bytes 1000000 | tf_op jit(solution)/shard_map/pallas_call | solution.py:412
  3.0 6.9 %collective-permute-start.2 = (f32[1,24,1024]{2,1,0:T(8,128)}, f32[1,24,1024]{2,1,0:T(8,128)S(1)}, u32[]{:S(2)}, u32[]{:S(2)}) collective-permute-start(f32[1,24,1024]{2,1,0:T(8,128)} %get-tuple-element.37), channel_id=1, source_target_pairs={{0,192},{32,224},{64,128},{96,160},{128,64},{160,96},{192,0},{224,... | collective-permute-start | bytes 294920 | tf_op jit(solution)/shard_map/ppermute | solution.py:426
  9.9 1.2 %collective-permute-start.1 = (f32[1,24,1024]{2,1,0:T(8,128)}, f32[1,24,1024]{2,1,0:T(8,128)S(1)}, u32[]{:S(2)}, u32[]{:S(2)}) collective-permute-start(f32[1,24,1024]{2,1,0:T(8,128)} %get-tuple-element.38), channel_id=1, source_target_pairs={{0,64},{32,96},{64,0},{96,32},{128,192},{160,224},{192,128},{224,1... | collective-permute-start | bytes 294920 | tf_op jit(solution)/shard_map/ppermute | solution.py:426
  11.1 1.2 %collective-permute-start = (f32[1,24,1024]{2,1,0:T(8,128)}, f32[1,24,1024]{2,1,0:T(8,128)S(1)}, u32[]{:S(2)}, u32[]{:S(2)}) collective-permute-start(f32[1,24,1024]{2,1,0:T(8,128)} %get-tuple-element.37), channel_id=1, source_target_pairs={{0,64},{32,96},{64,0},{96,32},{128,192},{160,224},{192,128},{224,1... | collective-permute-start | bytes 294920 | tf_op jit(solution)/shard_map/ppermute | solution.py:426
  12.4 1.8 %collective-permute-done.2 = f32[1,24,1024]{2,1,0:T(8,128)S(1)} collective-permute-done((f32[1,24,1024]{2,1,0:T(8,128)}, f32[1,24,1024]{2,1,0:T(8,128)S(1)}, u32[]{:S(2)}, u32[]{:S(2)}) %collective-permute-start.2) | collective-permute-done | bytes 98336 | tf_op jit(solution)/shard_map/ppermute | solution.py:426
  14.2 1.2 %collective-permute-start.3 = (f32[1,24,1024]{2,1,0:T(8,128)S(1)}, f32[1,24,1024]{2,1,0:T(8,128)S(1)}, u32[]{:S(2)}, u32[]{:S(2)}) collective-permute-start(f32[1,24,1024]{2,1,0:T(8,128)S(1)} %collective-permute-done.2), channel_id=1, source_target_pairs={{0,64},{32,96},{64,0},{96,32},{128,192},{160,224},{192,128},{224,1... | collective-permute-start | bytes 294920 | tf_op jit(solution)/shard_map/ppermute | solution.py:426
  15.3 3.2 %collective-permute-start.4 = (f32[1,24,1024]{2,1,0:T(8,128)S(1)}, f32[1,24,1024]{2,1,0:T(8,128)S(1)}, u32[]{:S(2)}, u32[]{:S(2)}) collective-permute-start(f32[1,24,1024]{2,1,0:T(8,128)S(1)} %collective-permute-done.1), channel_id=1, source_target_pairs={{0,192},{32,224},{64,128},{96,160},{128,64},{160,96},{192,0},{224,... | collective-permute-start | bytes 294920 | tf_op jit(solution)/shard_map/ppermute | solution.py:426
  18.5 2.8 %collective-permute-done = f32[1,24,1024]{2,1,0:T(8,128)S(1)} collective-permute-done((f32[1,24,1024]{2,1,0:T(8,128)}, f32[1,24,1024]{2,1,0:T(8,128)S(1)}, u32[]{:S(2)}, u32[]{:S(2)}) %collective-permute-start) | collective-permute-done | bytes 98336 | tf_op jit(solution)/shard_map/ppermute | solution.py:426
  21.3 0.7 collective-permute-done.5
  22.0 3.4 %collective-permute-done.3 = f32[1,24,1024]{2,1,0:T(8,128)S(1)} collective-permute-done((f32[1,24,1024]{2,1,0:T(8,128)S(1)}, f32[1,24,1024]{2,1,0:T(8,128)S(1)}, u32[]{:S(2)}, u32[]{:S(2)}) %collective-permute-start.3) | collective-permute-done | bytes 98336 | tf_op jit(solution)/shard_map/ppermute | solution.py:426
  25.4 1.0 maximum_maximum_fusion.data_ref
  26.4 1.9 %shard_map.104 = f32[120,128]{1,0:T(8,128)S(1)} custom-call(s32[1]{0:T(128)} %bitcast.window_ref, f32[4,24,2048]{2,1,0:T(8,128)S(1)} %maximum_maximum_fusion.data_ref), custom_call_target="tpu_custom_call" | custom-call | flops 1500000000 | bytes 1000000 | tf_op jit(solution)/shard_map/pallas_call | solution.py:412
  28.4 1.5 %shard_map.105 = f32[160,128]{1,0:T(8,128)S(1)} custom-call(s32[1]{0:T(128)} %bitcast.window_ref, f32[4,24,2048]{2,1,0:T(8,128)S(1)} %maximum_maximum_fusion.data_ref), custom_call_target="tpu_custom_call" | custom-call | flops 1500000000 | bytes 1000000 | tf_op jit(solution)/shard_map/pallas_call | solution.py:412
  30.0 1.0 collective-permute-done.6
  31.0 4.1 %collective-permute-start.7 = (f32[120,128]{1,0:T(8,128)S(1)}, f32[120,128]{1,0:T(8,128)S(1)}, u32[]{:S(2)}, u32[]{:S(2)}) collective-permute-start(f32[120,128]{1,0:T(8,128)S(1)} %pad_maximum_fusion), channel_id=1, source_target_pairs={{0,1},{1,0},{2,3},{3,2},{4,5},{5,4},{6,7},{7,6},{8,9},{9,8},{10,11... | collective-permute-start | bytes 184328 | tf_op jit(solution)/shard_map/ppermute | solution.py:426
  35.1 0.9 collective-permute-done.7
  36.0 2.8 %collective-permute-start.10 = (f32[120,128]{1,0:T(8,128)S(1)}, f32[120,128]{1,0:T(8,128)S(1)}, u32[]{:S(2)}, u32[]{:S(2)}) collective-permute-start(f32[120,128]{1,0:T(8,128)S(1)} %fusion.2), channel_id=1, source_target_pairs={{0,16},{1,17},{2,18},{3,19},{4,20},{5,21},{6,22},{7,23},{8,24},{9,... | collective-permute-start | bytes 184328 | tf_op jit(solution)/shard_map/ppermute | solution.py:426
  38.9 0.9 collective-permute-start.9
  39.7 1.0 collective-permute-done.10
  40.7 2.4 %collective-permute-done.9 = f32[120,128]{1,0:T(8,128)S(1)} collective-permute-done((f32[120,128]{1,0:T(8,128)S(1)}, f32[120,128]{1,0:T(8,128)S(1)}, u32[]{:S(2)}, u32[]{:S(2)}) %collective-permute-start.9) | collective-permute-done | bytes 61472 | tf_op jit(solution)/shard_map/ppermute | solution.py:426
  43.2 3.0 %collective-permute-start.14 = (f32[120,128]{1,0:T(8,128)S(1)}, f32[120,128]{1,0:T(8,128)S(1)}, u32[]{:S(2)}, u32[]{:S(2)}) collective-permute-start(f32[120,128]{1,0:T(8,128)S(1)} %add_add_fusion.5), channel_id=1, source_target_pairs={{0,4},{1,5},{2,6},{3,7},{4,0},{5,1},{6,2},{7,3},{8,12},{9,13},{10,... | collective-permute-start | bytes 184328 | tf_op jit(solution)/shard_map/ppermute | solution.py:426
  46.2 0.8 collective-permute-start.13
  46.9 1.0 shard_map.106
  48.0 2.8 %collective-permute-done.13 = f32[120,128]{1,0:T(8,128)S(1)} collective-permute-done((f32[120,128]{1,0:T(8,128)S(1)}, f32[120,128]{1,0:T(8,128)S(1)}, u32[]{:S(2)}, u32[]{:S(2)}) %collective-permute-start.13) | collective-permute-done | bytes 61472 | tf_op jit(solution)/shard_map/ppermute | solution.py:426
  50.8 3.4 %shard_map.107 = (f32[120,128]{1,0:T(8,128)S(1)}, f32[280,128]{1,0:T(8,128)S(1)}, f32[4,2048]{1,0:T(4,128)S(1)}, f32[8,128]{1,0:T(8,128)S(1)}) custom-call(s32[1]{0:T(128)} %bitcast.window_ref, f32[4,24,2048]{2,1,0:T(8,128)S(1)} %maximum_maximum_fusion.data_ref, f32[160,128]{1,0:T(8,128)S(1)} %add.90.stars_ref, f32[120,128]{1,0:T(8,128)S(1)} %add_add_fusion.4.rest_in_ref, ...), custom_call_target="tpu_custom_call" | custom-call | flops 1500000000 | bytes 1000000 | tf_op jit(solution)/shard_map/pallas_call | solution.py:412
  54.2 0.7 collective-permute-start.15
  54.9 1.6 %shard_map.108 = f32[160,128]{1,0:T(8,128)S(1)} custom-call(s32[1]{0:T(128)} %bitcast.window_ref, f32[4,24,2048]{2,1,0:T(8,128)S(1)} %maximum_maximum_fusion.data_ref, f32[4,2048]{1,0:T(4,128)S(1)} %get-tuple-element.46.row_ref.args_4_.args_7_, f32[8,128]{1,0:T(8,128)S(1)} %get-tuple-element.47.kept_ref.args_5_), custom_call_target="tpu_custom_call" | custom-call | flops 1500000000 | bytes 1000000 | tf_op jit(solution)/shard_map/pallas_call | solution.py:412
  56.5 0.4 collective-permute-done.15
  56.8 4.2 %collective-permute-start.16 = (f32[120,128]{1,0:T(8,128)S(1)}, f32[120,128]{1,0:T(8,128)S(1)}, u32[]{:S(2)}, u32[]{:S(2)}) collective-permute-start(f32[120,128]{1,0:T(8,128)S(1)} %pad_maximum_fusion.1), channel_id=1, source_target_pairs={{0,1},{1,0},{2,3},{3,2},{4,5},{5,4},{6,7},{7,6},{8,9},{9,8},{10,11... | collective-permute-start | bytes 184328 | tf_op jit(solution)/shard_map/ppermute | solution.py:426
  61.0 0.6 collective-permute-start.20
  61.6 0.3 collective-permute-done.16
  61.9 1.3 %collective-permute-start.19 = (f32[120,128]{1,0:T(8,128)S(1)}, f32[120,128]{1,0:T(8,128)S(1)}, u32[]{:S(2)}, u32[]{:S(2)}) collective-permute-start(f32[120,128]{1,0:T(8,128)S(1)} %fusion.1), channel_id=1, source_target_pairs={{0,16},{1,17},{2,18},{3,19},{4,20},{5,21},{6,22},{7,23},{8,24},{9,... | collective-permute-start | bytes 184328 | tf_op jit(solution)/shard_map/ppermute | solution.py:426
  63.2 1.0 collective-permute-start.18
  64.2 0.4 collective-permute-start.17
  64.7 0.4 collective-permute-done.20
  65.0 1.5 %collective-permute-done.19 = f32[120,128]{1,0:T(8,128)S(1)} collective-permute-done((f32[120,128]{1,0:T(8,128)S(1)}, f32[120,128]{1,0:T(8,128)S(1)}, u32[]{:S(2)}, u32[]{:S(2)}) %collective-permute-start.19) | collective-permute-done | bytes 61472 | tf_op jit(solution)/shard_map/ppermute | solution.py:426
  66.6 1.9 %collective-permute-done.18 = f32[120,128]{1,0:T(8,128)S(1)} collective-permute-done((f32[120,128]{1,0:T(8,128)S(1)}, f32[120,128]{1,0:T(8,128)S(1)}, u32[]{:S(2)}, u32[]{:S(2)}) %collective-permute-start.18) | collective-permute-done | bytes 61472 | tf_op jit(solution)/shard_map/ppermute | solution.py:426
  68.5 1.3 %collective-permute-start.23 = (f32[120,128]{1,0:T(8,128)S(1)}, f32[120,128]{1,0:T(8,128)S(1)}, u32[]{:S(2)}, u32[]{:S(2)}) collective-permute-start(f32[120,128]{1,0:T(8,128)S(1)} %add_add_fusion.3), channel_id=1, source_target_pairs={{0,4},{1,5},{2,6},{3,7},{4,0},{5,1},{6,2},{7,3},{8,12},{9,13},{10,... | collective-permute-start | bytes 184328 | tf_op jit(solution)/shard_map/ppermute | solution.py:426
  69.9 0.7 collective-permute-start.22
  70.6 0.7 collective-permute-start.21
  71.2 1.0 shard_map.109.args_2_
  72.2 1.0 collective-permute-done.23
  73.2 1.7 %collective-permute-done.22 = f32[120,128]{1,0:T(8,128)S(1)} collective-permute-done((f32[120,128]{1,0:T(8,128)S(1)}, f32[120,128]{1,0:T(8,128)S(1)}, u32[]{:S(2)}, u32[]{:S(2)}) %collective-permute-start.22) | collective-permute-done | bytes 61472 | tf_op jit(solution)/shard_map/ppermute | solution.py:426
  74.9 3.4 %shard_map.110 = (f32[120,128]{1,0:T(8,128)S(1)}, f32[280,128]{1,0:T(8,128)S(1)}, f32[280,128]{1,0:T(8,128)S(1)}, f32[4,2048]{1,0:T(4,128)S(1)}, f32[4,2048]{1,0:T(4,128)S(1)}, /*index=5*/f32[8,128]{1,0:T(8,128)S(1)}) custom-call(s32[1]{0:T(128)} %bitcast.window_ref, f32[4,24,2048]{2,1,0:T(8,128)S(1)} %maximum_maximum_fusion.data_ref, ...), custom_call_target="tpu_custom_call" | custom-call | flops 1500000000 | bytes 1000000 | tf_op jit(solution)/shard_map/pallas_call | solution.py:412
  78.2 0.7 collective-permute-start.24
  78.9 1.6 %shard_map.111 = f32[160,128]{1,0:T(8,128)S(1)} custom-call(s32[1]{0:T(128)} %bitcast.window_ref, f32[4,24,2048]{2,1,0:T(8,128)S(1)} %maximum_maximum_fusion.data_ref, f32[4,2048]{1,0:T(4,128)S(1)} %get-tuple-element.54.row_ref.args_8_, f32[8,128]{1,0:T(8,128)S(1)} %get-tuple-element.55.kept_ref.args_9_), custom_call_target="tpu_custom_call" | custom-call | flops 1500000000 | bytes 1000000 | tf_op jit(solution)/shard_map/pallas_call | solution.py:412
  80.5 0.4 collective-permute-done.24
  80.9 2.9 %collective-permute-start.25 = (f32[120,128]{1,0:T(8,128)S(1)}, f32[120,128]{1,0:T(8,128)S(1)}, u32[]{:S(2)}, u32[]{:S(2)}) collective-permute-start(f32[120,128]{1,0:T(8,128)S(1)} %pad_maximum_fusion.2), channel_id=1, source_target_pairs={{0,1},{1,0},{2,3},{3,2},{4,5},{5,4},{6,7},{7,6},{8,9},{9,8},{10,11... | collective-permute-start | bytes 184328 | tf_op jit(solution)/shard_map/ppermute | solution.py:426
  83.8 0.6 collective-permute-start.29
  84.4 0.3 collective-permute-done.25
  84.7 1.9 %collective-permute-start.28 = (f32[120,128]{1,0:T(8,128)S(1)}, f32[120,128]{1,0:T(8,128)S(1)}, u32[]{:S(2)}, u32[]{:S(2)}) collective-permute-start(f32[120,128]{1,0:T(8,128)S(1)} %fusion), channel_id=1, source_target_pairs={{0,16},{1,17},{2,18},{3,19},{4,20},{5,21},{6,22},{7,23},{8,24},{9,... | collective-permute-start | bytes 184328 | tf_op jit(solution)/shard_map/ppermute | solution.py:426
  86.6 0.9 collective-permute-start.27
  87.5 0.2 collective-permute-done.29
  87.8 1.5 %collective-permute-done.28 = f32[120,128]{1,0:T(8,128)S(1)} collective-permute-done((f32[120,128]{1,0:T(8,128)S(1)}, f32[120,128]{1,0:T(8,128)S(1)}, u32[]{:S(2)}, u32[]{:S(2)}) %collective-permute-start.28) | collective-permute-done | bytes 61472 | tf_op jit(solution)/shard_map/ppermute | solution.py:426
  89.3 1.5 %collective-permute-done.27 = f32[120,128]{1,0:T(8,128)S(1)} collective-permute-done((f32[120,128]{1,0:T(8,128)S(1)}, f32[120,128]{1,0:T(8,128)S(1)}, u32[]{:S(2)}, u32[]{:S(2)}) %collective-permute-start.27) | collective-permute-done | bytes 61472 | tf_op jit(solution)/shard_map/ppermute | solution.py:426
  90.9 2.0 %collective-permute-start.32 = (f32[120,128]{1,0:T(8,128)S(1)}, f32[120,128]{1,0:T(8,128)S(1)}, u32[]{:S(2)}, u32[]{:S(2)}) collective-permute-start(f32[120,128]{1,0:T(8,128)S(1)} %add_add_fusion.1), channel_id=1, source_target_pairs={{0,4},{1,5},{2,6},{3,7},{4,0},{5,1},{6,2},{7,3},{8,12},{9,13},{10,... | collective-permute-start | bytes 184328 | tf_op jit(solution)/shard_map/ppermute | solution.py:426
  92.9 0.9 collective-permute-start.31
  93.8 1.0 shard_map.112.args_2_
  94.8 0.8 collective-permute-done.32
  95.6 1.9 %collective-permute-done.31 = f32[120,128]{1,0:T(8,128)S(1)} collective-permute-done((f32[120,128]{1,0:T(8,128)S(1)}, f32[120,128]{1,0:T(8,128)S(1)}, u32[]{:S(2)}, u32[]{:S(2)}) %collective-permute-start.31) | collective-permute-done | bytes 61472 | tf_op jit(solution)/shard_map/ppermute | solution.py:426
  97.5 0.1 collective-permute-done.30
  97.6 1.7 %shard_map.113 = (f32[280,128]{1,0:T(8,128)S(1)}, f32[280,128]{1,0:T(8,128)S(1)}, f32[280,128]{1,0:T(8,128)S(1)}, f32[8,128]{1,0:T(8,128)S(1)}, f32[1,128]{1,0:T(1,128)S(1)}) custom-call(s32[1]{0:T(128)} %bitcast.window_ref, f32[4,24,2048]{2,1,0:T(8,128)S(1)} %maximum_maximum_fusion.data_ref, f32[160,128]{1,0:T(8,128)S(1)} %add.108.stars_ref.args_0_, ...), custom_call_target="tpu_custom_call" | custom-call | flops 1500000000 | bytes 1000000 | tf_op jit(solution)/shard_map/pallas_call | solution.py:412
  99.3 16.1 %all_to_all.5 = f32[64,1,128]{2,1,0:T(1,128)S(1)} all-to-all(f32[64,1,128]{2,1,0:T(1,128)S(1)} %broadcast_in_dim.9), channel_id=1, replica_groups=mesh['tm_high'=4,'tm_low'=2,'star'=32] {'tm_low','star'}, dimensions={0} | all-to-all | bytes 65536 | tf_op jit(solution)/shard_map/all_to_all | solution.py:518
  115.4 1.0 shard_map.114
  (41 shorter events, 0.5 us)
Async XLA Ops:
  3.0 11.2 %collective-permute-start.2 = (f32[1,24,1024]{2,1,0:T(8,128)}, f32[1,24,1024]{2,1,0:T(8,128)S(1)}, u32[]{:S(2)}, u32[]{:S(2)}) collective-permute-start(f32[1,24,1024]{2,1,0:T(8,128)} %get-tuple-element.37), channel_id=1, source_target_pairs={{0,192},{32,224},{64,128},{96,160},{128,64},{160,96},{192,0},{224,... | collective-permute-start | bytes 294920 | tf_op jit(solution)/shard_map/ppermute | solution.py:426
  9.9 5.4 %collective-permute-start.1 = (f32[1,24,1024]{2,1,0:T(8,128)}, f32[1,24,1024]{2,1,0:T(8,128)S(1)}, u32[]{:S(2)}, u32[]{:S(2)}) collective-permute-start(f32[1,24,1024]{2,1,0:T(8,128)} %get-tuple-element.38), channel_id=1, source_target_pairs={{0,64},{32,96},{64,0},{96,32},{128,192},{160,224},{192,128},{224,1... | collective-permute-start | bytes 294920 | tf_op jit(solution)/shard_map/ppermute | solution.py:426
  11.1 10.2 %collective-permute-start = (f32[1,24,1024]{2,1,0:T(8,128)}, f32[1,24,1024]{2,1,0:T(8,128)S(1)}, u32[]{:S(2)}, u32[]{:S(2)}) collective-permute-start(f32[1,24,1024]{2,1,0:T(8,128)} %get-tuple-element.37), channel_id=1, source_target_pairs={{0,64},{32,96},{64,0},{96,32},{128,192},{160,224},{192,128},{224,1... | collective-permute-start | bytes 294920 | tf_op jit(solution)/shard_map/ppermute | solution.py:426
  12.3 9.7 %collective-permute-start.5 = (f32[1,24,1024]{2,1,0:T(8,128)}, f32[1,24,1024]{2,1,0:T(8,128)S(1)}, u32[]{:S(2)}, u32[]{:S(2)}) collective-permute-start(f32[1,24,1024]{2,1,0:T(8,128)} %get-tuple-element.38), channel_id=1, source_target_pairs={{0,192},{32,224},{64,128},{96,160},{128,64},{160,96},{192,0},{224,... | collective-permute-start | bytes 294920 | tf_op jit(solution)/shard_map/ppermute | solution.py:426
  14.2 11.2 %collective-permute-start.3 = (f32[1,24,1024]{2,1,0:T(8,128)S(1)}, f32[1,24,1024]{2,1,0:T(8,128)S(1)}, u32[]{:S(2)}, u32[]{:S(2)}) collective-permute-start(f32[1,24,1024]{2,1,0:T(8,128)S(1)} %collective-permute-done.2), channel_id=1, source_target_pairs={{0,64},{32,96},{64,0},{96,32},{128,192},{160,224},{192,128},{224,1... | collective-permute-start | bytes 294920 | tf_op jit(solution)/shard_map/ppermute | solution.py:426
  15.3 10.1 %collective-permute-start.4 = (f32[1,24,1024]{2,1,0:T(8,128)S(1)}, f32[1,24,1024]{2,1,0:T(8,128)S(1)}, u32[]{:S(2)}, u32[]{:S(2)}) collective-permute-start(f32[1,24,1024]{2,1,0:T(8,128)S(1)} %collective-permute-done.1), channel_id=1, source_target_pairs={{0,192},{32,224},{64,128},{96,160},{128,64},{160,96},{192,0},{224,... | collective-permute-start | bytes 294920 | tf_op jit(solution)/shard_map/ppermute | solution.py:426
  28.3 2.6 %collective-permute-start.6 = (f32[24,128]{1,0:T(8,128)S(1)}, f32[24,128]{1,0:T(8,128)S(1)}, u32[]{:S(2)}, u32[]{:S(2)}) collective-permute-start(f32[24,128]{1,0:T(8,128)S(1)} %slice.24), channel_id=1, source_target_pairs={{0,32},{32,0},{64,96},{96,64},{128,160},{160,128},{192,224},{224,1... | collective-permute-start | bytes 36872 | tf_op jit(solution)/shard_map/ppermute | solution.py:426
  31.0 5.0 %collective-permute-start.7 = (f32[120,128]{1,0:T(8,128)S(1)}, f32[120,128]{1,0:T(8,128)S(1)}, u32[]{:S(2)}, u32[]{:S(2)}) collective-permute-start(f32[120,128]{1,0:T(8,128)S(1)} %pad_maximum_fusion), channel_id=1, source_target_pairs={{0,1},{1,0},{2,3},{3,2},{4,5},{5,4},{6,7},{7,6},{8,9},{9,8},{10,11... | collective-permute-start | bytes 184328 | tf_op jit(solution)/shard_map/ppermute | solution.py:426
  35.1 4.6 %collective-permute-start.11 = (f32[160,128]{1,0:T(8,128)S(1)}, f32[160,128]{1,0:T(8,128)S(1)}, u32[]{:S(2)}, u32[]{:S(2)}) collective-permute-start(f32[160,128]{1,0:T(8,128)S(1)} %shard_map.105), channel_id=1, source_target_pairs={{0,32},{32,0},{64,96},{96,64},{128,160},{160,128},{192,224},{224,1... | collective-permute-start | bytes 245768 | tf_op jit(solution)/shard_map/ppermute | solution.py:426
  36.0 4.7 %collective-permute-start.10 = (f32[120,128]{1,0:T(8,128)S(1)}, f32[120,128]{1,0:T(8,128)S(1)}, u32[]{:S(2)}, u32[]{:S(2)}) collective-permute-start(f32[120,128]{1,0:T(8,128)S(1)} %fusion.2), channel_id=1, source_target_pairs={{0,16},{1,17},{2,18},{3,19},{4,20},{5,21},{6,22},{7,23},{8,24},{9,... | collective-permute-start | bytes 184328 | tf_op jit(solution)/shard_map/ppermute | solution.py:426
  38.9 4.3 %collective-permute-start.9 = (f32[120,128]{1,0:T(8,128)S(1)}, f32[120,128]{1,0:T(8,128)S(1)}, u32[]{:S(2)}, u32[]{:S(2)}) collective-permute-start(f32[120,128]{1,0:T(8,128)S(1)} %fusion.2), channel_id=1, source_target_pairs={{0,24},{1,25},{2,26},{3,27},{4,28},{5,29},{6,30},{7,31},{8,16},{9,... | collective-permute-start | bytes 184328 | tf_op jit(solution)/shard_map/ppermute | solution.py:426
  39.7 3.4 %collective-permute-start.8 = (f32[120,128]{1,0:T(8,128)S(1)}, f32[120,128]{1,0:T(8,128)S(1)}, u32[]{:S(2)}, u32[]{:S(2)}) collective-permute-start(f32[120,128]{1,0:T(8,128)S(1)} %fusion.2), channel_id=1, source_target_pairs={{0,8},{1,9},{2,10},{3,11},{4,12},{5,13},{6,14},{7,15},{8,0},{9,1},... | collective-permute-start | bytes 184328 | tf_op jit(solution)/shard_map/ppermute | solution.py:426
  43.2 4.8 %collective-permute-start.14 = (f32[120,128]{1,0:T(8,128)S(1)}, f32[120,128]{1,0:T(8,128)S(1)}, u32[]{:S(2)}, u32[]{:S(2)}) collective-permute-start(f32[120,128]{1,0:T(8,128)S(1)} %add_add_fusion.5), channel_id=1, source_target_pairs={{0,4},{1,5},{2,6},{3,7},{4,0},{5,1},{6,2},{7,3},{8,12},{9,13},{10,... | collective-permute-start | bytes 184328 | tf_op jit(solution)/shard_map/ppermute | solution.py:426
  46.2 4.6 %collective-permute-start.13 = (f32[120,128]{1,0:T(8,128)S(1)}, f32[120,128]{1,0:T(8,128)S(1)}, u32[]{:S(2)}, u32[]{:S(2)}) collective-permute-start(f32[120,128]{1,0:T(8,128)S(1)} %add_add_fusion.5), channel_id=1, source_target_pairs={{0,6},{1,7},{2,4},{3,5},{4,2},{5,3},{6,0},{7,1},{8,14},{9,15},{10,... | collective-permute-start | bytes 184328 | tf_op jit(solution)/shard_map/ppermute | solution.py:426
  46.9 3.8 %collective-permute-start.12 = (f32[120,128]{1,0:T(8,128)S(1)}, f32[120,128]{1,0:T(8,128)S(1)}, u32[]{:S(2)}, u32[]{:S(2)}) collective-permute-start(f32[120,128]{1,0:T(8,128)S(1)} %add_add_fusion.5), channel_id=1, source_target_pairs={{0,2},{1,3},{2,0},{3,1},{4,6},{5,7},{6,4},{7,5},{8,10},{9,11},{10,... | collective-permute-start | bytes 184328 | tf_op jit(solution)/shard_map/ppermute | solution.py:426
  54.2 2.6 %collective-permute-start.15 = (f32[24,128]{1,0:T(8,128)S(1)}, f32[24,128]{1,0:T(8,128)S(1)}, u32[]{:S(2)}, u32[]{:S(2)}) collective-permute-start(f32[24,128]{1,0:T(8,128)S(1)} %slice.20), channel_id=1, source_target_pairs={{0,32},{32,0},{64,96},{96,64},{128,160},{160,128},{192,224},{224,1... | collective-permute-start | bytes 36872 | tf_op jit(solution)/shard_map/ppermute | solution.py:426
  56.8 5.1 %collective-permute-start.16 = (f32[120,128]{1,0:T(8,128)S(1)}, f32[120,128]{1,0:T(8,128)S(1)}, u32[]{:S(2)}, u32[]{:S(2)}) collective-permute-start(f32[120,128]{1,0:T(8,128)S(1)} %pad_maximum_fusion.1), channel_id=1, source_target_pairs={{0,1},{1,0},{2,3},{3,2},{4,5},{5,4},{6,7},{7,6},{8,9},{9,8},{10,11... | collective-permute-start | bytes 184328 | tf_op jit(solution)/shard_map/ppermute | solution.py:426
  61.0 4.0 %collective-permute-start.20 = (f32[160,128]{1,0:T(8,128)S(1)}, f32[160,128]{1,0:T(8,128)S(1)}, u32[]{:S(2)}, u32[]{:S(2)}) collective-permute-start(f32[160,128]{1,0:T(8,128)S(1)} %shard_map.108), channel_id=1, source_target_pairs={{0,32},{32,0},{64,96},{96,64},{128,160},{160,128},{192,224},{224,1... | collective-permute-start | bytes 245768 | tf_op jit(solution)/shard_map/ppermute | solution.py:426
  61.9 4.7 %collective-permute-start.19 = (f32[120,128]{1,0:T(8,128)S(1)}, f32[120,128]{1,0:T(8,128)S(1)}, u32[]{:S(2)}, u32[]{:S(2)}) collective-permute-start(f32[120,128]{1,0:T(8,128)S(1)} %fusion.1), channel_id=1, source_target_pairs={{0,16},{1,17},{2,18},{3,19},{4,20},{5,21},{6,22},{7,23},{8,24},{9,... | collective-permute-start | bytes 184328 | tf_op jit(solution)/shard_map/ppermute | solution.py:426
  63.2 5.3 %collective-permute-start.18 = (f32[120,128]{1,0:T(8,128)S(1)}, f32[120,128]{1,0:T(8,128)S(1)}, u32[]{:S(2)}, u32[]{:S(2)}) collective-permute-start(f32[120,128]{1,0:T(8,128)S(1)} %fusion.1), channel_id=1, source_target_pairs={{0,24},{1,25},{2,26},{3,27},{4,28},{5,29},{6,30},{7,31},{8,16},{9,... | collective-permute-start | bytes 184328 | tf_op jit(solution)/shard_map/ppermute | solution.py:426
  64.2 4.3 %collective-permute-start.17 = (f32[120,128]{1,0:T(8,128)S(1)}, f32[120,128]{1,0:T(8,128)S(1)}, u32[]{:S(2)}, u32[]{:S(2)}) collective-permute-start(f32[120,128]{1,0:T(8,128)S(1)} %fusion.1), channel_id=1, source_target_pairs={{0,8},{1,9},{2,10},{3,11},{4,12},{5,13},{6,14},{7,15},{8,0},{9,1},... | collective-permute-start | bytes 184328 | tf_op jit(solution)/shard_map/ppermute | solution.py:426
  68.5 4.7 %collective-permute-start.23 = (f32[120,128]{1,0:T(8,128)S(1)}, f32[120,128]{1,0:T(8,128)S(1)}, u32[]{:S(2)}, u32[]{:S(2)}) collective-permute-start(f32[120,128]{1,0:T(8,128)S(1)} %add_add_fusion.3), channel_id=1, source_target_pairs={{0,4},{1,5},{2,6},{3,7},{4,0},{5,1},{6,2},{7,3},{8,12},{9,13},{10,... | collective-permute-start | bytes 184328 | tf_op jit(solution)/shard_map/ppermute | solution.py:426
  69.9 5.0 %collective-permute-start.22 = (f32[120,128]{1,0:T(8,128)S(1)}, f32[120,128]{1,0:T(8,128)S(1)}, u32[]{:S(2)}, u32[]{:S(2)}) collective-permute-start(f32[120,128]{1,0:T(8,128)S(1)} %add_add_fusion.3), channel_id=1, source_target_pairs={{0,6},{1,7},{2,4},{3,5},{4,2},{5,3},{6,0},{7,1},{8,14},{9,15},{10,... | collective-permute-start | bytes 184328 | tf_op jit(solution)/shard_map/ppermute | solution.py:426
  70.6 4.3 %collective-permute-start.21 = (f32[120,128]{1,0:T(8,128)S(1)}, f32[120,128]{1,0:T(8,128)S(1)}, u32[]{:S(2)}, u32[]{:S(2)}) collective-permute-start(f32[120,128]{1,0:T(8,128)S(1)} %add_add_fusion.3), channel_id=1, source_target_pairs={{0,2},{1,3},{2,0},{3,1},{4,6},{5,7},{6,4},{7,5},{8,10},{9,11},{10,... | collective-permute-start | bytes 184328 | tf_op jit(solution)/shard_map/ppermute | solution.py:426
  78.2 2.6 %collective-permute-start.24 = (f32[24,128]{1,0:T(8,128)S(1)}, f32[24,128]{1,0:T(8,128)S(1)}, u32[]{:S(2)}, u32[]{:S(2)}) collective-permute-start(f32[24,128]{1,0:T(8,128)S(1)} %slice.22), channel_id=1, source_target_pairs={{0,32},{32,0},{64,96},{96,64},{128,160},{160,128},{192,224},{224,1... | collective-permute-start | bytes 36872 | tf_op jit(solution)/shard_map/ppermute | solution.py:426
  80.9 3.8 %collective-permute-start.25 = (f32[120,128]{1,0:T(8,128)S(1)}, f32[120,128]{1,0:T(8,128)S(1)}, u32[]{:S(2)}, u32[]{:S(2)}) collective-permute-start(f32[120,128]{1,0:T(8,128)S(1)} %pad_maximum_fusion.2), channel_id=1, source_target_pairs={{0,1},{1,0},{2,3},{3,2},{4,5},{5,4},{6,7},{7,6},{8,9},{9,8},{10,11... | collective-permute-start | bytes 184328 | tf_op jit(solution)/shard_map/ppermute | solution.py:426
  83.8 4.0 %collective-permute-start.29 = (f32[160,128]{1,0:T(8,128)S(1)}, f32[160,128]{1,0:T(8,128)S(1)}, u32[]{:S(2)}, u32[]{:S(2)}) collective-permute-start(f32[160,128]{1,0:T(8,128)S(1)} %shard_map.111), channel_id=1, source_target_pairs={{0,32},{32,0},{64,96},{96,64},{128,160},{160,128},{192,224},{224,1... | collective-permute-start | bytes 245768 | tf_op jit(solution)/shard_map/ppermute | solution.py:426
  84.7 4.7 %collective-permute-start.28 = (f32[120,128]{1,0:T(8,128)S(1)}, f32[120,128]{1,0:T(8,128)S(1)}, u32[]{:S(2)}, u32[]{:S(2)}) collective-permute-start(f32[120,128]{1,0:T(8,128)S(1)} %fusion), channel_id=1, source_target_pairs={{0,16},{1,17},{2,18},{3,19},{4,20},{5,21},{6,22},{7,23},{8,24},{9,... | collective-permute-start | bytes 184328 | tf_op jit(solution)/shard_map/ppermute | solution.py:426
  86.6 4.3 %collective-permute-start.27 = (f32[120,128]{1,0:T(8,128)S(1)}, f32[120,128]{1,0:T(8,128)S(1)}, u32[]{:S(2)}, u32[]{:S(2)}) collective-permute-start(f32[120,128]{1,0:T(8,128)S(1)} %fusion), channel_id=1, source_target_pairs={{0,24},{1,25},{2,26},{3,27},{4,28},{5,29},{6,30},{7,31},{8,16},{9,... | collective-permute-start | bytes 184328 | tf_op jit(solution)/shard_map/ppermute | solution.py:426
  87.5 3.3 %collective-permute-start.26 = (f32[120,128]{1,0:T(8,128)S(1)}, f32[120,128]{1,0:T(8,128)S(1)}, u32[]{:S(2)}, u32[]{:S(2)}) collective-permute-start(f32[120,128]{1,0:T(8,128)S(1)} %fusion), channel_id=1, source_target_pairs={{0,8},{1,9},{2,10},{3,11},{4,12},{5,13},{6,14},{7,15},{8,0},{9,1},... | collective-permute-start | bytes 184328 | tf_op jit(solution)/shard_map/ppermute | solution.py:426
  90.9 4.7 %collective-permute-start.32 = (f32[120,128]{1,0:T(8,128)S(1)}, f32[120,128]{1,0:T(8,128)S(1)}, u32[]{:S(2)}, u32[]{:S(2)}) collective-permute-start(f32[120,128]{1,0:T(8,128)S(1)} %add_add_fusion.1), channel_id=1, source_target_pairs={{0,4},{1,5},{2,6},{3,7},{4,0},{5,1},{6,2},{7,3},{8,12},{9,13},{10,... | collective-permute-start | bytes 184328 | tf_op jit(solution)/shard_map/ppermute | solution.py:426
  92.9 4.6 %collective-permute-start.31 = (f32[120,128]{1,0:T(8,128)S(1)}, f32[120,128]{1,0:T(8,128)S(1)}, u32[]{:S(2)}, u32[]{:S(2)}) collective-permute-start(f32[120,128]{1,0:T(8,128)S(1)} %add_add_fusion.1), channel_id=1, source_target_pairs={{0,6},{1,7},{2,4},{3,5},{4,2},{5,3},{6,0},{7,1},{8,14},{9,15},{10,... | collective-permute-start | bytes 184328 | tf_op jit(solution)/shard_map/ppermute | solution.py:426
  93.8 3.8 %collective-permute-start.30 = (f32[120,128]{1,0:T(8,128)S(1)}, f32[120,128]{1,0:T(8,128)S(1)}, u32[]{:S(2)}, u32[]{:S(2)}) collective-permute-start(f32[120,128]{1,0:T(8,128)S(1)} %add_add_fusion.1), channel_id=1, source_target_pairs={{0,2},{1,3},{2,0},{3,1},{4,6},{5,7},{6,4},{7,5},{8,10},{9,11},{10,... | collective-permute-start | bytes 184328 | tf_op jit(solution)/shard_map/ppermute | solution.py:426

commit v5 on v4

--- a/solution.py
+++ b/solution.py
@@ -43,7 +43,7 @@
 
 
 def total(value):
-    return jnp.sum(jnp.sum(value, axis=1, keepdims=True), axis=0, keepdims=True)
+    return jnp.sum(jnp.sum(value, axis=0, keepdims=True), axis=1, keepdims=True)
 
 
 def one_hot(index, count):
@@ -163,11 +163,8 @@
 
 
 def get_scalars(rest_ref):
-    bounds = rest_ref[N_C : N_C + N_B]
-    rows, lanes = iota((8, LO), 0), iota((8, LO), 1)
-    return [
-        total(jnp.where(jnp.logical_and(rows == i, lanes == SCALAR_LANE), bounds, 0.0)) for i in range(3)
-    ]
+    lanes = slice(SCALAR_LANE, SCALAR_LANE + 1)
+    return [rest_ref[N_C + i : N_C + i + 1, lanes] for i in range(3)]
 
 
 def read_sums(stars_ref, rest_ref):

time: 117 us -> 117 us (level)
  no operation moved by 1% of the time
where the time goes in v5:
time: 117 us
  starting transfers between devices  46.4 us (40%)
  waiting for transfers between devices  30.6 us (26%)
  Pallas kernels  20.8 us (18%)
  blocking collectives  16.1 us (14%)
  between operations  1.43 us (1%)
  other arithmetic  1.2 us (1%)
    ppermute x33, starting transfers between devices, swap(): return lax.ppermute(value, axis, [(i, i ^ bits) for i in range(count)])  46.4 us
    ppermute x33, waiting for transfers between devices, swap(): return lax.ppermute(value, axis, [(i, i ^ bits) for i in range(count)])  30.6 us
    pallas_call x12, Pallas kernels, call(): pl.pallas_call(kernel, out_shape=[jax.ShapeDtypeStruct(shape, F32) for sh...  20.8 us
    all_to_all x1, blocking collectives, shards(): lax.all_to_all(jnp.broadcast_to(partial[None], (count, 1, LO)), axes, 0, 0)  16.1 us
  transfers between devices with their start and end apart: 33, of which 24 were waited for; matrix products, arithmetic and copies ran while one was open for 0% of the time, Pallas kernels for 6%

profile of v5, /device:TPU:1, one launch (start us, length us, event | category | flops | bytes accessed | tf_op | source)
XLA Modules:
  0.0 116.5 jit_solution(4004707092028060973)
XLA Ops:
  1.3 1.7 %shard_map.103 = (f32[1,24,1024]{2,1,0:T(8,128)}, f32[1,24,1024]{2,1,0:T(8,128)}) custom-call(s32[1,1]{1,0:T(1,128)S(6)} %copy.11.blocks_ref, f32[5,2048]{1,0:T(8,128)} %args_0_.4, f32[12,2048]{1,0:T(8,128)} %args_1_.4, f32[1,2048]{1,0:T(1,128)} %bitcast.11, f32[1,2048]{1,0:T(1,128)} %bitcast.12, s32[1,2048]{1,0:T(1,128)} %bitcast.13, s32[1,2048]{1,0:T(1,128)} %bitcast.14, ...), custom_call_target="tpu_custom_call" | custom-call | flops 1500000000 | bytes 1000000 | tf_op jit(solution)/shard_map/pallas_call | solution.py:409
  3.0 6.9 %collective-permute-start.2 = (f32[1,24,1024]{2,1,0:T(8,128)}, f32[1,24,1024]{2,1,0:T(8,128)S(1)}, u32[]{:S(2)}, u32[]{:S(2)}) collective-permute-start(f32[1,24,1024]{2,1,0:T(8,128)} %get-tuple-element.37), channel_id=1, source_target_pairs={{0,192},{32,224},{64,128},{96,160},{128,64},{160,96},{192,0},{224,... | collective-permute-start | bytes 294920 | tf_op jit(solution)/shard_map/ppermute | solution.py:423
  9.9 1.2 %collective-permute-start.1 = (f32[1,24,1024]{2,1,0:T(8,128)}, f32[1,24,1024]{2,1,0:T(8,128)S(1)}, u32[]{:S(2)}, u32[]{:S(2)}) collective-permute-start(f32[1,24,1024]{2,1,0:T(8,128)} %get-tuple-element.38), channel_id=1, source_target_pairs={{0,64},{32,96},{64,0},{96,32},{128,192},{160,224},{192,128},{224,1... | collective-permute-start | bytes 294920 | tf_op jit(solution)/shard_map/ppermute | solution.py:423
  11.1 1.2 %collective-permute-start = (f32[1,24,1024]{2,1,0:T(8,128)}, f32[1,24,1024]{2,1,0:T(8,128)S(1)}, u32[]{:S(2)}, u32[]{:S(2)}) collective-permute-start(f32[1,24,1024]{2,1,0:T(8,128)} %get-tuple-element.37), channel_id=1, source_target_pairs={{0,64},{32,96},{64,0},{96,32},{128,192},{160,224},{192,128},{224,1... | collective-permute-start | bytes 294920 | tf_op jit(solution)/shard_map/ppermute | solution.py:423
  12.4 1.8 %collective-permute-done.2 = f32[1,24,1024]{2,1,0:T(8,128)S(1)} collective-permute-done((f32[1,24,1024]{2,1,0:T(8,128)}, f32[1,24,1024]{2,1,0:T(8,128)S(1)}, u32[]{:S(2)}, u32[]{:S(2)}) %collective-permute-start.2) | collective-permute-done | bytes 98336 | tf_op jit(solution)/shard_map/ppermute | solution.py:423
  14.2 1.2 %collective-permute-start.3 = (f32[1,24,1024]{2,1,0:T(8,128)S(1)}, f32[1,24,1024]{2,1,0:T(8,128)S(1)}, u32[]{:S(2)}, u32[]{:S(2)}) collective-permute-start(f32[1,24,1024]{2,1,0:T(8,128)S(1)} %collective-permute-done.2), channel_id=1, source_target_pairs={{0,64},{32,96},{64,0},{96,32},{128,192},{160,224},{192,128},{224,1... | collective-permute-start | bytes 294920 | tf_op jit(solution)/shard_map/ppermute | solution.py:423
  15.3 3.2 %collective-permute-start.4 = (f32[1,24,1024]{2,1,0:T(8,128)S(1)}, f32[1,24,1024]{2,1,0:T(8,128)S(1)}, u32[]{:S(2)}, u32[]{:S(2)}) collective-permute-start(f32[1,24,1024]{2,1,0:T(8,128)S(1)} %collective-permute-done.1), channel_id=1, source_target_pairs={{0,192},{32,224},{64,128},{96,160},{128,64},{160,96},{192,0},{224,... | collective-permute-start | bytes 294920 | tf_op jit(solution)/shard_map/ppermute | solution.py:423
  18.5 2.8 %collective-permute-done = f32[1,24,1024]{2,1,0:T(8,128)S(1)} collective-permute-done((f32[1,24,1024]{2,1,0:T(8,128)}, f32[1,24,1024]{2,1,0:T(8,128)S(1)}, u32[]{:S(2)}, u32[]{:S(2)}) %collective-permute-start) | collective-permute-done | bytes 98336 | tf_op jit(solution)/shard_map/ppermute | solution.py:423
  21.3 0.7 collective-permute-done.5
  22.0 3.4 %collective-permute-done.3 = f32[1,24,1024]{2,1,0:T(8,128)S(1)} collective-permute-done((f32[1,24,1024]{2,1,0:T(8,128)S(1)}, f32[1,24,1024]{2,1,0:T(8,128)S(1)}, u32[]{:S(2)}, u32[]{:S(2)}) %collective-permute-start.3) | collective-permute-done | bytes 98336 | tf_op jit(solution)/shard_map/ppermute | solution.py:423
  25.4 1.0 maximum_maximum_fusion.data_ref
  26.4 1.9 %shard_map.104 = f32[120,128]{1,0:T(8,128)S(1)} custom-call(s32[1]{0:T(128)} %bitcast.window_ref, f32[4,24,2048]{2,1,0:T(8,128)S(1)} %maximum_maximum_fusion.data_ref), custom_call_target="tpu_custom_call" | custom-call | flops 1500000000 | bytes 1000000 | tf_op jit(solution)/shard_map/pallas_call | solution.py:409
  28.4 1.5 %shard_map.105 = f32[160,128]{1,0:T(8,128)S(1)} custom-call(s32[1]{0:T(128)} %bitcast.window_ref, f32[4,24,2048]{2,1,0:T(8,128)S(1)} %maximum_maximum_fusion.data_ref), custom_call_target="tpu_custom_call" | custom-call | flops 1500000000 | bytes 1000000 | tf_op jit(solution)/shard_map/pallas_call | solution.py:409
  30.0 1.0 collective-permute-done.6
  31.0 4.1 %collective-permute-start.7 = (f32[120,128]{1,0:T(8,128)S(1)}, f32[120,128]{1,0:T(8,128)S(1)}, u32[]{:S(2)}, u32[]{:S(2)}) collective-permute-start(f32[120,128]{1,0:T(8,128)S(1)} %pad_maximum_fusion), channel_id=1, source_target_pairs={{0,1},{1,0},{2,3},{3,2},{4,5},{5,4},{6,7},{7,6},{8,9},{9,8},{10,11... | collective-permute-start | bytes 184328 | tf_op jit(solution)/shard_map/ppermute | solution.py:423
  35.1 0.9 collective-permute-done.7
  36.0 2.8 %collective-permute-start.10 = (f32[120,128]{1,0:T(8,128)S(1)}, f32[120,128]{1,0:T(8,128)S(1)}, u32[]{:S(2)}, u32[]{:S(2)}) collective-permute-start(f32[120,128]{1,0:T(8,128)S(1)} %fusion.2), channel_id=1, source_target_pairs={{0,16},{1,17},{2,18},{3,19},{4,20},{5,21},{6,22},{7,23},{8,24},{9,... | collective-permute-start | bytes 184328 | tf_op jit(solution)/shard_map/ppermute | solution.py:423
  38.9 0.9 collective-permute-start.9
  39.7 1.0 collective-permute-done.10
  40.7 2.4 %collective-permute-done.9 = f32[120,128]{1,0:T(8,128)S(1)} collective-permute-done((f32[120,128]{1,0:T(8,128)S(1)}, f32[120,128]{1,0:T(8,128)S(1)}, u32[]{:S(2)}, u32[]{:S(2)}) %collective-permute-start.9) | collective-permute-done | bytes 61472 | tf_op jit(solution)/shard_map/ppermute | solution.py:423
  43.2 3.0 %collective-permute-start.14 = (f32[120,128]{1,0:T(8,128)S(1)}, f32[120,128]{1,0:T(8,128)S(1)}, u32[]{:S(2)}, u32[]{:S(2)}) collective-permute-start(f32[120,128]{1,0:T(8,128)S(1)} %add_add_fusion.5), channel_id=1, source_target_pairs={{0,4},{1,5},{2,6},{3,7},{4,0},{5,1},{6,2},{7,3},{8,12},{9,13},{10,... | collective-permute-start | bytes 184328 | tf_op jit(solution)/shard_map/ppermute | solution.py:423
  46.2 0.8 collective-permute-start.13
  46.9 1.0 shard_map.106
  48.0 2.8 %collective-permute-done.13 = f32[120,128]{1,0:T(8,128)S(1)} collective-permute-done((f32[120,128]{1,0:T(8,128)S(1)}, f32[120,128]{1,0:T(8,128)S(1)}, u32[]{:S(2)}, u32[]{:S(2)}) %collective-permute-start.13) | collective-permute-done | bytes 61472 | tf_op jit(solution)/shard_map/ppermute | solution.py:423
  50.8 3.5 %shard_map.107 = (f32[120,128]{1,0:T(8,128)S(1)}, f32[280,128]{1,0:T(8,128)S(1)}, f32[4,2048]{1,0:T(4,128)S(1)}, f32[8,128]{1,0:T(8,128)S(1)}) custom-call(s32[1]{0:T(128)} %bitcast.window_ref, f32[4,24,2048]{2,1,0:T(8,128)S(1)} %maximum_maximum_fusion.data_ref, f32[160,128]{1,0:T(8,128)S(1)} %add.90.stars_ref, f32[120,128]{1,0:T(8,128)S(1)} %add_add_fusion.4.rest_in_ref, ...), custom_call_target="tpu_custom_call" | custom-call | flops 1500000000 | bytes 1000000 | tf_op jit(solution)/shard_map/pallas_call | solution.py:409
  54.2 0.7 collective-permute-start.15
  54.9 1.6 %shard_map.108 = f32[160,128]{1,0:T(8,128)S(1)} custom-call(s32[1]{0:T(128)} %bitcast.window_ref, f32[4,24,2048]{2,1,0:T(8,128)S(1)} %maximum_maximum_fusion.data_ref, f32[4,2048]{1,0:T(4,128)S(1)} %get-tuple-element.46.row_ref.args_4_.args_7_, f32[8,128]{1,0:T(8,128)S(1)} %get-tuple-element.47.kept_ref.args_5_), custom_call_target="tpu_custom_call" | custom-call | flops 1500000000 | bytes 1000000 | tf_op jit(solution)/shard_map/pallas_call | solution.py:409
  56.5 0.4 collective-permute-done.15
  56.9 4.2 %collective-permute-start.16 = (f32[120,128]{1,0:T(8,128)S(1)}, f32[120,128]{1,0:T(8,128)S(1)}, u32[]{:S(2)}, u32[]{:S(2)}) collective-permute-start(f32[120,128]{1,0:T(8,128)S(1)} %pad_maximum_fusion.1), channel_id=1, source_target_pairs={{0,1},{1,0},{2,3},{3,2},{4,5},{5,4},{6,7},{7,6},{8,9},{9,8},{10,11... | collective-permute-start | bytes 184328 | tf_op jit(solution)/shard_map/ppermute | solution.py:423
  61.0 0.6 collective-permute-start.20
  61.7 0.3 collective-permute-done.16
  61.9 1.3 %collective-permute-start.19 = (f32[120,128]{1,0:T(8,128)S(1)}, f32[120,128]{1,0:T(8,128)S(1)}, u32[]{:S(2)}, u32[]{:S(2)}) collective-permute-start(f32[120,128]{1,0:T(8,128)S(1)} %fusion.1), channel_id=1, source_target_pairs={{0,16},{1,17},{2,18},{3,19},{4,20},{5,21},{6,22},{7,23},{8,24},{9,... | collective-permute-start | bytes 184328 | tf_op jit(solution)/shard_map/ppermute | solution.py:423
  63.2 1.0 collective-permute-start.18
  64.3 0.4 collective-permute-start.17
  64.7 0.4 collective-permute-done.20
  65.1 1.5 %collective-permute-done.19 = f32[120,128]{1,0:T(8,128)S(1)} collective-permute-done((f32[120,128]{1,0:T(8,128)S(1)}, f32[120,128]{1,0:T(8,128)S(1)}, u32[]{:S(2)}, u32[]{:S(2)}) %collective-permute-start.19) | collective-permute-done | bytes 61472 | tf_op jit(solution)/shard_map/ppermute | solution.py:423
  66.6 1.9 %collective-permute-done.18 = f32[120,128]{1,0:T(8,128)S(1)} collective-permute-done((f32[120,128]{1,0:T(8,128)S(1)}, f32[120,128]{1,0:T(8,128)S(1)}, u32[]{:S(2)}, u32[]{:S(2)}) %collective-permute-start.18) | collective-permute-done | bytes 61472 | tf_op jit(solution)/shard_map/ppermute | solution.py:423
  68.5 1.4 %collective-permute-start.23 = (f32[120,128]{1,0:T(8,128)S(1)}, f32[120,128]{1,0:T(8,128)S(1)}, u32[]{:S(2)}, u32[]{:S(2)}) collective-permute-start(f32[120,128]{1,0:T(8,128)S(1)} %add_add_fusion.3), channel_id=1, source_target_pairs={{0,4},{1,5},{2,6},{3,7},{4,0},{5,1},{6,2},{7,3},{8,12},{9,13},{10,... | collective-permute-start | bytes 184328 | tf_op jit(solution)/shard_map/ppermute | solution.py:423
  69.9 0.7 collective-permute-start.22
  70.6 0.7 collective-permute-start.21
  71.3 1.0 shard_map.109.args_2_
  72.2 1.0 collective-permute-done.23
  73.2 1.7 %collective-permute-done.22 = f32[120,128]{1,0:T(8,128)S(1)} collective-permute-done((f32[120,128]{1,0:T(8,128)S(1)}, f32[120,128]{1,0:T(8,128)S(1)}, u32[]{:S(2)}, u32[]{:S(2)}) %collective-permute-start.22) | collective-permute-done | bytes 61472 | tf_op jit(solution)/shard_map/ppermute | solution.py:423
  74.9 3.4 %shard_map.110 = (f32[120,128]{1,0:T(8,128)S(1)}, f32[280,128]{1,0:T(8,128)S(1)}, f32[280,128]{1,0:T(8,128)S(1)}, f32[4,2048]{1,0:T(4,128)S(1)}, f32[4,2048]{1,0:T(4,128)S(1)}, /*index=5*/f32[8,128]{1,0:T(8,128)S(1)}) custom-call(s32[1]{0:T(128)} %bitcast.window_ref, f32[4,24,2048]{2,1,0:T(8,128)S(1)} %maximum_maximum_fusion.data_ref, ...), custom_call_target="tpu_custom_call" | custom-call | flops 1500000000 | bytes 1000000 | tf_op jit(solution)/shard_map/pallas_call | solution.py:409
  78.3 0.7 collective-permute-start.24
  79.0 1.6 %shard_map.111 = f32[160,128]{1,0:T(8,128)S(1)} custom-call(s32[1]{0:T(128)} %bitcast.window_ref, f32[4,24,2048]{2,1,0:T(8,128)S(1)} %maximum_maximum_fusion.data_ref, f32[4,2048]{1,0:T(4,128)S(1)} %get-tuple-element.54.row_ref.args_8_, f32[8,128]{1,0:T(8,128)S(1)} %get-tuple-element.55.kept_ref.args_9_), custom_call_target="tpu_custom_call" | custom-call | flops 1500000000 | bytes 1000000 | tf_op jit(solution)/shard_map/pallas_call | solution.py:409
  80.6 0.4 collective-permute-done.24
  81.0 2.9 %collective-permute-start.25 = (f32[120,128]{1,0:T(8,128)S(1)}, f32[120,128]{1,0:T(8,128)S(1)}, u32[]{:S(2)}, u32[]{:S(2)}) collective-permute-start(f32[120,128]{1,0:T(8,128)S(1)} %pad_maximum_fusion.2), channel_id=1, source_target_pairs={{0,1},{1,0},{2,3},{3,2},{4,5},{5,4},{6,7},{7,6},{8,9},{9,8},{10,11... | collective-permute-start | bytes 184328 | tf_op jit(solution)/shard_map/ppermute | solution.py:423
  83.9 0.6 collective-permute-start.29
  84.5 0.3 collective-permute-done.25
  84.8 1.9 %collective-permute-start.28 = (f32[120,128]{1,0:T(8,128)S(1)}, f32[120,128]{1,0:T(8,128)S(1)}, u32[]{:S(2)}, u32[]{:S(2)}) collective-permute-start(f32[120,128]{1,0:T(8,128)S(1)} %fusion), channel_id=1, source_target_pairs={{0,16},{1,17},{2,18},{3,19},{4,20},{5,21},{6,22},{7,23},{8,24},{9,... | collective-permute-start | bytes 184328 | tf_op jit(solution)/shard_map/ppermute | solution.py:423
  86.7 0.9 collective-permute-start.27
  87.6 0.2 collective-permute-done.29
  87.9 1.5 %collective-permute-done.28 = f32[120,128]{1,0:T(8,128)S(1)} collective-permute-done((f32[120,128]{1,0:T(8,128)S(1)}, f32[120,128]{1,0:T(8,128)S(1)}, u32[]{:S(2)}, u32[]{:S(2)}) %collective-permute-start.28) | collective-permute-done | bytes 61472 | tf_op jit(solution)/shard_map/ppermute | solution.py:423
  89.4 1.5 %collective-permute-done.27 = f32[120,128]{1,0:T(8,128)S(1)} collective-permute-done((f32[120,128]{1,0:T(8,128)S(1)}, f32[120,128]{1,0:T(8,128)S(1)}, u32[]{:S(2)}, u32[]{:S(2)}) %collective-permute-start.27) | collective-permute-done | bytes 61472 | tf_op jit(solution)/shard_map/ppermute | solution.py:423
  91.0 2.0 %collective-permute-start.32 = (f32[120,128]{1,0:T(8,128)S(1)}, f32[120,128]{1,0:T(8,128)S(1)}, u32[]{:S(2)}, u32[]{:S(2)}) collective-permute-start(f32[120,128]{1,0:T(8,128)S(1)} %add_add_fusion.1), channel_id=1, source_target_pairs={{0,4},{1,5},{2,6},{3,7},{4,0},{5,1},{6,2},{7,3},{8,12},{9,13},{10,... | collective-permute-start | bytes 184328 | tf_op jit(solution)/shard_map/ppermute | solution.py:423
  93.0 0.9 collective-permute-start.31
  93.9 0.9 shard_map.112.args_2_
  94.9 0.8 collective-permute-done.32
  95.7 1.9 %collective-permute-done.31 = f32[120,128]{1,0:T(8,128)S(1)} collective-permute-done((f32[120,128]{1,0:T(8,128)S(1)}, f32[120,128]{1,0:T(8,128)S(1)}, u32[]{:S(2)}, u32[]{:S(2)}) %collective-permute-start.31) | collective-permute-done | bytes 61472 | tf_op jit(solution)/shard_map/ppermute | solution.py:423
  97.6 0.1 collective-permute-done.30
  97.7 1.7 %shard_map.113 = (f32[280,128]{1,0:T(8,128)S(1)}, f32[280,128]{1,0:T(8,128)S(1)}, f32[280,128]{1,0:T(8,128)S(1)}, f32[8,128]{1,0:T(8,128)S(1)}, f32[1,128]{1,0:T(1,128)S(1)}) custom-call(s32[1]{0:T(128)} %bitcast.window_ref, f32[4,24,2048]{2,1,0:T(8,128)S(1)} %maximum_maximum_fusion.data_ref, f32[160,128]{1,0:T(8,128)S(1)} %add.108.stars_ref.args_0_, ...), custom_call_target="tpu_custom_call" | custom-call | flops 1500000000 | bytes 1000000 | tf_op jit(solution)/shard_map/pallas_call | solution.py:409
  99.5 16.1 %all_to_all.5 = f32[64,1,128]{2,1,0:T(1,128)S(1)} all-to-all(f32[64,1,128]{2,1,0:T(1,128)S(1)} %broadcast_in_dim.9), channel_id=1, replica_groups=mesh['tm_high'=4,'tm_low'=2,'star'=32] {'tm_low','star'}, dimensions={0} | all-to-all | bytes 65536 | tf_op jit(solution)/shard_map/all_to_all | solution.py:515
  115.5 1.0 shard_map.114
  (41 shorter events, 0.5 us)
Async XLA Ops:
  3.0 11.2 %collective-permute-start.2 = (f32[1,24,1024]{2,1,0:T(8,128)}, f32[1,24,1024]{2,1,0:T(8,128)S(1)}, u32[]{:S(2)}, u32[]{:S(2)}) collective-permute-start(f32[1,24,1024]{2,1,0:T(8,128)} %get-tuple-element.37), channel_id=1, source_target_pairs={{0,192},{32,224},{64,128},{96,160},{128,64},{160,96},{192,0},{224,... | collective-permute-start | bytes 294920 | tf_op jit(solution)/shard_map/ppermute | solution.py:423
  9.9 5.4 %collective-permute-start.1 = (f32[1,24,1024]{2,1,0:T(8,128)}, f32[1,24,1024]{2,1,0:T(8,128)S(1)}, u32[]{:S(2)}, u32[]{:S(2)}) collective-permute-start(f32[1,24,1024]{2,1,0:T(8,128)} %get-tuple-element.38), channel_id=1, source_target_pairs={{0,64},{32,96},{64,0},{96,32},{128,192},{160,224},{192,128},{224,1... | collective-permute-start | bytes 294920 | tf_op jit(solution)/shard_map/ppermute | solution.py:423
  11.1 10.2 %collective-permute-start = (f32[1,24,1024]{2,1,0:T(8,128)}, f32[1,24,1024]{2,1,0:T(8,128)S(1)}, u32[]{:S(2)}, u32[]{:S(2)}) collective-permute-start(f32[1,24,1024]{2,1,0:T(8,128)} %get-tuple-element.37), channel_id=1, source_target_pairs={{0,64},{32,96},{64,0},{96,32},{128,192},{160,224},{192,128},{224,1... | collective-permute-start | bytes 294920 | tf_op jit(solution)/shard_map/ppermute | solution.py:423
  12.3 9.7 %collective-permute-start.5 = (f32[1,24,1024]{2,1,0:T(8,128)}, f32[1,24,1024]{2,1,0:T(8,128)S(1)}, u32[]{:S(2)}, u32[]{:S(2)}) collective-permute-start(f32[1,24,1024]{2,1,0:T(8,128)} %get-tuple-element.38), channel_id=1, source_target_pairs={{0,192},{32,224},{64,128},{96,160},{128,64},{160,96},{192,0},{224,... | collective-permute-start | bytes 294920 | tf_op jit(solution)/shard_map/ppermute | solution.py:423
  14.2 11.2 %collective-permute-start.3 = (f32[1,24,1024]{2,1,0:T(8,128)S(1)}, f32[1,24,1024]{2,1,0:T(8,128)S(1)}, u32[]{:S(2)}, u32[]{:S(2)}) collective-permute-start(f32[1,24,1024]{2,1,0:T(8,128)S(1)} %collective-permute-done.2), channel_id=1, source_target_pairs={{0,64},{32,96},{64,0},{96,32},{128,192},{160,224},{192,128},{224,1... | collective-permute-start | bytes 294920 | tf_op jit(solution)/shard_map/ppermute | solution.py:423
  15.3 10.1 %collective-permute-start.4 = (f32[1,24,1024]{2,1,0:T(8,128)S(1)}, f32[1,24,1024]{2,1,0:T(8,128)S(1)}, u32[]{:S(2)}, u32[]{:S(2)}) collective-permute-start(f32[1,24,1024]{2,1,0:T(8,128)S(1)} %collective-permute-done.1), channel_id=1, source_target_pairs={{0,192},{32,224},{64,128},{96,160},{128,64},{160,96},{192,0},{224,... | collective-permute-start | bytes 294920 | tf_op jit(solution)/shard_map/ppermute | solution.py:423
  28.3 2.6 %collective-permute-start.6 = (f32[24,128]{1,0:T(8,128)S(1)}, f32[24,128]{1,0:T(8,128)S(1)}, u32[]{:S(2)}, u32[]{:S(2)}) collective-permute-start(f32[24,128]{1,0:T(8,128)S(1)} %slice.24), channel_id=1, source_target_pairs={{0,32},{32,0},{64,96},{96,64},{128,160},{160,128},{192,224},{224,1... | collective-permute-start | bytes 36872 | tf_op jit(solution)/shard_map/ppermute | solution.py:423
  31.0 5.0 %collective-permute-start.7 = (f32[120,128]{1,0:T(8,128)S(1)}, f32[120,128]{1,0:T(8,128)S(1)}, u32[]{:S(2)}, u32[]{:S(2)}) collective-permute-start(f32[120,128]{1,0:T(8,128)S(1)} %pad_maximum_fusion), channel_id=1, source_target_pairs={{0,1},{1,0},{2,3},{3,2},{4,5},{5,4},{6,7},{7,6},{8,9},{9,8},{10,11... | collective-permute-start | bytes 184328 | tf_op jit(solution)/shard_map/ppermute | solution.py:423
  35.1 4.6 %collective-permute-start.11 = (f32[160,128]{1,0:T(8,128)S(1)}, f32[160,128]{1,0:T(8,128)S(1)}, u32[]{:S(2)}, u32[]{:S(2)}) collective-permute-start(f32[160,128]{1,0:T(8,128)S(1)} %shard_map.105), channel_id=1, source_target_pairs={{0,32},{32,0},{64,96},{96,64},{128,160},{160,128},{192,224},{224,1... | collective-permute-start | bytes 245768 | tf_op jit(solution)/shard_map/ppermute | solution.py:423
  36.0 4.7 %collective-permute-start.10 = (f32[120,128]{1,0:T(8,128)S(1)}, f32[120,128]{1,0:T(8,128)S(1)}, u32[]{:S(2)}, u32[]{:S(2)}) collective-permute-start(f32[120,128]{1,0:T(8,128)S(1)} %fusion.2), channel_id=1, source_target_pairs={{0,16},{1,17},{2,18},{3,19},{4,20},{5,21},{6,22},{7,23},{8,24},{9,... | collective-permute-start | bytes 184328 | tf_op jit(solution)/shard_map/ppermute | solution.py:423
  38.9 4.3 %collective-permute-start.9 = (f32[120,128]{1,0:T(8,128)S(1)}, f32[120,128]{1,0:T(8,128)S(1)}, u32[]{:S(2)}, u32[]{:S(2)}) collective-permute-start(f32[120,128]{1,0:T(8,128)S(1)} %fusion.2), channel_id=1, source_target_pairs={{0,24},{1,25},{2,26},{3,27},{4,28},{5,29},{6,30},{7,31},{8,16},{9,... | collective-permute-start | bytes 184328 | tf_op jit(solution)/shard_map/ppermute | solution.py:423
  39.7 3.4 %collective-permute-start.8 = (f32[120,128]{1,0:T(8,128)S(1)}, f32[120,128]{1,0:T(8,128)S(1)}, u32[]{:S(2)}, u32[]{:S(2)}) collective-permute-start(f32[120,128]{1,0:T(8,128)S(1)} %fusion.2), channel_id=1, source_target_pairs={{0,8},{1,9},{2,10},{3,11},{4,12},{5,13},{6,14},{7,15},{8,0},{9,1},... | collective-permute-start | bytes 184328 | tf_op jit(solution)/shard_map/ppermute | solution.py:423
  43.2 4.8 %collective-permute-start.14 = (f32[120,128]{1,0:T(8,128)S(1)}, f32[120,128]{1,0:T(8,128)S(1)}, u32[]{:S(2)}, u32[]{:S(2)}) collective-permute-start(f32[120,128]{1,0:T(8,128)S(1)} %add_add_fusion.5), channel_id=1, source_target_pairs={{0,4},{1,5},{2,6},{3,7},{4,0},{5,1},{6,2},{7,3},{8,12},{9,13},{10,... | collective-permute-start | bytes 184328 | tf_op jit(solution)/shard_map/ppermute | solution.py:423
  46.2 4.6 %collective-permute-start.13 = (f32[120,128]{1,0:T(8,128)S(1)}, f32[120,128]{1,0:T(8,128)S(1)}, u32[]{:S(2)}, u32[]{:S(2)}) collective-permute-start(f32[120,128]{1,0:T(8,128)S(1)} %add_add_fusion.5), channel_id=1, source_target_pairs={{0,6},{1,7},{2,4},{3,5},{4,2},{5,3},{6,0},{7,1},{8,14},{9,15},{10,... | collective-permute-start | bytes 184328 | tf_op jit(solution)/shard_map/ppermute | solution.py:423
  46.9 3.8 %collective-permute-start.12 = (f32[120,128]{1,0:T(8,128)S(1)}, f32[120,128]{1,0:T(8,128)S(1)}, u32[]{:S(2)}, u32[]{:S(2)}) collective-permute-start(f32[120,128]{1,0:T(8,128)S(1)} %add_add_fusion.5), channel_id=1, source_target_pairs={{0,2},{1,3},{2,0},{3,1},{4,6},{5,7},{6,4},{7,5},{8,10},{9,11},{10,... | collective-permute-start | bytes 184328 | tf_op jit(solution)/shard_map/ppermute | solution.py:423
  54.2 2.6 %collective-permute-start.15 = (f32[24,128]{1,0:T(8,128)S(1)}, f32[24,128]{1,0:T(8,128)S(1)}, u32[]{:S(2)}, u32[]{:S(2)}) collective-permute-start(f32[24,128]{1,0:T(8,128)S(1)} %slice.20), channel_id=1, source_target_pairs={{0,32},{32,0},{64,96},{96,64},{128,160},{160,128},{192,224},{224,1... | collective-permute-start | bytes 36872 | tf_op jit(solution)/shard_map/ppermute | solution.py:423
  56.9 5.1 %collective-permute-start.16 = (f32[120,128]{1,0:T(8,128)S(1)}, f32[120,128]{1,0:T(8,128)S(1)}, u32[]{:S(2)}, u32[]{:S(2)}) collective-permute-start(f32[120,128]{1,0:T(8,128)S(1)} %pad_maximum_fusion.1), channel_id=1, source_target_pairs={{0,1},{1,0},{2,3},{3,2},{4,5},{5,4},{6,7},{7,6},{8,9},{9,8},{10,11... | collective-permute-start | bytes 184328 | tf_op jit(solution)/shard_map/ppermute | solution.py:423
  61.0 4.0 %collective-permute-start.20 = (f32[160,128]{1,0:T(8,128)S(1)}, f32[160,128]{1,0:T(8,128)S(1)}, u32[]{:S(2)}, u32[]{:S(2)}) collective-permute-start(f32[160,128]{1,0:T(8,128)S(1)} %shard_map.108), channel_id=1, source_target_pairs={{0,32},{32,0},{64,96},{96,64},{128,160},{160,128},{192,224},{224,1... | collective-permute-start | bytes 245768 | tf_op jit(solution)/shard_map/ppermute | solution.py:423
  61.9 4.7 %collective-permute-start.19 = (f32[120,128]{1,0:T(8,128)S(1)}, f32[120,128]{1,0:T(8,128)S(1)}, u32[]{:S(2)}, u32[]{:S(2)}) collective-permute-start(f32[120,128]{1,0:T(8,128)S(1)} %fusion.1), channel_id=1, source_target_pairs={{0,16},{1,17},{2,18},{3,19},{4,20},{5,21},{6,22},{7,23},{8,24},{9,... | collective-permute-start | bytes 184328 | tf_op jit(solution)/shard_map/ppermute | solution.py:423
  63.2 5.3 %collective-permute-start.18 = (f32[120,128]{1,0:T(8,128)S(1)}, f32[120,128]{1,0:T(8,128)S(1)}, u32[]{:S(2)}, u32[]{:S(2)}) collective-permute-start(f32[120,128]{1,0:T(8,128)S(1)} %fusion.1), channel_id=1, source_target_pairs={{0,24},{1,25},{2,26},{3,27},{4,28},{5,29},{6,30},{7,31},{8,16},{9,... | collective-permute-start | bytes 184328 | tf_op jit(solution)/shard_map/ppermute | solution.py:423
  64.3 4.3 %collective-permute-start.17 = (f32[120,128]{1,0:T(8,128)S(1)}, f32[120,128]{1,0:T(8,128)S(1)}, u32[]{:S(2)}, u32[]{:S(2)}) collective-permute-start(f32[120,128]{1,0:T(8,128)S(1)} %fusion.1), channel_id=1, source_target_pairs={{0,8},{1,9},{2,10},{3,11},{4,12},{5,13},{6,14},{7,15},{8,0},{9,1},... | collective-permute-start | bytes 184328 | tf_op jit(solution)/shard_map/ppermute | solution.py:423
  68.5 4.7 %collective-permute-start.23 = (f32[120,128]{1,0:T(8,128)S(1)}, f32[120,128]{1,0:T(8,128)S(1)}, u32[]{:S(2)}, u32[]{:S(2)}) collective-permute-start(f32[120,128]{1,0:T(8,128)S(1)} %add_add_fusion.3), channel_id=1, source_target_pairs={{0,4},{1,5},{2,6},{3,7},{4,0},{5,1},{6,2},{7,3},{8,12},{9,13},{10,... | collective-permute-start | bytes 184328 | tf_op jit(solution)/shard_map/ppermute | solution.py:423
  69.9 5.0 %collective-permute-start.22 = (f32[120,128]{1,0:T(8,128)S(1)}, f32[120,128]{1,0:T(8,128)S(1)}, u32[]{:S(2)}, u32[]{:S(2)}) collective-permute-start(f32[120,128]{1,0:T(8,128)S(1)} %add_add_fusion.3), channel_id=1, source_target_pairs={{0,6},{1,7},{2,4},{3,5},{4,2},{5,3},{6,0},{7,1},{8,14},{9,15},{10,... | collective-permute-start | bytes 184328 | tf_op jit(solution)/shard_map/ppermute | solution.py:423
  70.6 4.3 %collective-permute-start.21 = (f32[120,128]{1,0:T(8,128)S(1)}, f32[120,128]{1,0:T(8,128)S(1)}, u32[]{:S(2)}, u32[]{:S(2)}) collective-permute-start(f32[120,128]{1,0:T(8,128)S(1)} %add_add_fusion.3), channel_id=1, source_target_pairs={{0,2},{1,3},{2,0},{3,1},{4,6},{5,7},{6,4},{7,5},{8,10},{9,11},{10,... | collective-permute-start | bytes 184328 | tf_op jit(solution)/shard_map/ppermute | solution.py:423
  78.3 2.6 %collective-permute-start.24 = (f32[24,128]{1,0:T(8,128)S(1)}, f32[24,128]{1,0:T(8,128)S(1)}, u32[]{:S(2)}, u32[]{:S(2)}) collective-permute-start(f32[24,128]{1,0:T(8,128)S(1)} %slice.22), channel_id=1, source_target_pairs={{0,32},{32,0},{64,96},{96,64},{128,160},{160,128},{192,224},{224,1... | collective-permute-start | bytes 36872 | tf_op jit(solution)/shard_map/ppermute | solution.py:423
  81.0 3.8 %collective-permute-start.25 = (f32[120,128]{1,0:T(8,128)S(1)}, f32[120,128]{1,0:T(8,128)S(1)}, u32[]{:S(2)}, u32[]{:S(2)}) collective-permute-start(f32[120,128]{1,0:T(8,128)S(1)} %pad_maximum_fusion.2), channel_id=1, source_target_pairs={{0,1},{1,0},{2,3},{3,2},{4,5},{5,4},{6,7},{7,6},{8,9},{9,8},{10,11... | collective-permute-start | bytes 184328 | tf_op jit(solution)/shard_map/ppermute | solution.py:423
  83.9 4.0 %collective-permute-start.29 = (f32[160,128]{1,0:T(8,128)S(1)}, f32[160,128]{1,0:T(8,128)S(1)}, u32[]{:S(2)}, u32[]{:S(2)}) collective-permute-start(f32[160,128]{1,0:T(8,128)S(1)} %shard_map.111), channel_id=1, source_target_pairs={{0,32},{32,0},{64,96},{96,64},{128,160},{160,128},{192,224},{224,1... | collective-permute-start | bytes 245768 | tf_op jit(solution)/shard_map/ppermute | solution.py:423
  84.8 4.7 %collective-permute-start.28 = (f32[120,128]{1,0:T(8,128)S(1)}, f32[120,128]{1,0:T(8,128)S(1)}, u32[]{:S(2)}, u32[]{:S(2)}) collective-permute-start(f32[120,128]{1,0:T(8,128)S(1)} %fusion), channel_id=1, source_target_pairs={{0,16},{1,17},{2,18},{3,19},{4,20},{5,21},{6,22},{7,23},{8,24},{9,... | collective-permute-start | bytes 184328 | tf_op jit(solution)/shard_map/ppermute | solution.py:423
  86.7 4.3 %collective-permute-start.27 = (f32[120,128]{1,0:T(8,128)S(1)}, f32[120,128]{1,0:T(8,128)S(1)}, u32[]{:S(2)}, u32[]{:S(2)}) collective-permute-start(f32[120,128]{1,0:T(8,128)S(1)} %fusion), channel_id=1, source_target_pairs={{0,24},{1,25},{2,26},{3,27},{4,28},{5,29},{6,30},{7,31},{8,16},{9,... | collective-permute-start | bytes 184328 | tf_op jit(solution)/shard_map/ppermute | solution.py:423
  87.6 3.3 %collective-permute-start.26 = (f32[120,128]{1,0:T(8,128)S(1)}, f32[120,128]{1,0:T(8,128)S(1)}, u32[]{:S(2)}, u32[]{:S(2)}) collective-permute-start(f32[120,128]{1,0:T(8,128)S(1)} %fusion), channel_id=1, source_target_pairs={{0,8},{1,9},{2,10},{3,11},{4,12},{5,13},{6,14},{7,15},{8,0},{9,1},... | collective-permute-start | bytes 184328 | tf_op jit(solution)/shard_map/ppermute | solution.py:423
  91.0 4.7 %collective-permute-start.32 = (f32[120,128]{1,0:T(8,128)S(1)}, f32[120,128]{1,0:T(8,128)S(1)}, u32[]{:S(2)}, u32[]{:S(2)}) collective-permute-start(f32[120,128]{1,0:T(8,128)S(1)} %add_add_fusion.1), channel_id=1, source_target_pairs={{0,4},{1,5},{2,6},{3,7},{4,0},{5,1},{6,2},{7,3},{8,12},{9,13},{10,... | collective-permute-start | bytes 184328 | tf_op jit(solution)/shard_map/ppermute | solution.py:423
  93.0 4.6 %collective-permute-start.31 = (f32[120,128]{1,0:T(8,128)S(1)}, f32[120,128]{1,0:T(8,128)S(1)}, u32[]{:S(2)}, u32[]{:S(2)}) collective-permute-start(f32[120,128]{1,0:T(8,128)S(1)} %add_add_fusion.1), channel_id=1, source_target_pairs={{0,6},{1,7},{2,4},{3,5},{4,2},{5,3},{6,0},{7,1},{8,14},{9,15},{10,... | collective-permute-start | bytes 184328 | tf_op jit(solution)/shard_map/ppermute | solution.py:423
  93.9 3.8 %collective-permute-start.30 = (f32[120,128]{1,0:T(8,128)S(1)}, f32[120,128]{1,0:T(8,128)S(1)}, u32[]{:S(2)}, u32[]{:S(2)}) collective-permute-start(f32[120,128]{1,0:T(8,128)S(1)} %add_add_fusion.1), channel_id=1, source_target_pairs={{0,2},{1,3},{2,0},{3,1},{4,6},{5,7},{6,4},{7,5},{8,10},{9,11},{10,... | collective-permute-start | bytes 184328 | tf_op jit(solution)/shard_map/ppermute | solution.py:423
